TPU v7x, 128 devices: a whole 4x4x4 slice. The times are simulated.
128 devices in a mesh: chan: 16 (over y_hi, z, core), win: 8 (over y_lo, x).
Axes of the slice: x: 4, y: 4 (y_hi: 2, y_lo: 2; y = y_hi * 2 + y_lo), z: 4, core: 2. Of those that a mesh axis runs over, the one named last changes fastest.
Arguments:
- traces: bfloat16 [16, 8, 6144, 512], P('win', None, 'chan'), may hold values from -13.5 to 13.5
- channel_mask: int32 [6144], P('chan'), may hold values 0 or 1
- source_blocks: int32 [2, 4], replicated, may hold values from 0 to 767
Outputs:
- correlations: float32 [32, 2, 6144, 128], P('win', None, 'chan')
All inputs are finite; a program needn't handle non-finite values. No bound on the sum of `channel_mask` on one device may be relied on, other than what follows from the above.
Results may differ from a plain program's by a relative error of at most 0.0072.
Values may be sent and summed in bfloat16 or wider, within the bound.
No kernel may reach another device: no remote copies, remote signals or barrier semaphores. Data moves between devices by JAX's collectives and lax.ppermute only.
A program may use at most 192 MiB of HBM per device.

v0:
```python
import math

import jax
import jax.numpy as jnp
from jax import lax
from jax.sharding import PartitionSpec as P

NF = 128
F_LO = 8
NLAG = 128
VSB = 8
NSRC = 4
STEPS = 2


WATER_LEVEL = 0.05
TINY_ENERGY = 1e-06


def spread(array, axis, root):
    mine = lax.axis_index(axis) == root
    return lax.psum(jnp.where(mine, array, jnp.zeros_like(array)), axis)


def spectrum_table(length, bin_count, first_bin):
    sample_times = jnp.arange(length, dtype=jnp.int32)[:, None]
    bin_numbers = first_bin + jnp.arange(bin_count, dtype=jnp.int32)[None, :]
    angles = (sample_times * bin_numbers % length).astype(jnp.float32) * (2.0 * math.pi / length)
    window_taper = 0.5 - 0.5 * jnp.cos(
        (sample_times.astype(jnp.float32) + 0.5) * (2.0 * math.pi / length)
    )
    return jnp.concatenate(
        [window_taper * jnp.cos(angles), -window_taper * jnp.sin(angles)], axis=1
    ).astype(jnp.bfloat16)


def make_lags(length, bin_count, first_bin, lag_count):
    bin_numbers = (first_bin + jnp.arange(bin_count, dtype=jnp.int32))[:, None]
    shifts = (jnp.arange(lag_count, dtype=jnp.int32) - lag_count // 2)[None, :]
    angles = (bin_numbers * shifts % length).astype(jnp.float32) * (2.0 * math.pi / length)
    return jnp.concatenate([jnp.cos(angles), -jnp.sin(angles)], axis=0).astype(jnp.bfloat16)


def whiten(spectrum, bin_count):
    real_part = spectrum[..., :bin_count]
    imag_part = spectrum[..., bin_count:]
    energy = real_part * real_part + imag_part * imag_part
    mean_energy = jnp.mean(energy, axis=-1, keepdims=True)
    factor = lax.rsqrt(energy + WATER_LEVEL * mean_energy + TINY_ENERGY)
    return jnp.concatenate([real_part * factor, imag_part * factor], axis=-1)


def cross_spectra(senders, receivers, bin_count):

    def correlate_bins(left, right):
        return jnp.einsum("nif,njf->ifj", left, right, preferred_element_type=jnp.float32)

    send_real, send_imag = (senders[..., :bin_count], senders[..., bin_count:])
    recv_real, recv_imag = (receivers[..., :bin_count], receivers[..., bin_count:])
    in_phase = correlate_bins(send_real, recv_real) + correlate_bins(send_imag, recv_imag)
    quadrature = correlate_bins(send_real, recv_imag) - correlate_bins(send_imag, recv_real)
    return jnp.concatenate([in_phase, quadrature], axis=1).astype(jnp.bfloat16)


def on_device(traces, channel_mask, source_blocks):
    local_windows, segments, channels, length = traces.shape
    seg_count = local_windows * segments
    dft_table = spectrum_table(length, NF, F_LO)
    spectrum = jnp.dot(
        traces.reshape(-1, length), dft_table, preferred_element_type=jnp.float32
    ).reshape(seg_count, channels, 2 * NF)
    spectrum = spectrum * channel_mask.astype(jnp.float32)[None, :, None]
    whitened = whiten(spectrum, NF).astype(jnp.bfloat16)
    lag_weights = make_lags(length, NF, F_LO, NLAG)
    factor = 1.0 / (local_windows * lax.axis_size("win") * segments)
    per_device = channels // VSB
    row_count = NSRC * VSB // lax.axis_size("win")
    sources = []
    for step_index in range(STEPS):
        received = []
        for slot_index in range(NSRC):
            block_id = source_blocks[step_index, slot_index]
            holder = block_id // per_device
            candidate_offset = block_id % per_device * VSB
            portion = lax.dynamic_slice_in_dim(whitened, candidate_offset, VSB, 1)
            portion, holder = (portion, holder)
            received.append(spread(portion, "chan", holder))
        sources.append(jnp.concatenate(received, axis=1))
    results = []
    for step_index in range(STEPS):

        def corr_term(offset, amount, senders=sources[step_index]):
            stacked = cross_spectra(senders, whitened, NF)
            return (
                jnp.einsum("igj,gl->ijl", stacked, lag_weights, preferred_element_type=jnp.float32)
                * factor
            )

        results.append(
            lax.psum_scatter(
                corr_term(jnp.int32(0), lax.axis_size("win") * row_count),
                "win",
                scatter_dimension=0,
                tiled=True,
            )
        )
    return jnp.stack(results, axis=1)


def solution(mesh):
    in_specs = (P("win", None, "chan", None), P("chan"), P())
    out_specs = P("win", None, "chan", None)
    return jax.shard_map(
        on_device, mesh=mesh, in_specs=in_specs, out_specs=out_specs, check_vma=False
    )
```

profile of v0, /device:TPU:0, one launch (start us, length us, event | category | flops | bytes accessed | tf_op | source)
XLA Modules:
  0.0 412.5 jit_solution(3700655630012718370)
XLA Ops:
  25.3 7.4 %convolution_bitcast_fusion = f32[6144,256]{0,1:T(8,128)} fusion(bf16[6144,512]{1,0:T(8,128)(2,1)} %bitcast.62, bf16[512,128]{1,0:T(8,128)(2,1)S(1)} %get-tuple-element.38, bf16[512,128]{1,0:T(8,128)(2,1)S(1)} %get-tuple-element.37), kind=kOutput, calls=%fused_computation | convolution fusion | flops 1611137024 | bytes 12845056 | tf_op jit(solution)/shard_map/dot_general | solution.py:69
  32.7 6.6 %copy.21 = f32[6144,256]{1,0:T(8,128)} copy(f32[6144,256]{0,1:T(8,128)} %convolution_bitcast_fusion) | data formatting | bytes 12582912 | tf_op jit(solution)/shard_map/reshape | solution.py:71
  51.0 138.8 %all-reduce.3.cloned.1.call-done = (bf16[16,8,256]{2,1,0:T(8,128)(2,1)}, bf16[16,8,256]{2,1,0:T(8,128)(2,1)}, bf16[16,8,256]{2,1,0:T(8,128)(2,1)}, bf16[16,8,256...) async-done(((bf16[16,8,256]{2,1,0:T(8,128)(2,1)}, ...) | async-done | bytes 524304 | tf_op jit(solution)/shard_map/psum | solution.py:22
  195.6 4.8 %fusion.53 = f32[128,384,32]{1,2,0:T(8,128)} fusion(bf16[16,384,128]{1,0,2:T(8,128)(2,1)S(1)} %copy.10, bf16[16,32,128]{1,0,2:T(8,128)(2,1)} %copy.11), kind=kOutput, calls=%fused_computation.103 | convolution fusion | flops 50331648 | bytes 7995392 | tf_op jit(solution)/shard_map/nif,njf->ifj/dot_general | solution.py:56
  204.1 3.8 fusion.52
  207.9 3.7 fusion.54
  211.7 6.6 %copy.12 = f32[128,384,32]{0,1,2:T(8,128)} copy(f32[128,384,32]{1,2,0:T(8,128)} %fusion.53) | data formatting | bytes 12582912 | tf_op jit(solution)/shard_map/nif,njf->ifj/dot_general | solution.py:56
  218.3 6.6 %copy.9 = f32[128,384,32]{0,1,2:T(8,128)} copy(f32[128,384,32]{1,2,0:T(8,128)} %fusion.52) | data formatting | bytes 12582912 | tf_op jit(solution)/shard_map/nif,njf->ifj/dot_general | solution.py:56
  224.9 6.6 %copy.14 = f32[128,384,32]{0,1,2:T(8,128)} copy(f32[128,384,32]{1,2,0:T(8,128)} %fusion.55) | data formatting | bytes 12582912 | tf_op jit(solution)/shard_map/nif,njf->ifj/dot_general | solution.py:56
  231.5 6.6 %copy.13 = f32[128,384,32]{0,1,2:T(8,128)} copy(f32[128,384,32]{1,2,0:T(8,128)} %fusion.54) | data formatting | bytes 12582912 | tf_op jit(solution)/shard_map/nif,njf->ifj/dot_general | solution.py:56
  238.1 5.7 %fusion.8 = bf16[32,128,384]{1,2,0:T(8,128)(2,1)S(1)} fusion(f32[128,384,32]{0,1,2:T(8,128)} %copy.9, f32[128,384,32]{0,1,2:T(8,128)} %copy.12), kind=kLoop, calls=%fused_computation.29 | loop fusion | flops 3145728 | bytes 15728640 | tf_op jit(solution)/shard_map/add | solution.py:60
  249.0 6.3 %broadcast_multiply_fusion.1 = f32[32,384,128]{2,1,0:T(8,128)} fusion(bf16[32,128,384]{1,2,0:T(8,128)(2,1)} %fusion.9, bf16[32,128,384]{1,2,0:T(8,128)(2,1)S(1)} %fusion.8, bf16[128,128]{1,0:T(8,128)(2,1)S(1)} %get-tuple-element.28, bf16[128,128]{1,0:T(8,128)(2,1)S(1)} %get-tuple-element.27), kind=kOutput, calls=%fused_computation.34 | convolution fusion | flops 819593216 | bytes 12648448 | tf_op jit(solution)/shard_map/igj,gl->ijl/dot_general | solution.py:95
  257.5 4.7 %fusion.56 = f32[128,384,32]{1,2,0:T(8,128)} fusion(bf16[16,384,128]{1,0,2:T(8,128)(2,1)S(1)} %copy.7, bf16[16,32,128]{1,0,2:T(8,128)(2,1)} %copy.15), kind=kOutput, calls=%fused_computation.106 | convolution fusion | flops 50331648 | bytes 7995392 | tf_op jit(solution)/shard_map/nif,njf->ifj/dot_general | solution.py:56
  262.2 6.6 %copy.16 = f32[128,384,32]{0,1,2:T(8,128)} copy(f32[128,384,32]{1,2,0:T(8,128)} %fusion.56) | data formatting | bytes 12582912 | tf_op jit(solution)/shard_map/nif,njf->ifj/dot_general | solution.py:56
  270.0 4.7 %fusion.57 = f32[128,384,32]{1,2,0:T(8,128)} fusion(bf16[16,384,128]{1,0,2:T(8,128)(2,1)S(1)} %copy.10, bf16[16,32,128]{1,0,2:T(8,128)(2,1)} %copy.17), kind=kOutput, calls=%fused_computation.107 | convolution fusion | flops 50331648 | bytes 7995392 | tf_op jit(solution)/shard_map/nif,njf->ifj/dot_general | solution.py:56
  274.8 6.7 %copy.18 = f32[128,384,32]{0,1,2:T(8,128)} copy(f32[128,384,32]{1,2,0:T(8,128)} %fusion.57) | data formatting | bytes 12582912 | tf_op jit(solution)/shard_map/nif,njf->ifj/dot_general | solution.py:56
  281.5 4.8 %fusion.59 = f32[128,384,32]{1,2,0:T(8,128)} fusion(bf16[16,384,128]{1,0,2:T(8,128)(2,1)S(1)} %copy.7, bf16[16,32,128]{1,0,2:T(8,128)(2,1)} %copy.17), kind=kOutput, calls=%fused_computation.109 | convolution fusion | flops 50331648 | bytes 7995392 | tf_op jit(solution)/shard_map/nif,njf->ifj/dot_general | solution.py:56
  286.3 6.7 %copy.20 = f32[128,384,32]{0,1,2:T(8,128)} copy(f32[128,384,32]{1,2,0:T(8,128)} %fusion.59) | data formatting | bytes 12582912 | tf_op jit(solution)/shard_map/nif,njf->ifj/dot_general | solution.py:56
  293.0 3.8 fusion.58
  296.8 6.8 %copy.19 = f32[128,384,32]{0,1,2:T(8,128)} copy(f32[128,384,32]{1,2,0:T(8,128)} %fusion.58) | data formatting | bytes 12582912 | tf_op jit(solution)/shard_map/nif,njf->ifj/dot_general | solution.py:56
  303.7 5.8 %fusion.10 = bf16[32,128,384]{1,2,0:T(8,128)(2,1)S(1)} fusion(f32[128,384,32]{0,1,2:T(8,128)} %copy.16, f32[128,384,32]{0,1,2:T(8,128)} %copy.18), kind=kLoop, calls=%fused_computation.31 | loop fusion | flops 3145728 | bytes 15728640 | tf_op jit(solution)/shard_map/add | solution.py:60
  314.1 6.3 %broadcast_multiply_fusion = f32[32,384,128]{2,1,0:T(8,128)} fusion(bf16[32,128,384]{1,2,0:T(8,128)(2,1)} %fusion.11, bf16[32,128,384]{1,2,0:T(8,128)(2,1)S(1)} %fusion.10, bf16[128,128]{1,0:T(8,128)(2,1)S(1)} %get-tuple-element.28, bf16[128,128]{1,0:T(8,128)(2,1)S(1)} %get-tuple-element.27), kind=kOutput, calls=%fused_computation.33 | convolution fusion | flops 819593216 | bytes 12648448 | tf_op jit(solution)/shard_map/igj,gl->ijl/dot_general | solution.py:95
  320.5 8.5 %reduce-scatter.3.cloned.1.call-done = f32[4,384,128]{2,1,0:T(8,128)} async-done(((f32[32,384,128]{2,1,0:T(8,128)}), f32[4,384,128]{2,1,0:T(8,128)}) %reduce-scatter.3.cloned.1.call-update) | async-done | bytes 786448 | tf_op jit(solution)/shard_map/reduce_scatter | solution.py:100
  328.9 74.3 %reduce-scatter.5.cloned.1.call-done = f32[4,384,128]{2,1,0:T(8,128)} async-done(((f32[32,384,128]{2,1,0:T(8,128)}), f32[4,384,128]{2,1,0:T(8,128)}) %reduce-scatter.5.cloned.1.call-update) | async-done | bytes 786448 | tf_op jit(solution)/shard_map/reduce_scatter | solution.py:100
  (68 shorter events, 39.8 us)
Async XLA Ops:
  6.5 183.3 %all-reduce.3.cloned.1.call-start = ((), (), s32[]{:S(2)}) async-start(), calls=%async_computation.4 | async-start | bytes 1048576 | tf_op jit(solution)/shard_map/psum | solution.py:22
  32.7 6.6 %copy-start.11 = (s32[384]{0:T(512)S(1)}, s32[384]{0:T(512)}, u32[]{:S(2)}) copy-start(s32[384]{0:T(512)} %param.4) | copy-start | bytes 4612
  45.1 1.9 copy-start.3
  47.0 281.9 %reduce-scatter.3.cloned.1.call-start = ((), (), s32[]{:S(2)}) async-start(), calls=%async_computation.2 | async-start | bytes 7077888 | tf_op jit(solution)/shard_map/reduce_scatter | solution.py:100
  195.6 4.8 %copy-start.5 = (bf16[16,32,128]{1,0,2:T(8,128)(2,1)S(1)}, bf16[16,32,128]{1,0,2:T(8,128)(2,1)}, u32[]{:S(2)}) copy-start(bf16[16,32,128]{1,0,2:T(8,128)(2,1)} %copy.11) | copy-start | bytes 393220
  200.4 3.7 copy-start.6
  238.1 6.4 %copy-start = (f32[128,384,32]{0,1,2:T(8,128)S(1)}, f32[128,384,32]{0,1,2:T(8,128)}, u32[]{:S(2)}) copy-start(f32[128,384,32]{0,1,2:T(8,128)} %copy.14) | copy-start | bytes 18874372
  238.1 8.2 %copy-start.1 = (f32[128,384,32]{0,1,2:T(8,128)S(1)}, f32[128,384,32]{0,1,2:T(8,128)}, u32[]{:S(2)}) copy-start(f32[128,384,32]{0,1,2:T(8,128)} %copy.13) | copy-start | bytes 18874372
  255.3 0.8 copy-start.10
  255.3 0.9 copy-start.9
  255.3 0.9 copy-start.8
  255.3 0.9 copy-start.7
  255.4 147.8 %reduce-scatter.5.cloned.1.call-start = ((), (), s32[]{:S(2)}) async-start(), calls=%async_computation.3 | async-start | bytes 7077888 | tf_op jit(solution)/shard_map/reduce_scatter | solution.py:100
  286.3 6.7 %copy-start.4 = (bf16[16,32,128]{1,0,2:T(8,128)(2,1)S(1)}, bf16[16,32,128]{1,0,2:T(8,128)(2,1)}, u32[]{:S(2)}) copy-start(bf16[16,32,128]{1,0,2:T(8,128)(2,1)} %copy.15) | copy-start | bytes 393220
  296.8 12.7 %slice-start = ((s8[6291456]{0:T(1024)(128)(4,1)}), s8[2097152]{0:T(1024)(128)(4,1)S(1)}, s32[]{:S(2)}) async-start(s8[6291456]{0:T(1024)(128)(4,1)} %bitcast.59), calls=%async_computation.5 | async-start | bytes 4194304
  303.7 6.0 %slice-start.1 = ((s8[6291456]{0:T(1024)(128)(4,1)}), s8[4194304]{0:T(1024)(128)(4,1)S(1)}, s32[]{:S(2)}) async-start(s8[6291456]{0:T(1024)(128)(4,1)} %bitcast.59), calls=%async_computation.6 | async-start | bytes 8388608
  303.7 7.9 %copy-start.2 = (f32[128,384,32]{0,1,2:T(8,128)S(1)}, f32[128,384,32]{0,1,2:T(8,128)}, u32[]{:S(2)}) copy-start(f32[128,384,32]{0,1,2:T(8,128)} %copy.19) | copy-start | bytes 18874372
Sparse Core Ops, SparseCore 0:
  47.1 142.6 all-reduce.2
  255.5 73.3 reduce-scatter.2
  331.5 71.6 reduce-scatter.4
where the time goes:
time: 415 us; the launch traced here: 412 us
  waiting for transfers between devices  222 us (53%)
  local copies, waits for them, and re-layouts  79.6 us (19%)
  matrix products  54.1 us (13%)
  between operations  29.3 us (7%)
  other arithmetic  27.3 us (7%)
    psum x1, waiting for transfers between devices, spread(): return lax.psum(jnp.where(mine, array, jnp.zeros_like(array)), axis)  139 us
    reduce_scatter x2, waiting for transfers between devices, on_device(): lax.psum_scatter(corr_term(jnp.int32(0), lax.axis_size('win') * row_count...  82.7 us
    dot_general x8, local copies, waits for them, and re-layouts, correlate_bins(): jnp.einsum('nif,njf->ifj', left, right, preferred_element_type=jnp.float32)  53.3 us
    dot_general x8, matrix products, correlate_bins(): jnp.einsum('nif,njf->ifj', left, right, preferred_element_type=jnp.float32)  34.1 us
    dot_general x2, matrix products, corr_term(): jnp.einsum('igj,gl->ijl', stacked, lag_weights, preferred_element_type=jn...  12.7 us
    add x2, other arithmetic, cross_spectra(): correlate_bins(send_real, recv_real) + correlate_bins(send_imag, recv_imag)  11.5 us
  transfers between devices with their start and end apart: 3, of which 3 were waited for; matrix products, arithmetic and copies ran while one was open for 16% of the time, Pallas kernels for 0%

commit v1 on v0

v1 whole, which is shorter than its diff:
```python
import functools
import math

import jax
import jax.numpy as jnp
import ml_dtypes
import numpy as np
from jax import lax
from jax.experimental import pallas as pl
from jax.experimental.pallas import tpu as pltpu
from jax.sharding import PartitionSpec as P

NF = 128
F_LO = 8
NLAG = 128
VSB = 8
NSRC = 4
STEPS = 2
WATER_LEVEL = 0.05
TINY_ENERGY = 1e-06

FB = 16
BF16 = jnp.bfloat16
F32 = jnp.float32


def band_rows():
    row = np.arange(2 * NF)
    return F_LO + (row // 16) * 8 + row % 8, (row // 8) % 2


def dft_rows(length):
    bins, part = band_rows()
    t = np.arange(length)
    angle = (t[None, :] * bins[:, None] % length) * (2.0 * math.pi / length)
    taper = 0.5 - 0.5 * np.cos((t + 0.5) * (2.0 * math.pi / length))
    table = np.where(part[:, None] == 0, np.cos(angle), -np.sin(angle)) * taper[None, :]
    return table.astype(np.float32).astype(ml_dtypes.bfloat16)


def lag_rows(length, scale):
    bins, part = band_rows()
    shift = np.arange(NLAG) - NLAG // 2
    angle = (shift[:, None] * bins[None, :] % length) * (2.0 * math.pi / length)
    table = np.where(part[None, :] == 0, np.cos(angle), -np.sin(angle))
    table = table.astype(np.float32).astype(ml_dtypes.bfloat16)
    return (table.astype(np.float32) * scale).astype(ml_dtypes.bfloat16)


def dot(a, b, dims=((1,), (0,))):
    return lax.dot_general(a, b, (dims, ((), ())), preferred_element_type=F32)


def iota(shape, dim):
    return lax.broadcasted_iota(jnp.int32, shape, dim)


def whiten_rows(z, live=None):
    lanes = z.shape[-1]
    z = z.reshape(FB, 2, 8, lanes)
    re, im = z[:, 0], z[:, 1]
    energy = re * re + im * im
    mean = jnp.sum(jnp.sum(energy, axis=0), axis=0, keepdims=True) * (1.0 / NF)
    factor = lax.rsqrt(energy + WATER_LEVEL * mean[None] + TINY_ENERGY)
    if live is not None:
        factor = factor * live[None]
    out = jnp.concatenate([(re * factor)[:, None], (im * factor)[:, None]], axis=1)
    return out.reshape(FB, 16, lanes).astype(BF16)


def source_kernel(blocks_ref, mask_ref, me_ref, traces_ref, table_ref, *rest):
    keep0, send0, keep1, send1, xbuf, wsc, sems = rest
    count = xbuf.shape[0]
    per_device = traces_ref.shape[1] // VSB
    chan, core = me_ref[0], me_ref[1]
    nblk = STEPS * NSRC
    local, mine, copies = [], [], []
    for b in range(nblk):
        block = blocks_ref[b // NSRC, b % NSRC]
        holder = block // per_device
        loc = block - holder * per_device
        local.append(loc)
        mine.append(holder == chan)
        start = pl.multiple_of((loc // 2) * 16, 16)
        copy = pltpu.make_async_copy(
            traces_ref.at[:, pl.ds(start, 16), :], xbuf.at[:, pl.ds(b * 16, 16), :], sems.at[b]
        )
        copy.start()
        copies.append(copy)
    col = iota((1, 256), 1)
    col_block = (col >> 7) * NSRC + ((col & 31) >> 3)
    col_v = col & 7
    target = jnp.full((1, 256), -100, jnp.int32)
    for b in range(nblk):
        here = col_block == b
        row = jnp.where(mine[b], (local[b] & 1) * 8, -1000)
        target = jnp.where(here, col_v + row, target)
        for v in range(VSB):
            dead = mask_ref[local[b] * VSB + v] == 0
            target = jnp.where(here & (col_v == v) & dead, -1000, target)
    row = iota((512, 256), 0)
    key = ((row >> 7) << 7) + row % 128
    want = jnp.where(target >= 0, (((col >> 5) & 3) << 7) + col_block * 16 + target, -1)
    select = (key == want).astype(F32).astype(BF16)
    for copy in copies:
        copy.wait()

    def one(n, carry):
        z = dot(table_ref[...], xbuf[n], ((1,), (1,)))
        wsc[:, pl.ds(pl.multiple_of(n * 16, 16), 16), :] = whiten_rows(z)
        return carry

    lax.fori_loop(0, count, one, 0, unroll=2)
    for rel, pair in ((0, (keep0, keep1)), (1, (send0, send1))):
        half = core if rel == 0 else 1 - core
        for t in range(2):
            low = half * 2 + t
            left = jnp.concatenate([wsc[hi * 4 + low] for hi in range(4)], axis=1)
            out = dot(left, select).astype(BF16)
            pair[0][t * 256 : (t + 1) * 256, :] = out[:, :128]
            pair[1][t * 256 : (t + 1) * 256, :] = out[:, 128:]


def source_spectra(traces, mask, blocks, me, table):
    count, channels, length = traces.shape
    shape = jax.ShapeDtypeStruct((512, 128), BF16)
    smem = pl.BlockSpec(memory_space=pltpu.SMEM)
    vmem = pl.BlockSpec(memory_space=pltpu.VMEM)
    return pl.pallas_call(
        source_kernel,
        out_shape=[shape] * 4,
        in_specs=[smem, smem, smem, pl.BlockSpec(memory_space=pl.ANY), vmem],
        out_specs=[vmem] * 4,
        scratch_shapes=[
            pltpu.VMEM((count, 128, length), BF16),
            pltpu.VMEM((FB, 256, 128), BF16),
            pltpu.SemaphoreType.DMA((STEPS * NSRC,)),
        ],
        compiler_params=pltpu.CompilerParams(vmem_limit_bytes=32 * 2**20),
        cost_estimate=pl.CostEstimate(flops=10**9, bytes_accessed=3 * 10**6, transcendentals=0),
        name="source_spectra",
    )(blocks, mask, me, traces, table)


def receiver_kernel(traces_ref, table_ref, live_ref, out_ref):
    z = dot(table_ref[...], traces_ref[0], ((1,), (1,)))
    out_ref[:, 0] = whiten_rows(z, live_ref[...])


def receiver_spectra(traces, live, table):
    count, channels, length = traces.shape
    return pl.pallas_call(
        receiver_kernel,
        grid=(count,),
        out_shape=jax.ShapeDtypeStruct((FB, count, 16, channels), BF16),
        in_specs=[
            pl.BlockSpec((1, channels, length), lambda n: (n, 0, 0)),
            pl.BlockSpec((2 * NF, length), lambda n: (0, 0)),
            pl.BlockSpec((1, channels), lambda n: (0, 0)),
        ],
        out_specs=pl.BlockSpec((FB, 1, 16, channels), lambda n: (0, n, 0, 0)),
        compiler_params=pltpu.CompilerParams(vmem_limit_bytes=32 * 2**20),
        cost_estimate=pl.CostEstimate(
            flops=2 * count * channels * length * 256, bytes_accessed=10**7, transcendentals=10**6
        ),
        name="receiver_spectra",
    )(traces, table, live)


def swap_parts(x):
    y = x.astype(F32).reshape(16, 2, 8, x.shape[-1])
    y = jnp.concatenate([-y[:, 1:2], y[:, 0:1]], axis=1)
    return y.reshape(256, x.shape[-1]).astype(BF16)


def correlate_kernel(groups, me_ref, a_ref, b_ref, recv_ref, lag_ref, *rest):
    outs, (pick, both, stacked) = rest[: len(groups)], rest[len(groups) :]
    core, my_y, my_x = me_ref[1], me_ref[2], me_ref[3]
    row, col = iota((512, 256), 0), iota((512, 256), 1)
    rel = row >> 4
    source = (((my_y ^ (rel >> 4)) * 4 + ((my_x + (rel >> 2)) & 3)) << 2) + (rel & 3)
    key = (((row >> 3) & 1) << 7) + source
    for hi in range(4):
        pick[hi] = (col == key + hi * 32).astype(F32).astype(BF16)
    for half, ref in ((0, a_ref), (1, b_ref)):
        for t in range(2):
            x = ref[t * 256 : (t + 1) * 256, :]
            both[half * 2 + t] = jnp.concatenate([x, swap_parts(x)], axis=1)
    diagonal = ((iota((8, 256), 0)) == (iota((8, 256), 1) & 7)).astype(F32)

    def one(u, carry):
        lo, hi = u & 3, u >> 2
        block = hi * 4 + (((lo >> 1) ^ core) << 1) + (lo & 1)
        left = dot(pick[hi], both[lo], ((1,), (1,)))
        left = (left.reshape(64, 8, 256) * diagonal[None]).reshape(512, 256).astype(BF16)
        out = dot(left, recv_ref[block])
        stacked[:, block] = out.astype(BF16).reshape(32, 16, out.shape[-1])
        return carry

    lax.fori_loop(0, 16, one, 0)
    lag = lag_ref[...]
    for group, out in zip(groups, outs):
        for place, (first, amount) in group:

            def two(r, carry, place=place, first=first, out=out):
                x = stacked[first + r].reshape(256, stacked.shape[-1])
                out[place + r] = dot(lag, x).astype(BF16)
                return carry

            lax.fori_loop(0, amount, two, 0)


def correlate(groups, me, a, b, receivers, lags):
    channels = receivers.shape[-1]
    smem = pl.BlockSpec(memory_space=pltpu.SMEM)
    vmem = pl.BlockSpec(memory_space=pltpu.VMEM)
    sizes = [sum(amount for _, (_, amount) in group) for group in groups]
    return pl.pallas_call(
        functools.partial(correlate_kernel, groups),
        out_shape=[jax.ShapeDtypeStruct((n, NLAG, channels), BF16) for n in sizes],
        in_specs=[smem] + [vmem] * 4,
        out_specs=[vmem] * len(groups),
        scratch_shapes=[
            pltpu.VMEM((4, 512, 256), BF16),
            pltpu.VMEM((4, 256, 256), BF16),
            pltpu.VMEM((32, FB, 16, channels), BF16),
        ],
        compiler_params=pltpu.CompilerParams(vmem_limit_bytes=48 * 2**20),
        cost_estimate=pl.CostEstimate(flops=8 * 10**9, bytes_accessed=10**7, transcendentals=0),
        name="correlate",
    )(me, a, b, receivers, lags)


def finish_kernel(*refs):
    ins, out = refs[:-1], refs[-1]
    half = len(ins) // 2
    for step in range(2):
        total = ins[step * half][0].astype(F32)
        for ref in ins[step * half + 1 : (step + 1) * half]:
            total = total + ref[0].astype(F32)
        out[0, step] = total.T


def finish(first, second):
    rows, lags, channels = 4, NLAG, first[0].shape[-1]
    ins = list(first) + list(second)
    spec = pl.BlockSpec((1, lags, channels), lambda r: (r, 0, 0))
    return pl.pallas_call(
        finish_kernel,
        grid=(rows,),
        out_shape=jax.ShapeDtypeStruct((rows, 2, channels, lags), F32),
        in_specs=[spec] * len(ins),
        out_specs=pl.BlockSpec((1, 2, channels, lags), lambda r: (r, 0, 0, 0)),
        compiler_params=pltpu.CompilerParams(vmem_limit_bytes=32 * 2**20),
        name="finish",
    )(*ins)


def add(*xs):
    total = xs[0].astype(F32)
    for x in xs[1:]:
        total = total + x.astype(F32)
    return total.astype(BF16)


def on_device(axes, traces, channel_mask, source_blocks):
    windows, segments, channels, length = traces.shape
    traces = traces.reshape(windows * segments, channels, length)
    chan, win = lax.axis_index("chan"), lax.axis_index("win")
    me = jnp.stack([chan, chan & 1, win >> 2, win & 3]).astype(jnp.int32)
    table = jnp.asarray(dft_rows(length))
    scale = 1.0 / (windows * lax.axis_size("win") * segments)
    lags = jnp.asarray(lag_rows(length, scale))

    def chan_swap(x, bits):
        return lax.ppermute(x, "chan", [(i, i ^ bits) for i in range(16)])

    def win_to(x, dy, dx):
        return lax.ppermute(
            x, "win", [(y * 4 + i, (y ^ dy) * 4 + (i + dx) % 4) for y in range(2) for i in range(4)]
        )

    keep0, send0, keep1, send1 = source_spectra(traces, channel_mask, source_blocks, me, table)

    def share(keep, send):
        mine = keep + chan_swap(send, 1)
        for bits in (2, 6, 8):
            mine = mine + chan_swap(mine, bits)
        return mine, chan_swap(mine, 1)

    live = channel_mask.astype(F32)[None]
    receivers = receiver_spectra(traces, live, table).reshape(FB, 256, channels)

    a, b = share(keep0, send0)
    groups = [((0, (16, 16)),)] + [((0, (dx * 4, 4)),) for dx in range(4)]
    away, o0, o1, o2, o3 = correlate(groups, me, a, b, receivers, lags)
    got = win_to(away, 1, 0)
    up = win_to(add(o2[:2], got[8:10]), 0, 1)
    down = win_to(add(o2[2:], got[10:12]), 0, -1)
    right = jnp.concatenate([add(o1[:2], got[4:6], up), add(o1[2:], got[6:8])])
    left = jnp.concatenate([add(o3[:2], got[12:14]), add(o3[2:], got[14:16], down)])
    first = (o0, got, win_to(right, 0, 1), win_to(left, 0, -1))

    a, b = share(keep1, send1)
    groups = [
        ((0, (0, 4)), (4, (16, 4))),
        ((0, (4, 4)), (4, (20, 4))),
        ((0, (8, 4)),),
        ((0, (24, 4)),),
        ((0, (12, 4)), (4, (28, 4))),
    ]
    x0, x1, x2a, x2b, x3 = correlate(groups, me, a, b, receivers, lags)
    up = win_to(x2a, 0, 1)
    down = win_to(x2b, 0, -1)
    from_left = win_to(jnp.concatenate([add(x1[:4], up), x1[4:]]), 0, 1)
    from_right = win_to(jnp.concatenate([x3[:4], add(x3[4:], down)]), 0, -1)
    got = win_to(add(x0[4:], from_left[4:], from_right[4:]), 1, 0)
    second = (x0, from_left, from_right, got)
    return finish(first, second)


def solution(mesh):
    in_specs = (P("win", None, "chan", None), P("chan"), P())
    out_specs = P("win", None, "chan", None)
    return jax.shard_map(
        functools.partial(on_device, dict(mesh.shape)),
        mesh=mesh,
        in_specs=in_specs,
        out_specs=out_specs,
        check_vma=False,
    )
```

time: 415 us -> 138 us (0.33)
  waiting for transfers between devices: 222 us -> 50.4 us
  local copies, waits for them, and re-layouts: 79.6 us -> 6.83 us
  matrix products: 54.1 us -> 0 us
  Pallas kernels: 0 us -> 47.8 us
  starting transfers between devices: 0.49 us -> 31.4 us
  between operations: 29.3 us -> 0.25 us
  other arithmetic: 27.3 us -> 1.4 us
    psum x1 -> x0, waiting for transfers between devices: 139 us -> none  [spread(): return lax.psum(jnp.where(mine, array, jnp.zeros_like(array)), axis)]
    reduce_scatter x2 -> x0, waiting for transfers between devices: 82.7 us -> none  [on_device(): lax.psum_scatter(corr_term(jnp.int32(0), lax.axis_size('win') * row_count...]
    dot_general x11 -> x0, matrix products: 54.1 us -> none  [the longest x8 34.1 us: correlate_bins(): jnp.einsum('nif,njf->ifj', left, right, preferred_element_type=jnp.float32)]
    dot_general x8 -> x0, local copies, waits for them, and re-layouts: 53.3 us -> none  [correlate_bins(): jnp.einsum('nif,njf->ifj', left, right, preferred_element_type=jnp.float32)]
    ppermute x0 -> x20, waiting for transfers between devices: none -> 50.4 us  [the longest x10 42.1 us: win_to(): lax.ppermute(x, 'win', [(y * 4 + i, (y ^ dy) * 4 + (i + dx) % 4) for y in...]
    pallas_call x0 -> x5, Pallas kernels: none -> 47.8 us  [the longest x2 35 us: correlate(): pl.pallas_call(functools.partial(correlate_kernel, groups), out_shape=[ja...]
    ppermute x0 -> x20, starting transfers between devices: none -> 31.4 us  [the longest x10 16.1 us: win_to(): lax.ppermute(x, 'win', [(y * 4 + i, (y ^ dy) * 4 + (i + dx) % 4) for y in...]
    add x2 -> x8, other arithmetic: 11.5 us -> 0.3 us  [the longest x6 0.23 us: share(): mine = mine + chan_swap(mine, bits)]
  transfers between devices with their start and end apart: 3 -> 20, of which waited for: 3 -> 10; matrix products, arithmetic and copies ran while one was open for 16% -> 1% of each run, Pallas kernels for 0% -> 30%
where the time goes in v1:
time: 138 us
  waiting for transfers between devices  50.4 us (37%)
  Pallas kernels  47.8 us (35%)
  starting transfers between devices  31.4 us (23%)
  local copies, waits for them, and re-layouts  6.83 us (5%)
  other arithmetic  1.4 us (1%)
    ppermute x10, waiting for transfers between devices, win_to(): lax.ppermute(x, 'win', [(y * 4 + i, (y ^ dy) * 4 + (i + dx) % 4) for y in...  42.1 us
    pallas_call x2, Pallas kernels, correlate(): pl.pallas_call(functools.partial(correlate_kernel, groups), out_shape=[ja...  35 us
    ppermute x10, starting transfers between devices, win_to(): lax.ppermute(x, 'win', [(y * 4 + i, (y ^ dy) * 4 + (i + dx) % 4) for y in...  16.1 us
    ppermute x10, starting transfers between devices, chan_swap(): return lax.ppermute(x, 'chan', [(i, i ^ bits) for i in range(16)])  15.3 us
    ppermute x10, waiting for transfers between devices, chan_swap(): return lax.ppermute(x, 'chan', [(i, i ^ bits) for i in range(16)])  8.38 us
    unnamed x18, local copies, waits for them, and re-layouts  6.74 us
    pallas_call x1, Pallas kernels, receiver_spectra(): pl.pallas_call(receiver_kernel, grid=(count,), out_shape=jax.ShapeDtypeSt...  6.43 us
    pallas_call x1, Pallas kernels, source_spectra(): pl.pallas_call(source_kernel, out_shape=[shape] * 4, in_specs=[smem, smem...  4.27 us
  transfers between devices with their start and end apart: 20, of which 10 were waited for; matrix products, arithmetic and copies ran while one was open for 1% of the time, Pallas kernels for 30%

profile of v1, /device:TPU:0, one launch (start us, length us, event | category | flops | bytes accessed | tf_op | source)
XLA Modules:
  0.0 138.1 jit_solution(960868342578273912)
XLA Ops:
  0.1 2.8 %copy-done = bf16[2,8,384,512]{3,2,1,0:T(8,128)(2,1)S(1)} copy-done((bf16[2,8,384,512]{3,2,1,0:T(8,128)(2,1)S(1)}, bf16[2,8,384,512]{3,2,1,0:T(8,128)(2,1)}, u32[]{:S(2)}) %copy-start) | copy-done | bytes 6291480
  5.2 4.3 %source_spectra.1 = (bf16[512,128]{1,0:T(8,128)(2,1)S(1)}, bf16[512,128]{1,0:T(8,128)(2,1)S(1)}, bf16[512,128]{1,0:T(8,128)(2,1)S(1)}, bf16[512,128]{1,0:T(8,128)(2,1)S(1)}) custom-call(s32[2,4]{1,0:T(2,128)S(1)} %copy-done.7, s32[384]{0:T(512)S(1)} %copy-done.5, s32[4]{0:T(128)S(1)} %pad_add_fusion.me_ref, bf16[16,384,512]{2,1,0:T(8,128)(2,1)S(1)} %bitcast.6, ...), custom_call_target="tpu_custom_call" | custom-call | flops 1000000000 | bytes 3000000 | tf_op jit(solution)/shard_map/source_spectra/pallas_call | solution.py:129
  10.9 2.1 %collective-permute-start.11 = (bf16[512,128]{1,0:T(8,128)(2,1)S(1)}, bf16[512,128]{1,0:T(8,128)(2,1)S(1)}, u32[]{:S(2)}, u32[]{:S(2)}) collective-permute-start(bf16[512,128]{1,0:T(8,128)(2,1)S(1)} %add.72), channel_id=1, source_target_pairs={{0,16},{8,24},{16,0},{24,8},{32,48},{40,56},{48,32},{56,40},{64,80... | collective-permute-start | bytes 393224 | tf_op jit(solution)/shard_map/ppermute | solution.py:276
  13.2 4.1 %collective-permute-done.11 = bf16[512,128]{1,0:T(8,128)(2,1)S(1)} collective-permute-done((bf16[512,128]{1,0:T(8,128)(2,1)S(1)}, bf16[512,128]{1,0:T(8,128)(2,1)S(1)}, u32[]{:S(2)}, u32[]{:S(2)}) %collective-permute-start.11) | collective-permute-done | bytes 131104 | tf_op jit(solution)/shard_map/ppermute | solution.py:276
  17.4 4.2 %collective-permute-start.12 = (bf16[512,128]{1,0:T(8,128)(2,1)S(1)}, bf16[512,128]{1,0:T(8,128)(2,1)S(1)}, u32[]{:S(2)}, u32[]{:S(2)}) collective-permute-start(bf16[512,128]{1,0:T(8,128)(2,1)S(1)} %add.73), channel_id=1, source_target_pairs={{0,48},{8,56},{16,32},{24,40},{32,16},{40,24},{48,0},{56,8},{64,11... | collective-permute-start | bytes 393224 | tf_op jit(solution)/shard_map/ppermute | solution.py:276
  21.7 2.0 %collective-permute-start.2 = (bf16[512,128]{1,0:T(8,128)(2,1)S(1)}, bf16[512,128]{1,0:T(8,128)(2,1)S(1)}, u32[]{:S(2)}, u32[]{:S(2)}) collective-permute-start(bf16[512,128]{1,0:T(8,128)(2,1)S(1)} %add.61), channel_id=1, source_target_pairs={{0,48},{8,56},{16,32},{24,40},{32,16},{40,24},{48,0},{56,8},{64,11... | collective-permute-start | bytes 393224 | tf_op jit(solution)/shard_map/ppermute | solution.py:276
  23.6 1.7 %collective-permute-done.12 = bf16[512,128]{1,0:T(8,128)(2,1)S(1)} collective-permute-done((bf16[512,128]{1,0:T(8,128)(2,1)S(1)}, bf16[512,128]{1,0:T(8,128)(2,1)S(1)}, u32[]{:S(2)}, u32[]{:S(2)}) %collective-permute-start.12) | collective-permute-done | bytes 131104 | tf_op jit(solution)/shard_map/ppermute | solution.py:276
  25.4 3.3 %collective-permute-start.13 = (bf16[512,128]{1,0:T(8,128)(2,1)S(1)}, bf16[512,128]{1,0:T(8,128)(2,1)S(1)}, u32[]{:S(2)}, u32[]{:S(2)}) collective-permute-start(bf16[512,128]{1,0:T(8,128)(2,1)S(1)} %add.74), channel_id=1, source_target_pairs={{0,64},{8,72},{16,80},{24,88},{32,96},{40,104},{48,112},{56,120},{... | collective-permute-start | bytes 393224 | tf_op jit(solution)/shard_map/ppermute | solution.py:276
  28.7 2.5 %collective-permute-start.3 = (bf16[512,128]{1,0:T(8,128)(2,1)S(1)}, bf16[512,128]{1,0:T(8,128)(2,1)S(1)}, u32[]{:S(2)}, u32[]{:S(2)}) collective-permute-start(bf16[512,128]{1,0:T(8,128)(2,1)S(1)} %add.62), channel_id=1, source_target_pairs={{0,64},{8,72},{16,80},{24,88},{32,96},{40,104},{48,112},{56,120},{... | collective-permute-start | bytes 393224 | tf_op jit(solution)/shard_map/ppermute | solution.py:276
  31.2 1.7 %collective-permute-done.13 = bf16[512,128]{1,0:T(8,128)(2,1)S(1)} collective-permute-done((bf16[512,128]{1,0:T(8,128)(2,1)S(1)}, bf16[512,128]{1,0:T(8,128)(2,1)S(1)}, u32[]{:S(2)}, u32[]{:S(2)}) %collective-permute-start.13) | collective-permute-done | bytes 131104 | tf_op jit(solution)/shard_map/ppermute | solution.py:276
  33.1 6.4 %receiver_spectra.1 = bf16[16,16,16,384]{3,2,1,0:T(8,128)(2,1)S(1)} custom-call(bf16[16,384,512]{2,1,0:T(8,128)(2,1)S(1)} %bitcast.7, bf16[256,512]{1,0:T(8,128)(2,1)S(1)} %copy-done.4, f32[1,384]{1,0:T(1,128)S(1)} %broadcast_in_dim.3.live_ref), custom_call_target="tpu_custom_call" | custom-call | flops 1610612736 | bytes 10000000 | tf_op jit(solution)/shard_map/receiver_spectra/pallas_call | solution.py:152
  41.7 17.5 %correlate.3 = (bf16[8,128,384]{2,1,0:T(8,128)(2,1)S(1)}, bf16[8,128,384]{2,1,0:T(8,128)(2,1)S(1)}, bf16[4,128,384]{2,1,0:T(8,128)(2,1)S(1)}, bf16[4,128,384]{2,1,0:T(8,128)(2,1)S(1)}, bf16[8,128,384]{2,1,0:T(8,128)(2,1)S(1)}) custom-call(s32[4]{0:T(128)S(1)} %pad_add_fusion.me_ref, bf16[512,128]{1,0:T(8,128)(2,1)S(1)} %add.75.a_ref, ...), custom_call_target="tpu_custom_call" | custom-call | flops 8000000000 | bytes 10000000 | tf_op jit(solution)/shard_map/correlate/pallas_call | solution.py:218
  59.2 2.8 %collective-permute-start.17 = (bf16[4,128,384]{2,1,0:T(8,128)(2,1)S(1)}, bf16[4,128,384]{2,1,0:T(8,128)(2,1)S(1)}, u32[]{:S(2)}, u32[]{:S(2)}) collective-permute-start(bf16[4,128,384]{2,1,0:T(8,128)(2,1)S(1)} %get-tuple-element.32), channel_id=1, source_target_pairs={{0,3},{1,0},{2,1},{3,2},{4,7},{5,4},{6,5},{7,6},{8,11},{9,8},{10,9... | collective-permute-start | bytes 1179656 | tf_op jit(solution)/shard_map/ppermute | solution.py:279
  62.0 17.5 %correlate.2 = (bf16[16,128,384]{2,1,0:T(8,128)(2,1)S(1)}, bf16[4,128,384]{2,1,0:T(8,128)(2,1)S(1)}, bf16[4,128,384]{2,1,0:T(8,128)(2,1)S(1)}, bf16[4,128,384]{2,1,0:T(8,128)(2,1)S(1)}, bf16[4,128,384]{2,1,0:T(8,128)(2,1)S(1)}) custom-call(s32[4]{0:T(128)S(1)} %pad_add_fusion.me_ref, bf16[512,128]{1,0:T(8,128)(2,1)S(1)} %add.63.a_ref, ...), custom_call_target="tpu_custom_call" | custom-call | flops 8000000000 | bytes 10000000 | tf_op jit(solution)/shard_map/correlate/pallas_call | solution.py:218
  81.5 3.3 %collective-permute-start.18 = (bf16[8,128,384]{2,1,0:T(8,128)(2,1)S(1)}, bf16[8,128,384]{2,1,0:T(8,128)(2,1)S(1)}, u32[]{:S(2)}, u32[]{:S(2)}) collective-permute-start(bf16[8,128,384]{2,1,0:T(8,128)(2,1)S(1)} %pad_maximum_fusion.1), channel_id=1, source_target_pairs={{0,3},{1,0},{2,1},{3,2},{4,7},{5,4},{6,5},{7,6},{8,11},{9,8},{10,9... | collective-permute-start | bytes 2359304 | tf_op jit(solution)/shard_map/ppermute | solution.py:279
  84.8 8.2 %collective-permute-done.15 = bf16[4,128,384]{2,1,0:T(8,128)(2,1)S(1)} collective-permute-done((bf16[4,128,384]{2,1,0:T(8,128)(2,1)S(1)}, bf16[4,128,384]{2,1,0:T(8,128)(2,1)S(1)}, u32[]{:S(2)}, u32[]{:S(2)}) %collective-permute-start.15) | collective-permute-done | bytes 393248 | tf_op jit(solution)/shard_map/ppermute | solution.py:279
  93.3 22.5 %collective-permute-done.5.refs_1_ = bf16[16,128,384]{2,1,0:T(8,128)(2,1)S(1)} collective-permute-done((bf16[16,128,384]{2,1,0:T(8,128)(2,1)S(1)}, bf16[16,128,384]{2,1,0:T(8,128)(2,1)S(1)}, u32[]{:S(2)}, u32[]{:S(2)}) %collective-permute-start.5) | collective-permute-done | bytes 1572896 | tf_op jit(solution)/shard_map/ppermute | solution.py:279
  116.0 3.2 %collective-permute-start.8 = (bf16[2,128,384]{2,1,0:T(8,128)(2,1)S(1)}, bf16[2,128,384]{2,1,0:T(8,128)(2,1)S(1)}, u32[]{:S(2)}, u32[]{:S(2)}) collective-permute-start(bf16[2,128,384]{2,1,0:T(8,128)(2,1)S(1)} %get-tuple-element.35), channel_id=1, source_target_pairs={{0,3},{1,0},{2,1},{3,2},{4,7},{5,4},{6,5},{7,6},{8,11},{9,8},{10,9... | collective-permute-start | bytes 589832 | tf_op jit(solution)/shard_map/ppermute | solution.py:279
  121.0 1.9 %collective-permute-done.6 = bf16[2,128,384]{2,1,0:T(8,128)(2,1)S(1)} collective-permute-done((bf16[2,128,384]{2,1,0:T(8,128)(2,1)S(1)}, bf16[2,128,384]{2,1,0:T(8,128)(2,1)S(1)}, u32[]{:S(2)}, u32[]{:S(2)}) %collective-permute-start.6) | collective-permute-done | bytes 196640 | tf_op jit(solution)/shard_map/ppermute | solution.py:279
  123.3 3.2 %collective-permute-start.9 = (bf16[4,128,384]{2,1,0:T(8,128)(2,1)S(1)}, bf16[4,128,384]{2,1,0:T(8,128)(2,1)S(1)}, u32[]{:S(2)}, u32[]{:S(2)}) collective-permute-start(bf16[4,128,384]{2,1,0:T(8,128)(2,1)S(1)} %pad_maximum_fusion.3), channel_id=1, source_target_pairs={{0,3},{1,0},{2,1},{3,2},{4,7},{5,4},{6,5},{7,6},{8,11},{9,8},{10,9... | collective-permute-start | bytes 1179656 | tf_op jit(solution)/shard_map/ppermute | solution.py:279
  126.6 2.2 %collective-permute-done.19.refs_7_ = bf16[4,128,384]{2,1,0:T(8,128)(2,1)S(1)} collective-permute-done((bf16[4,128,384]{2,1,0:T(8,128)(2,1)S(1)}, bf16[4,128,384]{2,1,0:T(8,128)(2,1)S(1)}, u32[]{:S(2)}, u32[]{:S(2)}) %collective-permute-start.19) | collective-permute-done | bytes 393248 | tf_op jit(solution)/shard_map/ppermute | solution.py:279
  128.9 3.7 %collective-permute-done.9.refs_3_ = bf16[4,128,384]{2,1,0:T(8,128)(2,1)S(1)} collective-permute-done((bf16[4,128,384]{2,1,0:T(8,128)(2,1)S(1)}, bf16[4,128,384]{2,1,0:T(8,128)(2,1)S(1)}, u32[]{:S(2)}, u32[]{:S(2)}) %collective-permute-start.9) | collective-permute-done | bytes 393248 | tf_op jit(solution)/shard_map/ppermute | solution.py:279
  132.6 3.5 %collective-permute-done.7.refs_2_ = bf16[4,128,384]{2,1,0:T(8,128)(2,1)S(1)} collective-permute-done((bf16[4,128,384]{2,1,0:T(8,128)(2,1)S(1)}, bf16[4,128,384]{2,1,0:T(8,128)(2,1)S(1)}, u32[]{:S(2)}, u32[]{:S(2)}) %collective-permute-start.7) | collective-permute-done | bytes 393248 | tf_op jit(solution)/shard_map/ppermute | solution.py:279
  136.1 2.0 %finish.1 = f32[4,2,384,128]{3,2,1,0:T(8,128)} custom-call(bf16[4,128,384]{2,1,0:T(8,128)(2,1)S(1)} %get-tuple-element.21.refs_0_, bf16[16,128,384]{2,1,0:T(8,128)(2,1)S(1)} %collective-permute-done.5.refs_1_, bf16[4,128,384]{2,1,0:T(8,128)(2,1)S(1)} %collective-permute-done.7.refs_2_, bf16[4,128,384]{2,1,0:T(8,128)(2,1)S(1)} %collective-permute-done.9.refs_3_, ...), custom_call_target="tpu_custom_call" | custom-call | tf_op jit(solution)/shard_map/finish/pallas_call | solution.py:248
  (61 shorter events, 11.1 us)
Async XLA Ops:
  5.2 27.9 %copy-start.1 = (bf16[2,8,384,512]{3,2,1,0:T(8,128)(2,1)S(1)}, bf16[2,8,384,512]{3,2,1,0:T(8,128)(2,1)}, u32[]{:S(2)}) copy-start(bf16[2,8,384,512]{3,2,1,0:T(8,128)(2,1)} %param.5) | copy-start | bytes 18874372
  9.5 19.2 %copy-start.6 = (s32[384]{0:T(512)S(1)}, s32[384]{0:T(512)}, u32[]{:S(2)}) copy-start(s32[384]{0:T(512)} %mask_ref.1) | copy-start | bytes 4612
  9.5 23.6 %copy-start.4 = (bf16[256,512]{1,0:T(8,128)(2,1)S(1)}, bf16[256,512]{1,0:T(8,128)(2,1)}, u32[]{:S(2)}) copy-start(bf16[256,512]{1,0:T(8,128)(2,1)} %constant.19.clone.table_ref) | copy-start | bytes 786436
  9.5 1.4 %collective-permute-start.10 = (bf16[512,128]{1,0:T(8,128)(2,1)S(1)}, bf16[512,128]{1,0:T(8,128)(2,1)S(1)}, u32[]{:S(2)}, u32[]{:S(2)}) collective-permute-start(bf16[512,128]{1,0:T(8,128)(2,1)S(1)} %get-tuple-element.27), channel_id=1, source_target_pairs={{0,8},{8,0},{16,24},{24,16},{32,40},{40,32},{48,56},{56,48},{64,72... | collective-permute-start | bytes 393224 | tf_op jit(solution)/shard_map/ppermute | solution.py:276
  9.6 3.5 %collective-permute-start = (bf16[512,128]{1,0:T(8,128)(2,1)S(1)}, bf16[512,128]{1,0:T(8,128)(2,1)S(1)}, u32[]{:S(2)}, u32[]{:S(2)}) collective-permute-start(bf16[512,128]{1,0:T(8,128)(2,1)S(1)} %get-tuple-element.20), channel_id=1, source_target_pairs={{0,8},{8,0},{16,24},{24,16},{32,40},{40,32},{48,56},{56,48},{64,72... | collective-permute-start | bytes 393224 | tf_op jit(solution)/shard_map/ppermute | solution.py:276
  10.9 6.4 %collective-permute-start.11 = (bf16[512,128]{1,0:T(8,128)(2,1)S(1)}, bf16[512,128]{1,0:T(8,128)(2,1)S(1)}, u32[]{:S(2)}, u32[]{:S(2)}) collective-permute-start(bf16[512,128]{1,0:T(8,128)(2,1)S(1)} %add.72), channel_id=1, source_target_pairs={{0,16},{8,24},{16,0},{24,8},{32,48},{40,56},{48,32},{56,40},{64,80... | collective-permute-start | bytes 393224 | tf_op jit(solution)/shard_map/ppermute | solution.py:276
  13.1 8.5 %collective-permute-start.1 = (bf16[512,128]{1,0:T(8,128)(2,1)S(1)}, bf16[512,128]{1,0:T(8,128)(2,1)S(1)}, u32[]{:S(2)}, u32[]{:S(2)}) collective-permute-start(bf16[512,128]{1,0:T(8,128)(2,1)S(1)} %add.60), channel_id=1, source_target_pairs={{0,16},{8,24},{16,0},{24,8},{32,48},{40,56},{48,32},{56,40},{64,80... | collective-permute-start | bytes 393224 | tf_op jit(solution)/shard_map/ppermute | solution.py:276
  17.4 8.0 %collective-permute-start.12 = (bf16[512,128]{1,0:T(8,128)(2,1)S(1)}, bf16[512,128]{1,0:T(8,128)(2,1)S(1)}, u32[]{:S(2)}, u32[]{:S(2)}) collective-permute-start(bf16[512,128]{1,0:T(8,128)(2,1)S(1)} %add.73), channel_id=1, source_target_pairs={{0,48},{8,56},{16,32},{24,40},{32,16},{40,24},{48,0},{56,8},{64,11... | collective-permute-start | bytes 393224 | tf_op jit(solution)/shard_map/ppermute | solution.py:276
  21.7 7.0 %collective-permute-start.2 = (bf16[512,128]{1,0:T(8,128)(2,1)S(1)}, bf16[512,128]{1,0:T(8,128)(2,1)S(1)}, u32[]{:S(2)}, u32[]{:S(2)}) collective-permute-start(bf16[512,128]{1,0:T(8,128)(2,1)S(1)} %add.61), channel_id=1, source_target_pairs={{0,48},{8,56},{16,32},{24,40},{32,16},{40,24},{48,0},{56,8},{64,11... | collective-permute-start | bytes 393224 | tf_op jit(solution)/shard_map/ppermute | solution.py:276
  25.4 7.5 %collective-permute-start.13 = (bf16[512,128]{1,0:T(8,128)(2,1)S(1)}, bf16[512,128]{1,0:T(8,128)(2,1)S(1)}, u32[]{:S(2)}, u32[]{:S(2)}) collective-permute-start(bf16[512,128]{1,0:T(8,128)(2,1)S(1)} %add.74), channel_id=1, source_target_pairs={{0,64},{8,72},{16,80},{24,88},{32,96},{40,104},{48,112},{56,120},{... | collective-permute-start | bytes 393224 | tf_op jit(solution)/shard_map/ppermute | solution.py:276
  28.7 12.4 %collective-permute-start.3 = (bf16[512,128]{1,0:T(8,128)(2,1)S(1)}, bf16[512,128]{1,0:T(8,128)(2,1)S(1)}, u32[]{:S(2)}, u32[]{:S(2)}) collective-permute-start(bf16[512,128]{1,0:T(8,128)(2,1)S(1)} %add.62), channel_id=1, source_target_pairs={{0,64},{8,72},{16,80},{24,88},{32,96},{40,104},{48,112},{56,120},{... | collective-permute-start | bytes 393224 | tf_op jit(solution)/shard_map/ppermute | solution.py:276
  33.0 8.7 %copy-start.8 = (bf16[128,256]{1,0:T(8,128)(2,1)S(1)}, bf16[128,256]{1,0:T(8,128)(2,1)}, u32[]{:S(2)}) copy-start(bf16[128,256]{1,0:T(8,128)(2,1)} %constant.20.clone.lag_ref) | copy-start | bytes 196612
  33.0 8.7 %collective-permute-start.14 = (bf16[512,128]{1,0:T(8,128)(2,1)S(1)}, bf16[512,128]{1,0:T(8,128)(2,1)S(1)}, u32[]{:S(2)}, u32[]{:S(2)}) collective-permute-start(bf16[512,128]{1,0:T(8,128)(2,1)S(1)} %add.75.a_ref), channel_id=1, source_target_pairs={{0,8},{8,0},{16,24},{24,16},{32,40},{40,32},{48,56},{56,48},{64,72... | collective-permute-start | bytes 393224 | tf_op jit(solution)/shard_map/ppermute | solution.py:276
  41.2 20.8 %collective-permute-start.4 = (bf16[512,128]{1,0:T(8,128)(2,1)S(1)}, bf16[512,128]{1,0:T(8,128)(2,1)S(1)}, u32[]{:S(2)}, u32[]{:S(2)}) collective-permute-start(bf16[512,128]{1,0:T(8,128)(2,1)S(1)} %add.63.a_ref), channel_id=1, source_target_pairs={{0,8},{8,0},{16,24},{24,16},{32,40},{40,32},{48,56},{56,48},{64,72... | collective-permute-start | bytes 393224 | tf_op jit(solution)/shard_map/ppermute | solution.py:276
  59.2 22.1 %collective-permute-start.17 = (bf16[4,128,384]{2,1,0:T(8,128)(2,1)S(1)}, bf16[4,128,384]{2,1,0:T(8,128)(2,1)S(1)}, u32[]{:S(2)}, u32[]{:S(2)}) collective-permute-start(bf16[4,128,384]{2,1,0:T(8,128)(2,1)S(1)} %get-tuple-element.32), channel_id=1, source_target_pairs={{0,3},{1,0},{2,1},{3,2},{4,7},{5,4},{6,5},{7,6},{8,11},{9,8},{10,9... | collective-permute-start | bytes 1179656 | tf_op jit(solution)/shard_map/ppermute | solution.py:279
  79.6 36.2 %collective-permute-start.5 = (bf16[16,128,384]{2,1,0:T(8,128)(2,1)S(1)}, bf16[16,128,384]{2,1,0:T(8,128)(2,1)S(1)}, u32[]{:S(2)}, u32[]{:S(2)}) collective-permute-start(bf16[16,128,384]{2,1,0:T(8,128)(2,1)S(1)} %get-tuple-element.22), channel_id=1, source_target_pairs={{0,4},{1,5},{2,6},{3,7},{4,0},{5,1},{6,2},{7,3},{8,12},{9,13},{10,... | collective-permute-start | bytes 4718600 | tf_op jit(solution)/shard_map/ppermute | solution.py:279
  81.2 11.8 %collective-permute-start.15 = (bf16[4,128,384]{2,1,0:T(8,128)(2,1)S(1)}, bf16[4,128,384]{2,1,0:T(8,128)(2,1)S(1)}, u32[]{:S(2)}, u32[]{:S(2)}) collective-permute-start(bf16[4,128,384]{2,1,0:T(8,128)(2,1)S(1)} %get-tuple-element.30), channel_id=1, source_target_pairs={{0,1},{1,2},{2,3},{3,0},{4,5},{5,6},{6,7},{7,4},{8,9},{9,10},{10,1... | collective-permute-start | bytes 1179656 | tf_op jit(solution)/shard_map/ppermute | solution.py:279
  81.5 37.7 %collective-permute-start.18 = (bf16[8,128,384]{2,1,0:T(8,128)(2,1)S(1)}, bf16[8,128,384]{2,1,0:T(8,128)(2,1)S(1)}, u32[]{:S(2)}, u32[]{:S(2)}) collective-permute-start(bf16[8,128,384]{2,1,0:T(8,128)(2,1)S(1)} %pad_maximum_fusion.1), channel_id=1, source_target_pairs={{0,3},{1,0},{2,1},{3,2},{4,7},{5,4},{6,5},{7,6},{8,11},{9,8},{10,9... | collective-permute-start | bytes 2359304 | tf_op jit(solution)/shard_map/ppermute | solution.py:279
  93.2 26.0 %collective-permute-start.16 = (bf16[8,128,384]{2,1,0:T(8,128)(2,1)S(1)}, bf16[8,128,384]{2,1,0:T(8,128)(2,1)S(1)}, u32[]{:S(2)}, u32[]{:S(2)}) collective-permute-start(bf16[8,128,384]{2,1,0:T(8,128)(2,1)S(1)} %pad_maximum_fusion), channel_id=1, source_target_pairs={{0,1},{1,2},{2,3},{3,0},{4,5},{5,6},{6,7},{7,4},{8,9},{9,10},{10,1... | collective-permute-start | bytes 2359304 | tf_op jit(solution)/shard_map/ppermute | solution.py:279
  115.9 7.0 %collective-permute-start.6 = (bf16[2,128,384]{2,1,0:T(8,128)(2,1)S(1)}, bf16[2,128,384]{2,1,0:T(8,128)(2,1)S(1)}, u32[]{:S(2)}, u32[]{:S(2)}) collective-permute-start(bf16[2,128,384]{2,1,0:T(8,128)(2,1)S(1)} %get-tuple-element.36), channel_id=1, source_target_pairs={{0,1},{1,2},{2,3},{3,0},{4,5},{5,6},{6,7},{7,4},{8,9},{9,10},{10,1... | collective-permute-start | bytes 589832 | tf_op jit(solution)/shard_map/ppermute | solution.py:279
  116.0 7.0 %collective-permute-start.8 = (bf16[2,128,384]{2,1,0:T(8,128)(2,1)S(1)}, bf16[2,128,384]{2,1,0:T(8,128)(2,1)S(1)}, u32[]{:S(2)}, u32[]{:S(2)}) collective-permute-start(bf16[2,128,384]{2,1,0:T(8,128)(2,1)S(1)} %get-tuple-element.35), channel_id=1, source_target_pairs={{0,3},{1,0},{2,1},{3,2},{4,7},{5,4},{6,5},{7,6},{8,11},{9,8},{10,9... | collective-permute-start | bytes 589832 | tf_op jit(solution)/shard_map/ppermute | solution.py:279
  119.4 9.5 %collective-permute-start.19 = (bf16[4,128,384]{2,1,0:T(8,128)(2,1)S(1)}, bf16[4,128,384]{2,1,0:T(8,128)(2,1)S(1)}, u32[]{:S(2)}, u32[]{:S(2)}) collective-permute-start(bf16[4,128,384]{2,1,0:T(8,128)(2,1)S(1)} %add_convert_fusion), channel_id=1, source_target_pairs={{0,4},{1,5},{2,6},{3,7},{4,0},{5,1},{6,2},{7,3},{8,12},{9,13},{10,... | collective-permute-start | bytes 1179656 | tf_op jit(solution)/shard_map/ppermute | solution.py:279
  123.3 9.3 %collective-permute-start.9 = (bf16[4,128,384]{2,1,0:T(8,128)(2,1)S(1)}, bf16[4,128,384]{2,1,0:T(8,128)(2,1)S(1)}, u32[]{:S(2)}, u32[]{:S(2)}) collective-permute-start(bf16[4,128,384]{2,1,0:T(8,128)(2,1)S(1)} %pad_maximum_fusion.3), channel_id=1, source_target_pairs={{0,3},{1,0},{2,1},{3,2},{4,7},{5,4},{6,5},{7,6},{8,11},{9,8},{10,9... | collective-permute-start | bytes 1179656 | tf_op jit(solution)/shard_map/ppermute | solution.py:279
  126.5 9.6 %collective-permute-start.7 = (bf16[4,128,384]{2,1,0:T(8,128)(2,1)S(1)}, bf16[4,128,384]{2,1,0:T(8,128)(2,1)S(1)}, u32[]{:S(2)}, u32[]{:S(2)}) collective-permute-start(bf16[4,128,384]{2,1,0:T(8,128)(2,1)S(1)} %pad_maximum_fusion.2), channel_id=1, source_target_pairs={{0,1},{1,2},{2,3},{3,0},{4,5},{5,6},{6,7},{7,4},{8,9},{9,10},{10,1... | collective-permute-start | bytes 1179656 | tf_op jit(solution)/shard_map/ppermute | solution.py:279
  (5 other events, 6.7 us)

commit v2 on v1

--- a/solution.py
+++ b/solution.py
@@ -110,7 +110,7 @@
         wsc[:, pl.ds(pl.multiple_of(n * 16, 16), 16), :] = whiten_rows(z)
         return carry
 
-    lax.fori_loop(0, count, one, 0, unroll=2)
+    lax.fori_loop(0, count, one, 0, unroll=16)
     for rel, pair in ((0, (keep0, keep1)), (1, (send0, send1))):
         half = core if rel == 0 else 1 - core
         for t in range(2):
@@ -136,29 +136,31 @@
             pltpu.VMEM((FB, 256, 128), BF16),
             pltpu.SemaphoreType.DMA((STEPS * NSRC,)),
         ],
-        compiler_params=pltpu.CompilerParams(vmem_limit_bytes=32 * 2**20),
+        compiler_params=pltpu.CompilerParams(vmem_limit_bytes=60 * 2**20),
         cost_estimate=pl.CostEstimate(flops=10**9, bytes_accessed=3 * 10**6, transcendentals=0),
         name="source_spectra",
     )(blocks, mask, me, traces, table)
 
 
 def receiver_kernel(traces_ref, table_ref, live_ref, out_ref):
-    z = dot(table_ref[...], traces_ref[0], ((1,), (1,)))
-    out_ref[:, 0] = whiten_rows(z, live_ref[...])
+    for n in range(traces_ref.shape[0]):
+        z = dot(table_ref[...], traces_ref[n], ((1,), (1,)))
+        out_ref[:, n] = whiten_rows(z, live_ref[...])
 
 
 def receiver_spectra(traces, live, table):
     count, channels, length = traces.shape
+    chunk = math.gcd(count, 4)
     return pl.pallas_call(
         receiver_kernel,
-        grid=(count,),
+        grid=(count // chunk,),
         out_shape=jax.ShapeDtypeStruct((FB, count, 16, channels), BF16),
         in_specs=[
-            pl.BlockSpec((1, channels, length), lambda n: (n, 0, 0)),
+            pl.BlockSpec((chunk, channels, length), lambda n: (n, 0, 0)),
             pl.BlockSpec((2 * NF, length), lambda n: (0, 0)),
             pl.BlockSpec((1, channels), lambda n: (0, 0)),
         ],
-        out_specs=pl.BlockSpec((FB, 1, 16, channels), lambda n: (0, n, 0, 0)),
+        out_specs=pl.BlockSpec((FB, chunk, 16, channels), lambda n: (0, n, 0, 0)),
         compiler_params=pltpu.CompilerParams(vmem_limit_bytes=32 * 2**20),
         cost_estimate=pl.CostEstimate(
             flops=2 * count * channels * length * 256, bytes_accessed=10**7, transcendentals=10**6
@@ -186,18 +188,18 @@
         for t in range(2):
             x = ref[t * 256 : (t + 1) * 256, :]
             both[half * 2 + t] = jnp.concatenate([x, swap_parts(x)], axis=1)
-    diagonal = ((iota((8, 256), 0)) == (iota((8, 256), 1) & 7)).astype(F32)
+    diagonal = ((iota((16, 256), 0) & 7) == (iota((16, 256), 1) & 7)).astype(F32).astype(BF16)
 
     def one(u, carry):
         lo, hi = u & 3, u >> 2
         block = hi * 4 + (((lo >> 1) ^ core) << 1) + (lo & 1)
         left = dot(pick[hi], both[lo], ((1,), (1,)))
-        left = (left.reshape(64, 8, 256) * diagonal[None]).reshape(512, 256).astype(BF16)
+        left = (left.astype(BF16).reshape(32, 16, 256) * diagonal[None]).reshape(512, 256)
         out = dot(left, recv_ref[block])
         stacked[:, block] = out.astype(BF16).reshape(32, 16, out.shape[-1])
         return carry
 
-    lax.fori_loop(0, 16, one, 0)
+    lax.fori_loop(0, 16, one, 0, unroll=16)
     lag = lag_ref[...]
     for group, out in zip(groups, outs):
         for place, (first, amount) in group:
@@ -207,7 +209,7 @@
                 out[place + r] = dot(lag, x).astype(BF16)
                 return carry
 
-            lax.fori_loop(0, amount, two, 0)
+            lax.fori_loop(0, amount, two, 0, unroll=4)
 
 
 def correlate(groups, me, a, b, receivers, lags):
@@ -282,18 +284,22 @@
 
     keep0, send0, keep1, send1 = source_spectra(traces, channel_mask, source_blocks, me, table)
 
-    def share(keep, send):
-        mine = keep + chan_swap(send, 1)
-        for bits in (2, 6, 8):
-            mine = mine + chan_swap(mine, bits)
-        return mine, chan_swap(mine, 1)
-
     live = channel_mask.astype(F32)[None]
     receivers = receiver_spectra(traces, live, table).reshape(FB, 256, channels)
 
-    a, b = share(keep0, send0)
+    def share(keep, send, beside):
+        mine = keep + chan_swap(send, 1)
+        mine = mine + chan_swap(mine, 2)
+        mine, beside = lax.optimization_barrier((mine, beside))
+        for bits in (6, 8):
+            mine = mine + chan_swap(mine, bits)
+        return mine, chan_swap(mine, 1), beside
+
+    a, b, receivers = share(keep0, send0, receivers)
     groups = [((0, (16, 16)),)] + [((0, (dx * 4, 4)),) for dx in range(4)]
     away, o0, o1, o2, o3 = correlate(groups, me, a, b, receivers, lags)
+    share1 = share(keep1, send1, receivers)
+    a, b, receivers, away = lax.optimization_barrier((*share1, away))
     got = win_to(away, 1, 0)
     up = win_to(add(o2[:2], got[8:10]), 0, 1)
     down = win_to(add(o2[2:], got[10:12]), 0, -1)
@@ -301,7 +307,6 @@
     left = jnp.concatenate([add(o3[:2], got[12:14]), add(o3[2:], got[14:16], down)])
     first = (o0, got, win_to(right, 0, 1), win_to(left, 0, -1))
 
-    a, b = share(keep1, send1)
     groups = [
         ((0, (0, 4)), (4, (16, 4))),
         ((0, (4, 4)), (4, (20, 4))),

time: 138 us -> 114 us (0.83)
  Pallas kernels: 47.8 us -> 26.4 us
  waiting for transfers between devices: 50.4 us -> 47.2 us
  local copies, waits for them, and re-layouts: 6.83 us -> 4.52 us
  other arithmetic: 1.4 us -> 2.85 us
    pallas_call x2, Pallas kernels: 35 us -> 15.8 us  [correlate(): pl.pallas_call(functools.partial(correlate_kernel, groups), out_shape=[ja...]
    pallas_call x1, Pallas kernels: 6.43 us -> 3.47 us  [receiver_spectra(): pl.pallas_call(receiver_kernel, grid=(count // chunk,), out_shape=jax.Sha...]
    ppermute x10, waiting for transfers between devices: 8.38 us -> 5.53 us  [chan_swap(): return lax.ppermute(x, 'chan', [(i, i ^ bits) for i in range(16)])]
    unnamed x18 -> x14, local copies, waits for them, and re-layouts: 6.74 us -> 4.44 us
  transfers between devices with their start and end apart: 20 -> 20, of which waited for: 10 -> 12; matrix products, arithmetic and copies ran while one was open for 1% -> 2% of each run, Pallas kernels for 30% -> 10%
where the time goes in v2:
time: 114 us; the launch traced here: 113 us
  waiting for transfers between devices  47.2 us (41%)
  starting transfers between devices  31.8 us (28%)
  Pallas kernels  26.4 us (23%)
  local copies, waits for them, and re-layouts  4.52 us (4%)
  other arithmetic  2.85 us (2%)
    ppermute x10, waiting for transfers between devices, win_to(): lax.ppermute(x, 'win', [(y * 4 + i, (y ^ dy) * 4 + (i + dx) % 4) for y in...  41.7 us
    ppermute x10, starting transfers between devices, chan_swap(): return lax.ppermute(x, 'chan', [(i, i ^ bits) for i in range(16)])  16.5 us
    pallas_call x2, Pallas kernels, correlate(): pl.pallas_call(functools.partial(correlate_kernel, groups), out_shape=[ja...  15.8 us
    ppermute x10, starting transfers between devices, win_to(): lax.ppermute(x, 'win', [(y * 4 + i, (y ^ dy) * 4 + (i + dx) % 4) for y in...  15.3 us
    ppermute x10, waiting for transfers between devices, chan_swap(): return lax.ppermute(x, 'chan', [(i, i ^ bits) for i in range(16)])  5.53 us
    pallas_call x1, Pallas kernels, source_spectra(): pl.pallas_call(source_kernel, out_shape=[shape] * 4, in_specs=[smem, smem...  5.1 us
    unnamed x14, local copies, waits for them, and re-layouts  4.44 us
    pallas_call x1, Pallas kernels, receiver_spectra(): pl.pallas_call(receiver_kernel, grid=(count // chunk,), out_shape=jax.Sha...  3.47 us
  transfers between devices with their start and end apart: 20, of which 12 were waited for; matrix products, arithmetic and copies ran while one was open for 2% of the time, Pallas kernels for 10%

profile of v2, /device:TPU:0, one launch (start us, length us, event | category | flops | bytes accessed | tf_op | source)
XLA Modules:
  0.0 113.0 jit_solution(2669119418275917300)
XLA Ops:
  0.6 5.1 %source_spectra.1 = (bf16[512,128]{1,0:T(8,128)(2,1)}, bf16[512,128]{1,0:T(8,128)(2,1)}, bf16[512,128]{1,0:T(8,128)(2,1)}, bf16[512,128]{1,0:T(8,128)(2,1)}) custom-call(s32[2,4]{1,0:T(2,128)} %blocks_ref.1, s32[384]{0:T(512)} %mask_ref.1, s32[4]{0:T(128)} %pad_add_fusion.me_ref, bf16[16,384,512]{2,1,0:T(8,128)(2,1)} %bitcast.6, ...), custom_call_target="tpu_custom_call" | custom-call | flops 1000000000 | bytes 3000000 | tf_op jit(solution)/shard_map/source_spectra/pallas_call | solution.py:129
  8.3 2.1 %collective-permute-start.1 = (bf16[512,128]{1,0:T(8,128)(2,1)S(1)}, bf16[512,128]{1,0:T(8,128)(2,1)S(1)}, u32[]{:S(2)}, u32[]{:S(2)}) collective-permute-start(bf16[512,128]{1,0:T(8,128)(2,1)S(1)} %add.60), channel_id=1, source_target_pairs={{0,16},{8,24},{16,0},{24,8},{32,48},{40,56},{48,32},{56,40},{64,80... | collective-permute-start | bytes 393224 | tf_op jit(solution)/shard_map/ppermute | solution.py:278
  10.4 2.8 %copy-done = bf16[2,8,384,512]{3,2,1,0:T(8,128)(2,1)S(1)} copy-done((bf16[2,8,384,512]{3,2,1,0:T(8,128)(2,1)S(1)}, bf16[2,8,384,512]{3,2,1,0:T(8,128)(2,1)}, u32[]{:S(2)}) %copy-start) | copy-done | bytes 6291480
  13.2 3.5 %receiver_spectra.1 = bf16[16,16,16,384]{3,2,1,0:T(8,128)(2,1)S(1)} custom-call(bf16[16,384,512]{2,1,0:T(8,128)(2,1)S(1)} %bitcast.7, bf16[256,512]{1,0:T(8,128)(2,1)S(1)} %copy-done.2, f32[1,384]{1,0:T(1,128)S(1)} %broadcast_in_dim.3.live_ref), custom_call_target="tpu_custom_call" | custom-call | flops 1610612736 | bytes 10000000 | tf_op jit(solution)/shard_map/receiver_spectra/pallas_call | solution.py:154
  16.7 1.6 %copy-done.1 = bf16[16,16,16,384]{3,2,1,0:T(8,128)(2,1)} copy-done((bf16[16,16,16,384]{3,2,1,0:T(8,128)(2,1)}, bf16[16,16,16,384]{3,2,1,0:T(8,128)(2,1)S(1)}, u32[]{:S(2)}) %copy-start.1) | copy-done | bytes 3145752
  18.5 4.2 %collective-permute-start.2 = (bf16[512,128]{1,0:T(8,128)(2,1)S(1)}, bf16[512,128]{1,0:T(8,128)(2,1)S(1)}, u32[]{:S(2)}, u32[]{:S(2)}) collective-permute-start(bf16[512,128]{1,0:T(8,128)(2,1)S(1)} %add.61), channel_id=1, source_target_pairs={{0,48},{8,56},{16,32},{24,40},{32,16},{40,24},{48,0},{56,8},{64,11... | collective-permute-start | bytes 393224 | tf_op jit(solution)/shard_map/ppermute | solution.py:278
  23.8 2.6 %collective-permute-start.7 = (bf16[512,128]{1,0:T(8,128)(2,1)S(1)}, bf16[512,128]{1,0:T(8,128)(2,1)S(1)}, u32[]{:S(2)}, u32[]{:S(2)}) collective-permute-start(bf16[512,128]{1,0:T(8,128)(2,1)S(1)} %add.65), channel_id=1, source_target_pairs={{0,48},{8,56},{16,32},{24,40},{32,16},{40,24},{48,0},{56,8},{64,11... | collective-permute-start | bytes 393224 | tf_op jit(solution)/shard_map/ppermute | solution.py:278
  26.4 3.3 %collective-permute-start.3 = (bf16[512,128]{1,0:T(8,128)(2,1)S(1)}, bf16[512,128]{1,0:T(8,128)(2,1)S(1)}, u32[]{:S(2)}, u32[]{:S(2)}) collective-permute-start(bf16[512,128]{1,0:T(8,128)(2,1)S(1)} %add.62), channel_id=1, source_target_pairs={{0,64},{8,72},{16,80},{24,88},{32,96},{40,104},{48,112},{56,120},{... | collective-permute-start | bytes 393224 | tf_op jit(solution)/shard_map/ppermute | solution.py:278
  30.1 3.3 %collective-permute-start.8 = (bf16[512,128]{1,0:T(8,128)(2,1)S(1)}, bf16[512,128]{1,0:T(8,128)(2,1)S(1)}, u32[]{:S(2)}, u32[]{:S(2)}) collective-permute-start(bf16[512,128]{1,0:T(8,128)(2,1)S(1)} %add.66), channel_id=1, source_target_pairs={{0,64},{8,72},{16,80},{24,88},{32,96},{40,104},{48,112},{56,120},{... | collective-permute-start | bytes 393224 | tf_op jit(solution)/shard_map/ppermute | solution.py:278
  33.7 2.9 %collective-permute-done.8 = bf16[512,128]{1,0:T(8,128)(2,1)S(1)} collective-permute-done((bf16[512,128]{1,0:T(8,128)(2,1)S(1)}, bf16[512,128]{1,0:T(8,128)(2,1)S(1)}, u32[]{:S(2)}, u32[]{:S(2)}) %collective-permute-start.8) | collective-permute-done | bytes 131104 | tf_op jit(solution)/shard_map/ppermute | solution.py:278
  37.0 8.2 %correlate.2 = (bf16[16,128,384]{2,1,0:T(8,128)(2,1)S(1)}, bf16[4,128,384]{2,1,0:T(8,128)(2,1)S(1)}, bf16[4,128,384]{2,1,0:T(8,128)(2,1)S(1)}, bf16[4,128,384]{2,1,0:T(8,128)(2,1)S(1)}, bf16[4,128,384]{2,1,0:T(8,128)(2,1)S(1)}) custom-call(s32[4]{0:T(128)S(1)} %copy-done.3, bf16[512,128]{1,0:T(8,128)(2,1)S(1)} %add.63.a_ref, ...), custom_call_target="tpu_custom_call" | custom-call | flops 8000000000 | bytes 10000000 | tf_op jit(solution)/shard_map/correlate/pallas_call | solution.py:220
  45.1 7.6 %correlate.3 = (bf16[8,128,384]{2,1,0:T(8,128)(2,1)S(1)}, bf16[8,128,384]{2,1,0:T(8,128)(2,1)S(1)}, bf16[4,128,384]{2,1,0:T(8,128)(2,1)S(1)}, bf16[4,128,384]{2,1,0:T(8,128)(2,1)S(1)}, bf16[8,128,384]{2,1,0:T(8,128)(2,1)S(1)}) custom-call(s32[4]{0:T(128)S(1)} %copy-done.3, bf16[512,128]{1,0:T(8,128)(2,1)S(1)} %add.67.a_ref, ...), custom_call_target="tpu_custom_call" | custom-call | flops 8000000000 | bytes 10000000 | tf_op jit(solution)/shard_map/correlate/pallas_call | solution.py:220
  52.7 2.8 %collective-permute-start.17 = (bf16[4,128,384]{2,1,0:T(8,128)(2,1)S(1)}, bf16[4,128,384]{2,1,0:T(8,128)(2,1)S(1)}, u32[]{:S(2)}, u32[]{:S(2)}) collective-permute-start(bf16[4,128,384]{2,1,0:T(8,128)(2,1)S(1)} %get-tuple-element.48), channel_id=1, source_target_pairs={{0,3},{1,0},{2,1},{3,2},{4,7},{5,4},{6,5},{7,6},{8,11},{9,8},{10,9... | collective-permute-start | bytes 1179656 | tf_op jit(solution)/shard_map/ppermute | solution.py:281
  55.6 1.6 %collective-permute-start.10 = (bf16[16,128,384]{2,1,0:T(8,128)(2,1)S(1)}, bf16[16,128,384]{2,1,0:T(8,128)(2,1)S(1)}, u32[]{:S(2)}, u32[]{:S(2)}) collective-permute-start(bf16[16,128,384]{2,1,0:T(8,128)(2,1)S(1)} %get-tuple-element.37), channel_id=1, source_target_pairs={{0,4},{1,5},{2,6},{3,7},{4,0},{5,1},{6,2},{7,3},{8,12},{9,13},{10,... | collective-permute-start | bytes 4718600 | tf_op jit(solution)/shard_map/ppermute | solution.py:281
  57.2 7.3 %collective-permute-done.17 = bf16[4,128,384]{2,1,0:T(8,128)(2,1)S(1)} collective-permute-done((bf16[4,128,384]{2,1,0:T(8,128)(2,1)S(1)}, bf16[4,128,384]{2,1,0:T(8,128)(2,1)S(1)}, u32[]{:S(2)}, u32[]{:S(2)}) %collective-permute-start.17) | collective-permute-done | bytes 393248 | tf_op jit(solution)/shard_map/ppermute | solution.py:281
  64.8 3.8 %collective-permute-start.18 = (bf16[8,128,384]{2,1,0:T(8,128)(2,1)S(1)}, bf16[8,128,384]{2,1,0:T(8,128)(2,1)S(1)}, u32[]{:S(2)}, u32[]{:S(2)}) collective-permute-start(bf16[8,128,384]{2,1,0:T(8,128)(2,1)S(1)} %pad_maximum_fusion.1), channel_id=1, source_target_pairs={{0,3},{1,0},{2,1},{3,2},{4,7},{5,4},{6,5},{7,6},{8,11},{9,8},{10,9... | collective-permute-start | bytes 2359304 | tf_op jit(solution)/shard_map/ppermute | solution.py:281
  69.6 22.5 %collective-permute-done.10.refs_1_ = bf16[16,128,384]{2,1,0:T(8,128)(2,1)S(1)} collective-permute-done((bf16[16,128,384]{2,1,0:T(8,128)(2,1)S(1)}, bf16[16,128,384]{2,1,0:T(8,128)(2,1)S(1)}, u32[]{:S(2)}, u32[]{:S(2)}) %collective-permute-start.10) | collective-permute-done | bytes 1572896 | tf_op jit(solution)/shard_map/ppermute | solution.py:281
  93.1 1.2 %collective-permute-start.11 = (bf16[2,128,384]{2,1,0:T(8,128)(2,1)S(1)}, bf16[2,128,384]{2,1,0:T(8,128)(2,1)S(1)}, u32[]{:S(2)}, u32[]{:S(2)}) collective-permute-start(bf16[2,128,384]{2,1,0:T(8,128)(2,1)S(1)} %get-tuple-element.52), channel_id=1, source_target_pairs={{0,1},{1,2},{2,3},{3,0},{4,5},{5,6},{6,7},{7,4},{8,9},{9,10},{10,1... | collective-permute-start | bytes 589832 | tf_op jit(solution)/shard_map/ppermute | solution.py:281
  94.4 1.7 %collective-permute-start.19 = (bf16[4,128,384]{2,1,0:T(8,128)(2,1)S(1)}, bf16[4,128,384]{2,1,0:T(8,128)(2,1)S(1)}, u32[]{:S(2)}, u32[]{:S(2)}) collective-permute-start(bf16[4,128,384]{2,1,0:T(8,128)(2,1)S(1)} %add_convert_fusion), channel_id=1, source_target_pairs={{0,4},{1,5},{2,6},{3,7},{4,0},{5,1},{6,2},{7,3},{8,12},{9,13},{10,... | collective-permute-start | bytes 1179656 | tf_op jit(solution)/shard_map/ppermute | solution.py:281
  96.1 2.3 %collective-permute-done.13 = bf16[2,128,384]{2,1,0:T(8,128)(2,1)S(1)} collective-permute-done((bf16[2,128,384]{2,1,0:T(8,128)(2,1)S(1)}, bf16[2,128,384]{2,1,0:T(8,128)(2,1)S(1)}, u32[]{:S(2)}, u32[]{:S(2)}) %collective-permute-start.13) | collective-permute-done | bytes 196640 | tf_op jit(solution)/shard_map/ppermute | solution.py:281
  98.4 1.8 %collective-permute-done.11 = bf16[2,128,384]{2,1,0:T(8,128)(2,1)S(1)} collective-permute-done((bf16[2,128,384]{2,1,0:T(8,128)(2,1)S(1)}, bf16[2,128,384]{2,1,0:T(8,128)(2,1)S(1)}, u32[]{:S(2)}, u32[]{:S(2)}) %collective-permute-start.11) | collective-permute-done | bytes 196640 | tf_op jit(solution)/shard_map/ppermute | solution.py:281
  100.6 3.3 %collective-permute-start.14 = (bf16[4,128,384]{2,1,0:T(8,128)(2,1)S(1)}, bf16[4,128,384]{2,1,0:T(8,128)(2,1)S(1)}, u32[]{:S(2)}, u32[]{:S(2)}) collective-permute-start(bf16[4,128,384]{2,1,0:T(8,128)(2,1)S(1)} %pad_maximum_fusion.3), channel_id=1, source_target_pairs={{0,3},{1,0},{2,1},{3,2},{4,7},{5,4},{6,5},{7,6},{8,11},{9,8},{10,9... | collective-permute-start | bytes 1179656 | tf_op jit(solution)/shard_map/ppermute | solution.py:281
  104.3 6.6 %collective-permute-done.12.refs_2_ = bf16[4,128,384]{2,1,0:T(8,128)(2,1)S(1)} collective-permute-done((bf16[4,128,384]{2,1,0:T(8,128)(2,1)S(1)}, bf16[4,128,384]{2,1,0:T(8,128)(2,1)S(1)}, u32[]{:S(2)}, u32[]{:S(2)}) %collective-permute-start.12) | collective-permute-done | bytes 393248 | tf_op jit(solution)/shard_map/ppermute | solution.py:281
  111.0 2.0 %finish.1 = f32[4,2,384,128]{3,2,1,0:T(8,128)} custom-call(bf16[4,128,384]{2,1,0:T(8,128)(2,1)S(1)} %get-tuple-element.31.refs_0_, bf16[16,128,384]{2,1,0:T(8,128)(2,1)S(1)} %collective-permute-done.10.refs_1_, bf16[4,128,384]{2,1,0:T(8,128)(2,1)S(1)} %collective-permute-done.12.refs_2_, bf16[4,128,384]{2,1,0:T(8,128)(2,1)S(1)} %collective-permute-done.14.refs_3_, ...), custom_call_target="tpu_custom_call" | custom-call | tf_op jit(solution)/shard_map/finish/pallas_call | solution.py:250
  (57 shorter events, 8.9 us)
Async XLA Ops:
  0.6 5.7 %copy-start.6 = (s32[384]{0:T(512)S(1)}, s32[384]{0:T(512)}, u32[]{:S(2)}) copy-start(s32[384]{0:T(512)} %mask_ref.1) | copy-start | bytes 4612
  0.6 9.8 %copy-start.2 = (bf16[256,512]{1,0:T(8,128)(2,1)S(1)}, bf16[256,512]{1,0:T(8,128)(2,1)}, u32[]{:S(2)}) copy-start(bf16[256,512]{1,0:T(8,128)(2,1)} %constant.19.clone.table_ref) | copy-start | bytes 786436
  5.7 1.6 %collective-permute-start = (bf16[512,128]{1,0:T(8,128)(2,1)}, bf16[512,128]{1,0:T(8,128)(2,1)S(1)}, u32[]{:S(2)}, u32[]{:S(2)}) collective-permute-start(bf16[512,128]{1,0:T(8,128)(2,1)} %get-tuple-element.28), channel_id=1, source_target_pairs={{0,8},{8,0},{16,24},{24,16},{32,40},{40,32},{48,56},{56,48},{64,72... | collective-permute-start | bytes 393224 | tf_op jit(solution)/shard_map/ppermute | solution.py:278
  5.8 12.5 %collective-permute-start.5 = (bf16[512,128]{1,0:T(8,128)(2,1)}, bf16[512,128]{1,0:T(8,128)(2,1)S(1)}, u32[]{:S(2)}, u32[]{:S(2)}) collective-permute-start(bf16[512,128]{1,0:T(8,128)(2,1)} %get-tuple-element.33), channel_id=1, source_target_pairs={{0,8},{8,0},{16,24},{24,16},{32,40},{40,32},{48,56},{56,48},{64,72... | collective-permute-start | bytes 393224 | tf_op jit(solution)/shard_map/ppermute | solution.py:278
  8.3 10.2 %collective-permute-start.1 = (bf16[512,128]{1,0:T(8,128)(2,1)S(1)}, bf16[512,128]{1,0:T(8,128)(2,1)S(1)}, u32[]{:S(2)}, u32[]{:S(2)}) collective-permute-start(bf16[512,128]{1,0:T(8,128)(2,1)S(1)} %add.60), channel_id=1, source_target_pairs={{0,16},{8,24},{16,0},{24,8},{32,48},{40,56},{48,32},{56,40},{64,80... | collective-permute-start | bytes 393224 | tf_op jit(solution)/shard_map/ppermute | solution.py:278
  18.3 18.6 %copy-start.3 = (s32[4]{0:T(128)S(1)}, s32[4]{0:T(128)}, u32[]{:S(2)}) copy-start(s32[4]{0:T(128)} %pad_add_fusion.me_ref) | copy-start | bytes 52
  18.3 18.6 %copy-start.4 = (bf16[128,256]{1,0:T(8,128)(2,1)S(1)}, bf16[128,256]{1,0:T(8,128)(2,1)}, u32[]{:S(2)}) copy-start(bf16[128,256]{1,0:T(8,128)(2,1)} %constant.20.clone.lag_ref) | copy-start | bytes 196612
  18.4 5.4 %collective-permute-start.6 = (bf16[512,128]{1,0:T(8,128)(2,1)S(1)}, bf16[512,128]{1,0:T(8,128)(2,1)S(1)}, u32[]{:S(2)}, u32[]{:S(2)}) collective-permute-start(bf16[512,128]{1,0:T(8,128)(2,1)S(1)} %add.64), channel_id=1, source_target_pairs={{0,16},{8,24},{16,0},{24,8},{32,48},{40,56},{48,32},{56,40},{64,80... | collective-permute-start | bytes 393224 | tf_op jit(solution)/shard_map/ppermute | solution.py:278
  18.5 7.8 %collective-permute-start.2 = (bf16[512,128]{1,0:T(8,128)(2,1)S(1)}, bf16[512,128]{1,0:T(8,128)(2,1)S(1)}, u32[]{:S(2)}, u32[]{:S(2)}) collective-permute-start(bf16[512,128]{1,0:T(8,128)(2,1)S(1)} %add.61), channel_id=1, source_target_pairs={{0,48},{8,56},{16,32},{24,40},{32,16},{40,24},{48,0},{56,8},{64,11... | collective-permute-start | bytes 393224 | tf_op jit(solution)/shard_map/ppermute | solution.py:278
  23.8 6.3 %collective-permute-start.7 = (bf16[512,128]{1,0:T(8,128)(2,1)S(1)}, bf16[512,128]{1,0:T(8,128)(2,1)S(1)}, u32[]{:S(2)}, u32[]{:S(2)}) collective-permute-start(bf16[512,128]{1,0:T(8,128)(2,1)S(1)} %add.65), channel_id=1, source_target_pairs={{0,48},{8,56},{16,32},{24,40},{32,16},{40,24},{48,0},{56,8},{64,11... | collective-permute-start | bytes 393224 | tf_op jit(solution)/shard_map/ppermute | solution.py:278
  26.4 7.2 %collective-permute-start.3 = (bf16[512,128]{1,0:T(8,128)(2,1)S(1)}, bf16[512,128]{1,0:T(8,128)(2,1)S(1)}, u32[]{:S(2)}, u32[]{:S(2)}) collective-permute-start(bf16[512,128]{1,0:T(8,128)(2,1)S(1)} %add.62), channel_id=1, source_target_pairs={{0,64},{8,72},{16,80},{24,88},{32,96},{40,104},{48,112},{56,120},{... | collective-permute-start | bytes 393224 | tf_op jit(solution)/shard_map/ppermute | solution.py:278
  30.1 6.6 %collective-permute-start.8 = (bf16[512,128]{1,0:T(8,128)(2,1)S(1)}, bf16[512,128]{1,0:T(8,128)(2,1)S(1)}, u32[]{:S(2)}, u32[]{:S(2)}) collective-permute-start(bf16[512,128]{1,0:T(8,128)(2,1)S(1)} %add.66), channel_id=1, source_target_pairs={{0,64},{8,72},{16,80},{24,88},{32,96},{40,104},{48,112},{56,120},{... | collective-permute-start | bytes 393224 | tf_op jit(solution)/shard_map/ppermute | solution.py:278
  33.6 3.3 %collective-permute-start.4 = (bf16[512,128]{1,0:T(8,128)(2,1)S(1)}, bf16[512,128]{1,0:T(8,128)(2,1)S(1)}, u32[]{:S(2)}, u32[]{:S(2)}) collective-permute-start(bf16[512,128]{1,0:T(8,128)(2,1)S(1)} %add.63.a_ref), channel_id=1, source_target_pairs={{0,8},{8,0},{16,24},{24,16},{32,40},{40,32},{48,56},{56,48},{64,72... | collective-permute-start | bytes 393224 | tf_op jit(solution)/shard_map/ppermute | solution.py:278
  36.7 8.5 %collective-permute-start.9 = (bf16[512,128]{1,0:T(8,128)(2,1)S(1)}, bf16[512,128]{1,0:T(8,128)(2,1)S(1)}, u32[]{:S(2)}, u32[]{:S(2)}) collective-permute-start(bf16[512,128]{1,0:T(8,128)(2,1)S(1)} %add.67.a_ref), channel_id=1, source_target_pairs={{0,8},{8,0},{16,24},{24,16},{32,40},{40,32},{48,56},{56,48},{64,72... | collective-permute-start | bytes 393224 | tf_op jit(solution)/shard_map/ppermute | solution.py:278
  52.7 11.8 %collective-permute-start.17 = (bf16[4,128,384]{2,1,0:T(8,128)(2,1)S(1)}, bf16[4,128,384]{2,1,0:T(8,128)(2,1)S(1)}, u32[]{:S(2)}, u32[]{:S(2)}) collective-permute-start(bf16[4,128,384]{2,1,0:T(8,128)(2,1)S(1)} %get-tuple-element.48), channel_id=1, source_target_pairs={{0,3},{1,0},{2,1},{3,2},{4,7},{5,4},{6,5},{7,6},{8,11},{9,8},{10,9... | collective-permute-start | bytes 1179656 | tf_op jit(solution)/shard_map/ppermute | solution.py:281
  55.6 36.5 %collective-permute-start.10 = (bf16[16,128,384]{2,1,0:T(8,128)(2,1)S(1)}, bf16[16,128,384]{2,1,0:T(8,128)(2,1)S(1)}, u32[]{:S(2)}, u32[]{:S(2)}) collective-permute-start(bf16[16,128,384]{2,1,0:T(8,128)(2,1)S(1)} %get-tuple-element.37), channel_id=1, source_target_pairs={{0,4},{1,5},{2,6},{3,7},{4,0},{5,1},{6,2},{7,3},{8,12},{9,13},{10,... | collective-permute-start | bytes 4718600 | tf_op jit(solution)/shard_map/ppermute | solution.py:281
  57.1 12.1 %collective-permute-start.15 = (bf16[4,128,384]{2,1,0:T(8,128)(2,1)S(1)}, bf16[4,128,384]{2,1,0:T(8,128)(2,1)S(1)}, u32[]{:S(2)}, u32[]{:S(2)}) collective-permute-start(bf16[4,128,384]{2,1,0:T(8,128)(2,1)S(1)} %get-tuple-element.46), channel_id=1, source_target_pairs={{0,1},{1,2},{2,3},{3,0},{4,5},{5,6},{6,7},{7,4},{8,9},{9,10},{10,1... | collective-permute-start | bytes 1179656 | tf_op jit(solution)/shard_map/ppermute | solution.py:281
  64.8 29.5 %collective-permute-start.18 = (bf16[8,128,384]{2,1,0:T(8,128)(2,1)S(1)}, bf16[8,128,384]{2,1,0:T(8,128)(2,1)S(1)}, u32[]{:S(2)}, u32[]{:S(2)}) collective-permute-start(bf16[8,128,384]{2,1,0:T(8,128)(2,1)S(1)} %pad_maximum_fusion.1), channel_id=1, source_target_pairs={{0,3},{1,0},{2,1},{3,2},{4,7},{5,4},{6,5},{7,6},{8,11},{9,8},{10,9... | collective-permute-start | bytes 2359304 | tf_op jit(solution)/shard_map/ppermute | solution.py:281
  69.5 24.8 %collective-permute-start.16 = (bf16[8,128,384]{2,1,0:T(8,128)(2,1)S(1)}, bf16[8,128,384]{2,1,0:T(8,128)(2,1)S(1)}, u32[]{:S(2)}, u32[]{:S(2)}) collective-permute-start(bf16[8,128,384]{2,1,0:T(8,128)(2,1)S(1)} %pad_maximum_fusion), channel_id=1, source_target_pairs={{0,1},{1,2},{2,3},{3,0},{4,5},{5,6},{6,7},{7,4},{8,9},{9,10},{10,1... | collective-permute-start | bytes 2359304 | tf_op jit(solution)/shard_map/ppermute | solution.py:281
  92.2 6.2 %collective-permute-start.13 = (bf16[2,128,384]{2,1,0:T(8,128)(2,1)S(1)}, bf16[2,128,384]{2,1,0:T(8,128)(2,1)S(1)}, u32[]{:S(2)}, u32[]{:S(2)}) collective-permute-start(bf16[2,128,384]{2,1,0:T(8,128)(2,1)S(1)} %get-tuple-element.51), channel_id=1, source_target_pairs={{0,3},{1,0},{2,1},{3,2},{4,7},{5,4},{6,5},{7,6},{8,11},{9,8},{10,9... | collective-permute-start | bytes 589832 | tf_op jit(solution)/shard_map/ppermute | solution.py:281
  93.1 7.1 %collective-permute-start.11 = (bf16[2,128,384]{2,1,0:T(8,128)(2,1)S(1)}, bf16[2,128,384]{2,1,0:T(8,128)(2,1)S(1)}, u32[]{:S(2)}, u32[]{:S(2)}) collective-permute-start(bf16[2,128,384]{2,1,0:T(8,128)(2,1)S(1)} %get-tuple-element.52), channel_id=1, source_target_pairs={{0,1},{1,2},{2,3},{3,0},{4,5},{5,6},{6,7},{7,4},{8,9},{9,10},{10,1... | collective-permute-start | bytes 589832 | tf_op jit(solution)/shard_map/ppermute | solution.py:281
  94.4 9.9 %collective-permute-start.19 = (bf16[4,128,384]{2,1,0:T(8,128)(2,1)S(1)}, bf16[4,128,384]{2,1,0:T(8,128)(2,1)S(1)}, u32[]{:S(2)}, u32[]{:S(2)}) collective-permute-start(bf16[4,128,384]{2,1,0:T(8,128)(2,1)S(1)} %add_convert_fusion), channel_id=1, source_target_pairs={{0,4},{1,5},{2,6},{3,7},{4,0},{5,1},{6,2},{7,3},{8,12},{9,13},{10,... | collective-permute-start | bytes 1179656 | tf_op jit(solution)/shard_map/ppermute | solution.py:281
  100.5 10.5 %collective-permute-start.12 = (bf16[4,128,384]{2,1,0:T(8,128)(2,1)S(1)}, bf16[4,128,384]{2,1,0:T(8,128)(2,1)S(1)}, u32[]{:S(2)}, u32[]{:S(2)}) collective-permute-start(bf16[4,128,384]{2,1,0:T(8,128)(2,1)S(1)} %pad_maximum_fusion.2), channel_id=1, source_target_pairs={{0,1},{1,2},{2,3},{3,0},{4,5},{5,6},{6,7},{7,4},{8,9},{9,10},{10,1... | collective-permute-start | bytes 1179656 | tf_op jit(solution)/shard_map/ppermute | solution.py:281
  100.6 10.3 %collective-permute-start.14 = (bf16[4,128,384]{2,1,0:T(8,128)(2,1)S(1)}, bf16[4,128,384]{2,1,0:T(8,128)(2,1)S(1)}, u32[]{:S(2)}, u32[]{:S(2)}) collective-permute-start(bf16[4,128,384]{2,1,0:T(8,128)(2,1)S(1)} %pad_maximum_fusion.3), channel_id=1, source_target_pairs={{0,3},{1,0},{2,1},{3,2},{4,7},{5,4},{6,5},{7,6},{8,11},{9,8},{10,9... | collective-permute-start | bytes 1179656 | tf_op jit(solution)/shard_map/ppermute | solution.py:281
  (3 other events, 9.6 us)

commit v3 on v0

v3 whole, which is shorter than its diff:
```python
import functools
import math

import jax
import jax.numpy as jnp
import ml_dtypes
import numpy as np
from jax import lax
from jax.experimental import pallas as pl
from jax.experimental.pallas import tpu as pltpu
from jax.sharding import PartitionSpec as P

NF = 128
F_LO = 8
NLAG = 128
VSB = 8
NSRC = 4
STEPS = 2
WATER_LEVEL = 0.05
TINY_ENERGY = 1e-06

FB = 16
BF16 = jnp.bfloat16
F32 = jnp.float32
MB = 2**20

PLACES = ((0, 0), (0, 1), (0, 2), (0, 3), (1, 0), (1, 1), (1, 3))
KEPT = (((0, 0), (0, 1), (0, 2), (0, 3)), ((0, 0), (0, 3), (1, 0), (1, 3)), ((0, 0), (0, 1), (1, 0), (1, 1)))
PAIRS = ((1, 0), (0, 1), (0, 3))
PARTS_12 = (
    ((1, (1, 0), 0, 2), (1, (1, 3), 0, 2), (2, (1, 0), 0, 2), (2, (1, 1), 0, 2)),
    ((2, (0, 1), 2, 2), (2, (1, 1), 2, 2)),
    ((1, (0, 3), 2, 2), (1, (1, 3), 2, 2)),
    ((1, (0, 0), 0, 4),),
    ((1, (0, 3), 0, 2),),
    ((1, (1, 0), 2, 2),),
    ((2, (0, 0), 0, 4),),
    ((2, (0, 1), 0, 2),),
    ((2, (1, 0), 2, 2),),
)
PARTS_0 = (
    ((0, (0, 2), 0, 2),),
    ((0, (0, 2), 2, 2),),
    ((0, (0, 0), 0, 4),),
    ((0, (0, 1), 0, 4),),
    ((0, (0, 3), 0, 4),),
)


def band_rows():
    row = np.arange(2 * NF)
    return F_LO + (row // 16) * 8 + row % 8, (row // 8) % 2


def dft_rows(length):
    bins, part = band_rows()
    t = np.arange(length)
    angle = (t[None, :] * bins[:, None] % length) * (2.0 * math.pi / length)
    taper = 0.5 - 0.5 * np.cos((t + 0.5) * (2.0 * math.pi / length))
    table = np.where(part[:, None] == 0, np.cos(angle), -np.sin(angle)) * taper[None, :]
    return table.astype(np.float32).astype(ml_dtypes.bfloat16)


def lag_rows(length, scale):
    bins, part = band_rows()
    shift = np.arange(NLAG) - NLAG // 2
    angle = (shift[:, None] * bins[None, :] % length) * (2.0 * math.pi / length)
    table = np.where(part[None, :] == 0, np.cos(angle), -np.sin(angle))
    table = table.astype(np.float32).astype(ml_dtypes.bfloat16)
    return (table.astype(np.float32) * scale).astype(ml_dtypes.bfloat16)


def dot(a, b, dims=((1,), (0,))):
    return lax.dot_general(a, b, (dims, ((), ())), preferred_element_type=F32)


def iota(shape, dim):
    return lax.broadcasted_iota(jnp.int32, shape, dim)


def whiten_rows(z, live):
    lanes = z.shape[-1]
    z = z.reshape(FB, 2, 8, lanes)
    re, im = z[:, 0], z[:, 1]
    energy = re * re + im * im
    mean = jnp.sum(jnp.sum(energy, axis=0), axis=0, keepdims=True) * (1.0 / NF)
    factor = lax.rsqrt(energy + WATER_LEVEL * mean[None] + TINY_ENERGY) * live[None]
    out = jnp.concatenate([(re * factor)[:, None], (im * factor)[:, None]], axis=1)
    return out.reshape(FB, 16, lanes).astype(BF16)


def spectra_kernel(blocks_ref, traces_ref, table_ref, mask_ref, *rest):
    thirds, (keep0, keep1, send0, send1) = rest[:3], rest[3:]
    chunk, channels = traces_ref.shape[0], traces_ref.shape[1]
    step = pl.program_id(0)
    live = mask_ref[...].astype(F32)[None]
    for n in range(chunk):
        z = dot(table_ref[...], traces_ref[n], ((1,), (1,)))
        w = whiten_rows(z, live)
        start = pl.multiple_of((step * chunk + n) * 16, 16)
        for third, ref in enumerate(thirds):
            ref[:, pl.ds(start, 16), :] = w[:, :, third * 128 : (third + 1) * 128]

    @pl.when(step == pl.num_programs(0) - 1)
    def _():
        chan = lax.axis_index("chan")
        core = chan & 1
        per_device = channels // VSB
        col = iota((1, 256), 1)
        col_block = (col >> 7) * NSRC + ((col & 31) >> 3)
        want = jnp.full((1, 256), -1, jnp.int32)
        for b in range(STEPS * NSRC):
            block = blocks_ref[b // NSRC, b % NSRC]
            holder = block // per_device
            first = jnp.where(holder == chan, (block - holder * per_device) * VSB, -1000)
            want = jnp.where(col_block == b, first + (col & 7), want)
        row = iota((channels, 256), 0)
        select = [
            (row == jnp.where(((col >> 5) & 3) == hi, want, -1)).astype(F32).astype(BF16)
            for hi in range(4)
        ]
        select = jnp.concatenate(select, axis=0)
        for half, pair in ((core, (keep0, keep1)), (1 - core, (send0, send1))):
            for t in range(2):
                low = half * 2 + t
                left = jnp.concatenate(
                    [ref[hi * 4 + low] for hi in range(4) for ref in thirds], axis=1
                )
                out = dot(left, select).astype(BF16)
                pair[0][t * 256 : (t + 1) * 256, :] = out[:, :128]
                pair[1][t * 256 : (t + 1) * 256, :] = out[:, 128:]


def spectra(traces, mask, blocks, table):
    count, channels, length = traces.shape
    chunk = math.gcd(count, 4)
    smem = pl.BlockSpec(memory_space=pltpu.SMEM)
    third = jax.ShapeDtypeStruct((FB, count * 16, channels // 3), BF16)
    shape = jax.ShapeDtypeStruct((512, 128), BF16)
    return pl.pallas_call(
        spectra_kernel,
        grid=(count // chunk,),
        out_shape=[third] * 3 + [shape] * 4,
        in_specs=[
            smem,
            pl.BlockSpec((chunk, channels, length), lambda n: (n, 0, 0)),
            pl.BlockSpec((2 * NF, length), lambda n: (0, 0)),
            pl.BlockSpec((channels,), lambda n: (0,)),
        ],
        out_specs=[pl.BlockSpec(third.shape, lambda n: (0, 0, 0))] * 3
        + [pl.BlockSpec((512, 128), lambda n: (0, 0))] * 4,
        compiler_params=pltpu.CompilerParams(vmem_limit_bytes=60 * MB),
        cost_estimate=pl.CostEstimate(flops=10**9, bytes_accessed=10**7, transcendentals=0),
        name="spectra",
    )(blocks, traces, table, mask)


def swap_parts(x):
    y = x.astype(F32).reshape(16, 2, 8, x.shape[-1])
    y = jnp.concatenate([-y[:, 1:2], y[:, 0:1]], axis=1)
    return y.reshape(256, x.shape[-1]).astype(BF16)


def pick_kernel(pick):
    win = lax.axis_index("win")
    my_y, my_x = win >> 2, win & 3
    for g, (ey, ex) in enumerate(PLACES):
        row, col = iota((64, 256), 0), iota((64, 256), 1)
        source = ((((my_y ^ ey) * 4) + (my_x ^ ex)) << 2) + (row >> 4)
        key = (((row >> 3) & 1) << 7) + source
        for hi in range(4):
            pick[hi, g * 64 : (g + 1) * 64, :] = (col == key + hi * 32).astype(F32).astype(BF16)


def pick_rows():
    return pl.pallas_call(
        pick_kernel,
        out_shape=jax.ShapeDtypeStruct((4, 64 * len(PLACES), 256), BF16),
        out_specs=pl.BlockSpec(memory_space=pltpu.VMEM),
        cost_estimate=pl.CostEstimate(flops=10**6, bytes_accessed=10**6, transcendentals=0),
        name="pick_rows",
    )()


def correlate_kernel(thirds, steps, parts, *rest):
    nt = len(thirds)
    rest = list(rest)
    ins = [rest.pop(0) for _ in range(4 + 4 * nt)]
    outs = [rest.pop(0) for _ in parts]
    results = [rest.pop(0) for _ in parts]
    pick, lag_ref, senders, held, both, stacked, sems, out_sems = rest
    core = lax.axis_index("chan") & 1
    targets = [pick, lag_ref] + [senders.at[i] for i in range(2 + 2 * nt)]
    early = [
        pltpu.make_async_copy(src, dst, sems.at[i])
        for i, (src, dst) in enumerate(zip(ins, targets))
    ]
    sources = ins[len(early) :]
    late = [
        [
            pltpu.make_async_copy(
                ref.at[pl.ds(hi * 4, 4)],
                held.at[i, pl.ds(hi * 4, 4)],
                sems.at[len(early) + hi * 2 * nt + i],
            )
            for i, ref in enumerate(sources)
        ]
        for hi in range(4)
    ]
    for copy in early[2:] + early[:2]:
        copy.start()
    for some in late:
        for copy in some:
            copy.start()
    diagonal = ((iota((16, 256), 0) & 7) == (iota((16, 256), 1) & 7)).astype(F32).astype(BF16)
    rows_of = sorted({place for t in thirds for place in KEPT[t]})

    def spread(rows, right):
        left = dot(rows, right, ((1,), (1,))).astype(BF16)
        return (left.reshape(-1, 16, 256) * diagonal[None]).reshape(left.shape)

    def some(x, order, third):
        at = [order.index(place) * 64 for place in KEPT[third]]
        return jnp.concatenate([x[i : i + 64] for i in at], axis=0)

    for who in range(1 + nt):
        for half in range(2):
            early[2 + who * 2 + half].wait()
            for s in range(steps):
                for t in range(2):
                    at = s * 512 + t * 256
                    x = senders[who * 2 + half, at : at + 256, :]
                    both[s, who, half * 2 + t] = jnp.concatenate([x, swap_parts(x)], axis=1)
    early[0].wait()
    for hi in range(4):
        for copy in late[hi]:
            copy.wait()
        rows = pick[hi]
        mine = jnp.concatenate(
            [rows[PLACES.index(p) * 64 : PLACES.index(p) * 64 + 64] for p in rows_of], axis=0
        )
        for lo in range(4):
            block = hi * 4 + (((lo >> 1) ^ core) << 1) + (lo & 1)
            own = [spread(mine, both[s, 0, lo]) for s in range(steps)]
            for i, third in enumerate(thirds):
                left = []
                for s in range(steps):
                    other = spread(some(rows, PLACES, third), both[s, 1 + i, lo])
                    left.append(jnp.concatenate([some(own[s], rows_of, third), other], axis=1))
                left = jnp.concatenate(left, axis=0)
                right = jnp.concatenate([held[i, block], held[nt + i, block]], axis=0)
                out = dot(left, right).astype(BF16).reshape(steps, 16, 16, 128)
                for s in range(steps):
                    stacked[s, i, :, block] = out[s]
    early[1].wait()
    lag = lag_ref[...]
    writes = []
    for p, (part, result, out) in enumerate(zip(parts, results, outs)):
        for s in range(steps):
            place = s * (out.shape[0] // steps)
            for third, where, first, amount in part:
                i, at = thirds.index(third), KEPT[third].index(where) * 4 + first
                for r in range(0, amount, 2):
                    x = [stacked[s, i, at + r + k].reshape(256, 128) for k in range(2)]
                    y = dot(lag, jnp.concatenate(x, axis=1)).astype(BF16)
                    result[place + r], result[place + r + 1] = y[:, :128], y[:, 128:]
                place += amount
        write = pltpu.make_async_copy(result, out, out_sems.at[p])
        write.start()
        writes.append(write)
    for write in writes:
        write.wait()


def correlate(thirds, parts, pick, lags, senders, receivers, partners, limit=60):
    steps, nt = senders[0].shape[0] // 512, len(thirds)
    hbm = pl.BlockSpec(memory_space=pl.ANY)
    sizes = [sum(piece[3] for piece in part) * steps for part in parts]
    ins = [pick, lags, *senders, *receivers, *partners]
    return pl.pallas_call(
        functools.partial(correlate_kernel, thirds, steps, parts),
        out_shape=[jax.ShapeDtypeStruct((n, NLAG, 128), BF16) for n in sizes],
        in_specs=[hbm] * len(ins),
        out_specs=[hbm] * len(sizes),
        scratch_shapes=[pltpu.VMEM((n, NLAG, 128), BF16) for n in sizes]
        + [
            pltpu.VMEM(pick.shape, BF16),
            pltpu.VMEM(lags.shape, BF16),
            pltpu.VMEM((2 + 2 * nt,) + senders[0].shape, BF16),
            pltpu.VMEM((2 * nt, FB, 256, 128), BF16),
            pltpu.VMEM((steps, 1 + nt, 4, 256, 256), BF16),
            pltpu.VMEM((steps, nt, 16, FB, 16, 128), BF16),
            pltpu.SemaphoreType.DMA((4 + 2 * nt + 8 * nt,)),
            pltpu.SemaphoreType.DMA((len(sizes),)),
        ],
        compiler_params=pltpu.CompilerParams(vmem_limit_bytes=limit * MB),
        cost_estimate=pl.CostEstimate(flops=10**6, bytes_accessed=10**6, transcendentals=0),
        name="correlate",
    )(*ins)


def finish_kernel(*refs):
    ins, out = refs[:-1], refs[-1]
    half = pl.program_id(0)

    def total(*xs):
        first = xs[0].astype(F32)
        for x in xs[1:]:
            first = first + x.astype(F32)
        return first.T

    for s in range(STEPS):
        rows = [ref.shape[0] // STEPS for ref in ins]
        g0, k1, k2, y1, xa1, xb1, y2, xa2, xb2 = [
            ref.at[pl.ds(s * n, n)] for ref, n in zip(ins, rows)
        ]

        def put(r, third, value, s=s):
            out[r, s, third * 128 : (third + 1) * 128, :] = value

        @pl.when(half == 0)
        def _():
            for r in range(2):
                put(r, 0, total(g0[r], xa2[r], xb2[r]))
                put(r, 1, total(k1[r], y1[r], xb2[4 + r]))
                put(r, 2, total(k2[r], y1[4 + r], xa2[4 + r]))

        @pl.when(half == 1)
        def _():
            for r in range(2):
                put(r, 0, total(g0[2 + r], xa2[2 + r], xb2[2 + r]))
                put(r, 1, total(k1[2 + r], xb1[r], y2[r]))
                put(r, 2, total(k2[2 + r], xa1[r], y2[2 + r]))


def finish(ins, channels):
    def whole(x):
        return pl.BlockSpec(x.shape, lambda h: (0, 0, 0))

    return pl.pallas_call(
        finish_kernel,
        grid=(2,),
        out_shape=jax.ShapeDtypeStruct((4, STEPS, channels, NLAG), F32),
        in_specs=[whole(x) for x in ins],
        out_specs=pl.BlockSpec((2, STEPS, channels, NLAG), lambda h: (h, 0, 0, 0)),
        compiler_params=pltpu.CompilerParams(vmem_limit_bytes=60 * MB),
        name="finish",
    )(*ins)


def merge_kernel(*refs):
    rows = [ref.shape[0] // STEPS for ref in refs]

    def add(x, y):
        return (x.astype(F32) + y.astype(F32)).astype(BF16)

    for s in range(STEPS):
        g1, g3, k13, k10, k21, k20, y, xa, xb, ua, ub, y2, xa2, xb2 = [
            ref.at[pl.ds(s * n, n)] for ref, n in zip(refs, rows)
        ]
        for r in range(2):
            y2[r] = add(k10[r], xb[2 + r])
            y2[2 + r] = add(k20[r], xa[2 + r])
            xa2[r] = g1[r]
            xa2[2 + r] = add(g1[2 + r], ub[r])
            xa2[4 + r] = add(k21[r], y[6 + r])
            xb2[r] = add(g3[r], ua[r])
            xb2[2 + r] = g3[2 + r]
            xb2[4 + r] = add(k13[r], y[2 + r])


def merge(ins, sizes):
    vmem = pl.BlockSpec(memory_space=pltpu.VMEM)
    return pl.pallas_call(
        merge_kernel,
        out_shape=[jax.ShapeDtypeStruct((n,) + ins[0].shape[1:], BF16) for n in sizes],
        in_specs=[vmem] * len(ins),
        out_specs=[vmem] * len(sizes),
        compiler_params=pltpu.CompilerParams(vmem_limit_bytes=60 * MB),
        name="merge",
    )(*ins)


def on_device(traces, channel_mask, source_blocks):
    windows, segments, channels, length = traces.shape
    traces = traces.reshape(windows * segments, channels, length)
    table = jnp.asarray(dft_rows(length))
    scale = 1.0 / (windows * lax.axis_size("win") * segments)
    lags = jnp.asarray(lag_rows(length, scale))

    def chan_swap(x, bits):
        return lax.ppermute(x, "chan", [(i, i ^ bits) for i in range(16)])

    def win_swap(x, pair):
        bits = pair[0] * 4 + pair[1]
        return lax.ppermute(x, "win", [(i, i ^ bits) for i in range(8)])

    r0, r1, r2, keep0, keep1, send0, send1 = spectra(traces, channel_mask, source_blocks, table)
    p1, p2 = win_swap(r1, PAIRS[1]), win_swap(r2, PAIRS[2])
    part0, part1 = keep0 + chan_swap(send0, 1), keep1 + chan_swap(send1, 1)
    part0, part1 = part0 + chan_swap(part0, 8), part1 + chan_swap(part1, 8)
    pick = pick_rows()
    part0, part1, r0, pick = lax.optimization_barrier((part0, part1, r0, pick))
    p0 = win_swap(r0, PAIRS[0])

    for one, other in ((2, 6), (6, 2)):
        part0, part1 = part0 + chan_swap(part0, one), part1 + chan_swap(part1, other)
    part0, part1, p1, p2 = lax.optimization_barrier((part0, part1, p1, p2))
    part = jnp.concatenate([part0, part1])
    own, *found = [part] + [win_swap(part, pair) for pair in (PAIRS[1], PAIRS[2], PAIRS[0])]
    own = (own, chan_swap(own, 1))
    from_a, from_b = [(half, chan_swap(half, 1)) for half in found[:2]]
    y1, xa1, xb1, k1, k13, k10, k2, k21, k20 = correlate(
        (1, 2), PARTS_12, pick, lags, own + from_a + from_b, (r1, r2), (p1, p2)
    )
    own, from_y, p0, y1, xa1, xb1 = lax.optimization_barrier((own, found[2], p0, y1, xa1, xb1))
    from_y = (from_y, chan_swap(from_y, 1))
    y1, xa1, xb1 = win_swap(y1, (1, 0)), win_swap(xa1, (0, 1)), win_swap(xb1, (0, 3))
    ua, ub, g0, g1, g3 = correlate((0,), PARTS_0, pick, lags, own + from_y, (r0,), (p0,))
    ua, ub = win_swap(ua, (0, 1)), win_swap(ub, (0, 3))
    y2, xa2, xb2 = merge([g1, g3, k13, k10, k21, k20, y1, xa1, xb1, ua, ub], [8, 12, 12])
    y2, xa2, xb2 = win_swap(y2, (1, 0)), win_swap(xa2, (0, 1)), win_swap(xb2, (0, 3))
    return finish([g0, k1, k2, y1, xa1, xb1, y2, xa2, xb2], channels)


def solution(mesh):
    in_specs = (P("win", None, "chan", None), P("chan"), P())
    out_specs = P("win", None, "chan", None)
    return jax.shard_map(
        on_device, mesh=mesh, in_specs=in_specs, out_specs=out_specs, check_vma=False
    )
```

time: 415 us -> 106 us (0.26)
  waiting for transfers between devices: 222 us -> 37.8 us
  local copies, waits for them, and re-layouts: 79.6 us -> 3.64 us
  matrix products: 54.1 us -> 0 us
  Pallas kernels: 0 us -> 37.7 us
  between operations: 29.3 us -> 0.23 us
  other arithmetic: 27.3 us -> 2.12 us
  starting transfers between devices: 0.49 us -> 24.7 us
    psum x1 -> x0, waiting for transfers between devices: 139 us -> none  [spread(): return lax.psum(jnp.where(mine, array, jnp.zeros_like(array)), axis)]
    reduce_scatter x2 -> x0, waiting for transfers between devices: 82.7 us -> none  [on_device(): lax.psum_scatter(corr_term(jnp.int32(0), lax.axis_size('win') * row_count...]
    dot_general x11 -> x0, matrix products: 54.1 us -> none  [the longest x8 34.1 us: correlate_bins(): jnp.einsum('nif,njf->ifj', left, right, preferred_element_type=jnp.float32)]
    dot_general x8 -> x0, local copies, waits for them, and re-layouts: 53.3 us -> none  [correlate_bins(): jnp.einsum('nif,njf->ifj', left, right, preferred_element_type=jnp.float32)]
    ppermute x0 -> x26, waiting for transfers between devices: none -> 37.8 us  [the longest x14 19 us: win_swap(): return lax.ppermute(x, 'win', [(i, i ^ bits) for i in range(8)])]
    pallas_call x0 -> x6, Pallas kernels: none -> 37.7 us  [the longest x2 22.2 us: correlate(): pl.pallas_call(functools.partial(correlate_kernel, thirds, steps, parts),...]
    ppermute x0 -> x26, starting transfers between devices: none -> 24.7 us  [the longest x14 16.1 us: win_swap(): return lax.ppermute(x, 'win', [(i, i ^ bits) for i in range(8)])]
    slice x9 -> x0, local copies, waits for them, and re-layouts: 9.87 us -> none  [the longest x6 4.87 us: cross_spectra(): send_real, send_imag = (senders[..., :bin_count], senders[..., bin_count:])]
  transfers between devices with their start and end apart: 3 -> 26, of which waited for: 3 -> 16; matrix products, arithmetic and copies ran while one was open for 16% -> 2% of each run, Pallas kernels for 0% -> 22%
where the time goes in v3:
time: 106 us
  waiting for transfers between devices  37.8 us (36%)
  Pallas kernels  37.7 us (36%)
  starting transfers between devices  24.7 us (23%)
  local copies, waits for them, and re-layouts  3.64 us (3%)
  other arithmetic  2.12 us (2%)
    pallas_call x2, Pallas kernels, correlate(): pl.pallas_call(functools.partial(correlate_kernel, thirds, steps, parts),...  22.2 us
    ppermute x14, waiting for transfers between devices, win_swap(): return lax.ppermute(x, 'win', [(i, i ^ bits) for i in range(8)])  19 us
    ppermute x12, waiting for transfers between devices, chan_swap(): return lax.ppermute(x, 'chan', [(i, i ^ bits) for i in range(16)])  18.7 us
    ppermute x14, starting transfers between devices, win_swap(): return lax.ppermute(x, 'win', [(i, i ^ bits) for i in range(8)])  16.1 us
    ppermute x12, starting transfers between devices, chan_swap(): return lax.ppermute(x, 'chan', [(i, i ^ bits) for i in range(16)])  8.62 us
    pallas_call x1, Pallas kernels, spectra(): pl.pallas_call(spectra_kernel, grid=(count // chunk,), out_shape=[third]...  8.25 us
    unnamed x37, local copies, waits for them, and re-layouts  3.62 us
    pallas_call x1, Pallas kernels, finish(): pl.pallas_call(finish_kernel, grid=(2,), out_shape=jax.ShapeDtypeStruct((...  3.36 us
  transfers between devices with their start and end apart: 26, of which 16 were waited for; matrix products, arithmetic and copies ran while one was open for 2% of the time, Pallas kernels for 22%

profile of v3, /device:TPU:0, one launch (start us, length us, event | category | flops | bytes accessed | tf_op | source)
XLA Modules:
  0.0 106.2 jit_solution(1807841680247126163)
XLA Ops:
  0.0 8.3 %spectra.1 = (bf16[16,256,128]{2,1,0:T(8,128)(2,1)}, bf16[16,256,128]{2,1,0:T(8,128)(2,1)}, bf16[16,256,128]{2,1,0:T(8,128)(2,1)}, bf16[512,128]{1,0:T(8,128)(2,...) custom-call(s32[2,4]{1,0:T(2,128)} %blocks_ref.1, ...), custom_call_target="tpu_custom_call" | custom-call | flops 1000000000 | bytes 10000000 | tf_op jit(solution)/shard_map/spectra/pallas_call | solution.py:140
  8.3 1.6 %collective-permute-start.8 = (bf16[16,256,128]{2,1,0:T(8,128)(2,1)}, bf16[16,256,128]{2,1,0:T(8,128)(2,1)S(1)}, u32[]{:S(2)}, u32[]{:S(2)}) collective-permute-start(bf16[16,256,128]{2,1,0:T(8,128)(2,1)} %get-tuple-element.52.rest_8_), channel_id=1, source_target_pairs={{0,1},{1,0},{2,3},{3,2},{4,5},{5,4},{6,7},{7,6},{8,9},{9,8},{10,11... | collective-permute-start | bytes 3145736 | tf_op jit(solution)/shard_map/ppermute | solution.py:396
  9.9 2.1 %collective-permute-start.9 = (bf16[16,256,128]{2,1,0:T(8,128)(2,1)}, bf16[16,256,128]{2,1,0:T(8,128)(2,1)S(1)}, u32[]{:S(2)}, u32[]{:S(2)}) collective-permute-start(bf16[16,256,128]{2,1,0:T(8,128)(2,1)} %get-tuple-element.53.rest_9_), channel_id=1, source_target_pairs={{0,3},{1,2},{2,1},{3,0},{4,7},{5,6},{6,5},{7,4},{8,11},{9,10},{10,... | collective-permute-start | bytes 3145736 | tf_op jit(solution)/shard_map/ppermute | solution.py:396
  14.5 3.3 %collective-permute-start.3 = (bf16[512,128]{1,0:T(8,128)(2,1)S(1)}, bf16[512,128]{1,0:T(8,128)(2,1)S(1)}, u32[]{:S(2)}, u32[]{:S(2)}) collective-permute-start(bf16[512,128]{1,0:T(8,128)(2,1)S(1)} %add.26), channel_id=1, source_target_pairs={{0,64},{8,72},{16,80},{24,88},{32,96},{40,104},{48,112},{56,120},{... | collective-permute-start | bytes 393224 | tf_op jit(solution)/shard_map/ppermute | solution.py:392
  20.3 1.3 %collective-permute-done.3 = bf16[512,128]{1,0:T(8,128)(2,1)S(1)} collective-permute-done((bf16[512,128]{1,0:T(8,128)(2,1)S(1)}, bf16[512,128]{1,0:T(8,128)(2,1)S(1)}, u32[]{:S(2)}, u32[]{:S(2)}) %collective-permute-start.3) | collective-permute-done | bytes 131104 | tf_op jit(solution)/shard_map/ppermute | solution.py:392
  21.6 3.9 %collective-permute-done.1 = bf16[512,128]{1,0:T(8,128)(2,1)S(1)} collective-permute-done((bf16[512,128]{1,0:T(8,128)(2,1)S(1)}, bf16[512,128]{1,0:T(8,128)(2,1)S(1)}, u32[]{:S(2)}, u32[]{:S(2)}) %collective-permute-start.1) | collective-permute-done | bytes 131104 | tf_op jit(solution)/shard_map/ppermute | solution.py:392
  26.3 4.0 %collective-permute-start.6 = (bf16[512,128]{1,0:T(8,128)(2,1)S(1)}, bf16[512,128]{1,0:T(8,128)(2,1)S(1)}, u32[]{:S(2)}, u32[]{:S(2)}) collective-permute-start(bf16[512,128]{1,0:T(8,128)(2,1)S(1)} %add.27), channel_id=1, source_target_pairs={{0,48},{8,56},{16,32},{24,40},{32,16},{40,24},{48,0},{56,8},{64,11... | collective-permute-start | bytes 393224 | tf_op jit(solution)/shard_map/ppermute | solution.py:392
  30.4 2.9 %collective-permute-done.6 = bf16[512,128]{1,0:T(8,128)(2,1)S(1)} collective-permute-done((bf16[512,128]{1,0:T(8,128)(2,1)S(1)}, bf16[512,128]{1,0:T(8,128)(2,1)S(1)}, u32[]{:S(2)}, u32[]{:S(2)}) %collective-permute-start.6) | collective-permute-done | bytes 131104 | tf_op jit(solution)/shard_map/ppermute | solution.py:392
  33.5 3.0 %collective-permute-done.4 = bf16[512,128]{1,0:T(8,128)(2,1)S(1)} collective-permute-done((bf16[512,128]{1,0:T(8,128)(2,1)S(1)}, bf16[512,128]{1,0:T(8,128)(2,1)S(1)}, u32[]{:S(2)}, u32[]{:S(2)}) %collective-permute-start.4) | collective-permute-done | bytes 131104 | tf_op jit(solution)/shard_map/ppermute | solution.py:392
  36.8 1.6 %collective-permute-done.7 = bf16[512,128]{1,0:T(8,128)(2,1)S(1)} collective-permute-done((bf16[512,128]{1,0:T(8,128)(2,1)S(1)}, bf16[512,128]{1,0:T(8,128)(2,1)S(1)}, u32[]{:S(2)}, u32[]{:S(2)}) %collective-permute-start.7) | collective-permute-done | bytes 131104 | tf_op jit(solution)/shard_map/ppermute | solution.py:392
  38.5 4.3 %collective-permute-done.5 = bf16[512,128]{1,0:T(8,128)(2,1)S(1)} collective-permute-done((bf16[512,128]{1,0:T(8,128)(2,1)S(1)}, bf16[512,128]{1,0:T(8,128)(2,1)S(1)}, u32[]{:S(2)}, u32[]{:S(2)}) %collective-permute-start.5) | collective-permute-done | bytes 131104 | tf_op jit(solution)/shard_map/ppermute | solution.py:392
  44.4 5.0 %collective-permute-done.13.rest_4_ = bf16[1024,128]{1,0:T(8,128)(2,1)S(1)} collective-permute-done((bf16[1024,128]{1,0:T(8,128)(2,1)S(1)}, bf16[1024,128]{1,0:T(8,128)(2,1)S(1)}, u32[]{:S(2)}, u32[]{:S(2)}) %collective-permute-start.13) | collective-permute-done | bytes 262176 | tf_op jit(solution)/shard_map/ppermute | solution.py:396
  49.4 2.0 %collective-permute-done.15.rest_6_ = bf16[1024,128]{1,0:T(8,128)(2,1)S(1)} collective-permute-done((bf16[1024,128]{1,0:T(8,128)(2,1)S(1)}, bf16[1024,128]{1,0:T(8,128)(2,1)S(1)}, u32[]{:S(2)}, u32[]{:S(2)}) %collective-permute-start.15) | collective-permute-done | bytes 262176 | tf_op jit(solution)/shard_map/ppermute | solution.py:396
  51.4 1.3 %collective-permute-start.11 = (bf16[1024,128]{1,0:T(8,128)(2,1)S(1)}, bf16[1024,128]{1,0:T(8,128)(2,1)S(1)}, u32[]{:S(2)}, u32[]{:S(2)}) collective-permute-start(bf16[1024,128]{1,0:T(8,128)(2,1)S(1)} %constant_dynamic-update-slice_fusion.rest_2_), channel_id=1, source_target_pairs={{0,4},{1,5},{2,6},{3,7},{4,0},{5,1},{6,2},{7,3},{8,12},{9,13},{10,... | collective-permute-start | bytes 786440 | tf_op jit(solution)/shard_map/ppermute | solution.py:396
  54.2 13.5 %correlate.2 = (bf16[16,128,128]{2,1,0:T(8,128)(2,1)}, bf16[8,128,128]{2,1,0:T(8,128)(2,1)}, bf16[8,128,128]{2,1,0:T(8,128)(2,1)}, bf16[8,128,128]{2,1,0:T(8,128...) custom-call(bf16[4,448,256]{2,1,0:T(8,128)(2,1)} %pick_rows.1.rest_0, ...), custom_call_target="tpu_custom_call" | custom-call | flops 1000000 | bytes 1000000 | tf_op jit(solution)/shard_map/correlate/pallas_call | solution.py:280
  70.9 8.7 %correlate.3 = (bf16[4,128,128]{2,1,0:T(8,128)(2,1)}, bf16[4,128,128]{2,1,0:T(8,128)(2,1)}, bf16[8,128,128]{2,1,0:T(8,128)(2,1)}, bf16[8,128,128]{2,1,0:T(8,128)(2,1)}, bf16[8,128,128]{2,1,0:T(8,128)(2,1)}) custom-call(bf16[4,448,256]{2,1,0:T(8,128)(2,1)} %pick_rows.1.rest_0_, bf16[128,256]{1,0:T(8,128)(2,1)} %constant.5.clone.rest_1_, ...), custom_call_target="tpu_custom_call" | custom-call | flops 1000000 | bytes 1000000 | tf_op jit(solution)/shard_map/correlate/pallas_call | solution.py:280
  80.2 2.6 %collective-permute-start.22 = (bf16[4,128,128]{2,1,0:T(8,128)(2,1)}, bf16[4,128,128]{2,1,0:T(8,128)(2,1)S(1)}, u32[]{:S(2)}, u32[]{:S(2)}) collective-permute-start(bf16[4,128,128]{2,1,0:T(8,128)(2,1)} %get-tuple-element.79), channel_id=1, source_target_pairs={{0,3},{1,2},{2,1},{3,0},{4,7},{5,6},{6,5},{7,4},{8,11},{9,10},{10,... | collective-permute-start | bytes 393224 | tf_op jit(solution)/shard_map/ppermute | solution.py:396
  82.9 2.6 %collective-permute-done.21.refs_9_ = bf16[4,128,128]{2,1,0:T(8,128)(2,1)S(1)} collective-permute-done((bf16[4,128,128]{2,1,0:T(8,128)(2,1)}, bf16[4,128,128]{2,1,0:T(8,128)(2,1)S(1)}, u32[]{:S(2)}, u32[]{:S(2)}) %collective-permute-start.21) | collective-permute-done | bytes 131104 | tf_op jit(solution)/shard_map/ppermute | solution.py:396
  85.5 1.5 %collective-permute-done.22.refs_10_ = bf16[4,128,128]{2,1,0:T(8,128)(2,1)S(1)} collective-permute-done((bf16[4,128,128]{2,1,0:T(8,128)(2,1)}, bf16[4,128,128]{2,1,0:T(8,128)(2,1)S(1)}, u32[]{:S(2)}, u32[]{:S(2)}) %collective-permute-start.22) | collective-permute-done | bytes 131104 | tf_op jit(solution)/shard_map/ppermute | solution.py:396
  87.8 2.7 %merge.1 = (bf16[8,128,128]{2,1,0:T(8,128)(2,1)}, bf16[12,128,128]{2,1,0:T(8,128)(2,1)}, bf16[12,128,128]{2,1,0:T(8,128)(2,1)}) custom-call(bf16[8,128,128]{2,1,0:T(8,128)(2,1)} %get-tuple-element.72.refs_0_, bf16[8,128,128]{2,1,0:T(8,128)(2,1)} %get-tuple-element.73.refs_1_, bf16[4,128,128]{2,1,0:T(8,128)(2,1)} %get-tuple-element.74.refs_2_, ...), custom_call_target="tpu_custom_call" | custom-call | tf_op jit(solution)/shard_map/merge/pallas_call | solution.py:374
  90.7 2.1 %collective-permute-start.25 = (bf16[12,128,128]{2,1,0:T(8,128)(2,1)}, bf16[12,128,128]{2,1,0:T(8,128)(2,1)S(1)}, u32[]{:S(2)}, u32[]{:S(2)}) collective-permute-start(bf16[12,128,128]{2,1,0:T(8,128)(2,1)} %get-tuple-element.82), channel_id=1, source_target_pairs={{0,3},{1,2},{2,1},{3,0},{4,7},{5,6},{6,5},{7,4},{8,11},{9,10},{10,... | collective-permute-start | bytes 1179656 | tf_op jit(solution)/shard_map/ppermute | solution.py:396
  92.9 1.3 %collective-permute-start.23 = (bf16[8,128,128]{2,1,0:T(8,128)(2,1)}, bf16[8,128,128]{2,1,0:T(8,128)(2,1)S(1)}, u32[]{:S(2)}, u32[]{:S(2)}) collective-permute-start(bf16[8,128,128]{2,1,0:T(8,128)(2,1)} %get-tuple-element.80), channel_id=1, source_target_pairs={{0,4},{1,5},{2,6},{3,7},{4,0},{5,1},{6,2},{7,3},{8,12},{9,13},{10,... | collective-permute-start | bytes 786440 | tf_op jit(solution)/shard_map/ppermute | solution.py:396
  94.1 5.7 %collective-permute-done.23.refs_6_ = bf16[8,128,128]{2,1,0:T(8,128)(2,1)S(1)} collective-permute-done((bf16[8,128,128]{2,1,0:T(8,128)(2,1)}, bf16[8,128,128]{2,1,0:T(8,128)(2,1)S(1)}, u32[]{:S(2)}, u32[]{:S(2)}) %collective-permute-start.23) | collective-permute-done | bytes 262176 | tf_op jit(solution)/shard_map/ppermute | solution.py:396
  102.8 3.4 %finish.1 = f32[4,2,384,128]{3,2,1,0:T(8,128)} custom-call(bf16[8,128,128]{2,1,0:T(8,128)(2,1)} %get-tuple-element.66.refs_0_, bf16[8,128,128]{2,1,0:T(8,128)(2,1)} %get-tuple-element.67.refs_1_, bf16[8,128,128]{2,1,0:T(8,128)(2,1)} %get-tuple-element.68.refs_2_, bf16[16,128,128]{2,1,0:T(8,128)(2,1)} %copy-done, bf16[8,128,128]{2,1,0:T(8,128)(2,1)} %copy-done.4, ...), custom_call_target="tpu_custom_call" | custom-call | tf_op jit(solution)/shard_map/finish/pallas_call | solution.py:340
  (80 shorter events, 17.1 us)
Async XLA Ops:
  8.3 34.6 %collective-permute-start.8 = (bf16[16,256,128]{2,1,0:T(8,128)(2,1)}, bf16[16,256,128]{2,1,0:T(8,128)(2,1)S(1)}, u32[]{:S(2)}, u32[]{:S(2)}) collective-permute-start(bf16[16,256,128]{2,1,0:T(8,128)(2,1)} %get-tuple-element.52.rest_8_), channel_id=1, source_target_pairs={{0,1},{1,0},{2,3},{3,2},{4,5},{5,4},{6,7},{7,6},{8,9},{9,8},{10,11... | collective-permute-start | bytes 3145736 | tf_op jit(solution)/shard_map/ppermute | solution.py:396
  9.9 33.0 %collective-permute-start.9 = (bf16[16,256,128]{2,1,0:T(8,128)(2,1)}, bf16[16,256,128]{2,1,0:T(8,128)(2,1)S(1)}, u32[]{:S(2)}, u32[]{:S(2)}) collective-permute-start(bf16[16,256,128]{2,1,0:T(8,128)(2,1)} %get-tuple-element.53.rest_9_), channel_id=1, source_target_pairs={{0,3},{1,2},{2,1},{3,0},{4,7},{5,6},{6,5},{7,4},{8,11},{9,10},{10,... | collective-permute-start | bytes 3145736 | tf_op jit(solution)/shard_map/ppermute | solution.py:396
  12.0 1.6 %collective-permute-start.2 = (bf16[512,128]{1,0:T(8,128)(2,1)}, bf16[512,128]{1,0:T(8,128)(2,1)S(1)}, u32[]{:S(2)}, u32[]{:S(2)}) collective-permute-start(bf16[512,128]{1,0:T(8,128)(2,1)} %get-tuple-element.47), channel_id=1, source_target_pairs={{0,8},{8,0},{16,24},{24,16},{32,40},{40,32},{48,56},{56,48},{64,72... | collective-permute-start | bytes 393224 | tf_op jit(solution)/shard_map/ppermute | solution.py:392
  12.0 5.8 %collective-permute-start = (bf16[512,128]{1,0:T(8,128)(2,1)}, bf16[512,128]{1,0:T(8,128)(2,1)S(1)}, u32[]{:S(2)}, u32[]{:S(2)}) collective-permute-start(bf16[512,128]{1,0:T(8,128)(2,1)} %get-tuple-element.45), channel_id=1, source_target_pairs={{0,8},{8,0},{16,24},{24,16},{32,40},{40,32},{48,56},{56,48},{64,72... | collective-permute-start | bytes 393224 | tf_op jit(solution)/shard_map/ppermute | solution.py:392
  14.5 7.1 %collective-permute-start.3 = (bf16[512,128]{1,0:T(8,128)(2,1)S(1)}, bf16[512,128]{1,0:T(8,128)(2,1)S(1)}, u32[]{:S(2)}, u32[]{:S(2)}) collective-permute-start(bf16[512,128]{1,0:T(8,128)(2,1)S(1)} %add.26), channel_id=1, source_target_pairs={{0,64},{8,72},{16,80},{24,88},{32,96},{40,104},{48,112},{56,120},{... | collective-permute-start | bytes 393224 | tf_op jit(solution)/shard_map/ppermute | solution.py:392
  18.7 6.9 %collective-permute-start.1 = (bf16[512,128]{1,0:T(8,128)(2,1)S(1)}, bf16[512,128]{1,0:T(8,128)(2,1)S(1)}, u32[]{:S(2)}, u32[]{:S(2)}) collective-permute-start(bf16[512,128]{1,0:T(8,128)(2,1)S(1)} %add.24), channel_id=1, source_target_pairs={{0,64},{8,72},{16,80},{24,88},{32,96},{40,104},{48,112},{56,120},{... | collective-permute-start | bytes 393224 | tf_op jit(solution)/shard_map/ppermute | solution.py:392
  25.6 42.2 %collective-permute-start.12 = (bf16[16,256,128]{2,1,0:T(8,128)(2,1)}, bf16[16,256,128]{2,1,0:T(8,128)(2,1)}, u32[]{:S(2)}, u32[]{:S(2)}) collective-permute-start(bf16[16,256,128]{2,1,0:T(8,128)(2,1)} %get-tuple-element.56.rest_6_), channel_id=1, source_target_pairs={{0,4},{1,5},{2,6},{3,7},{4,0},{5,1},{6,2},{7,3},{8,12},{9,13},{10,... | collective-permute-start | bytes 3145736 | tf_op jit(solution)/shard_map/ppermute | solution.py:396
  26.3 7.0 %collective-permute-start.6 = (bf16[512,128]{1,0:T(8,128)(2,1)S(1)}, bf16[512,128]{1,0:T(8,128)(2,1)S(1)}, u32[]{:S(2)}, u32[]{:S(2)}) collective-permute-start(bf16[512,128]{1,0:T(8,128)(2,1)S(1)} %add.27), channel_id=1, source_target_pairs={{0,48},{8,56},{16,32},{24,40},{32,16},{40,24},{48,0},{56,8},{64,11... | collective-permute-start | bytes 393224 | tf_op jit(solution)/shard_map/ppermute | solution.py:392
  30.4 6.1 %collective-permute-start.4 = (bf16[512,128]{1,0:T(8,128)(2,1)S(1)}, bf16[512,128]{1,0:T(8,128)(2,1)S(1)}, u32[]{:S(2)}, u32[]{:S(2)}) collective-permute-start(bf16[512,128]{1,0:T(8,128)(2,1)S(1)} %add.25), channel_id=1, source_target_pairs={{0,16},{8,24},{16,0},{24,8},{32,48},{40,56},{48,32},{56,40},{64,80... | collective-permute-start | bytes 393224 | tf_op jit(solution)/shard_map/ppermute | solution.py:392
  33.4 5.0 %collective-permute-start.7 = (bf16[512,128]{1,0:T(8,128)(2,1)S(1)}, bf16[512,128]{1,0:T(8,128)(2,1)S(1)}, u32[]{:S(2)}, u32[]{:S(2)}) collective-permute-start(bf16[512,128]{1,0:T(8,128)(2,1)S(1)} %add.30), channel_id=1, source_target_pairs={{0,16},{8,24},{16,0},{24,8},{32,48},{40,56},{48,32},{56,40},{64,80... | collective-permute-start | bytes 393224 | tf_op jit(solution)/shard_map/ppermute | solution.py:392
  36.5 6.3 %collective-permute-start.5 = (bf16[512,128]{1,0:T(8,128)(2,1)S(1)}, bf16[512,128]{1,0:T(8,128)(2,1)S(1)}, u32[]{:S(2)}, u32[]{:S(2)}) collective-permute-start(bf16[512,128]{1,0:T(8,128)(2,1)S(1)} %add.28), channel_id=1, source_target_pairs={{0,48},{8,56},{16,32},{24,40},{32,16},{40,24},{48,0},{56,8},{64,11... | collective-permute-start | bytes 393224 | tf_op jit(solution)/shard_map/ppermute | solution.py:392
  42.9 6.5 %collective-permute-start.13 = (bf16[1024,128]{1,0:T(8,128)(2,1)S(1)}, bf16[1024,128]{1,0:T(8,128)(2,1)S(1)}, u32[]{:S(2)}, u32[]{:S(2)}) collective-permute-start(bf16[1024,128]{1,0:T(8,128)(2,1)S(1)} %constant_dynamic-update-slice_fusion.rest_2_), channel_id=1, source_target_pairs={{0,1},{1,0},{2,3},{3,2},{4,5},{5,4},{6,7},{7,6},{8,9},{9,8},{10,11... | collective-permute-start | bytes 786440 | tf_op jit(solution)/shard_map/ppermute | solution.py:396
  43.8 7.6 %collective-permute-start.15 = (bf16[1024,128]{1,0:T(8,128)(2,1)S(1)}, bf16[1024,128]{1,0:T(8,128)(2,1)S(1)}, u32[]{:S(2)}, u32[]{:S(2)}) collective-permute-start(bf16[1024,128]{1,0:T(8,128)(2,1)S(1)} %constant_dynamic-update-slice_fusion.rest_2_), channel_id=1, source_target_pairs={{0,3},{1,2},{2,1},{3,0},{4,7},{5,6},{6,5},{7,4},{8,11},{9,10},{10,... | collective-permute-start | bytes 786440 | tf_op jit(solution)/shard_map/ppermute | solution.py:396
  44.4 8.3 %collective-permute-start.10 = (bf16[1024,128]{1,0:T(8,128)(2,1)S(1)}, bf16[1024,128]{1,0:T(8,128)(2,1)S(1)}, u32[]{:S(2)}, u32[]{:S(2)}) collective-permute-start(bf16[1024,128]{1,0:T(8,128)(2,1)S(1)} %constant_dynamic-update-slice_fusion.rest_2_), channel_id=1, source_target_pairs={{0,8},{8,0},{16,24},{24,16},{32,40},{40,32},{48,56},{56,48},{64,72... | collective-permute-start | bytes 786440 | tf_op jit(solution)/shard_map/ppermute | solution.py:392
  49.4 3.3 %collective-permute-start.14 = (bf16[1024,128]{1,0:T(8,128)(2,1)S(1)}, bf16[1024,128]{1,0:T(8,128)(2,1)S(1)}, u32[]{:S(2)}, u32[]{:S(2)}) collective-permute-start(bf16[1024,128]{1,0:T(8,128)(2,1)S(1)} %collective-permute-done.13.rest_4_), channel_id=1, source_target_pairs={{0,8},{8,0},{16,24},{24,16},{32,40},{40,32},{48,56},{56,48},{64,72... | collective-permute-start | bytes 786440 | tf_op jit(solution)/shard_map/ppermute | solution.py:392
  51.4 16.4 %collective-permute-start.11 = (bf16[1024,128]{1,0:T(8,128)(2,1)S(1)}, bf16[1024,128]{1,0:T(8,128)(2,1)S(1)}, u32[]{:S(2)}, u32[]{:S(2)}) collective-permute-start(bf16[1024,128]{1,0:T(8,128)(2,1)S(1)} %constant_dynamic-update-slice_fusion.rest_2_), channel_id=1, source_target_pairs={{0,4},{1,5},{2,6},{3,7},{4,0},{5,1},{6,2},{7,3},{8,12},{9,13},{10,... | collective-permute-start | bytes 786440 | tf_op jit(solution)/shard_map/ppermute | solution.py:396
  67.8 19.2 %collective-permute-start.18 = (bf16[16,128,128]{2,1,0:T(8,128)(2,1)}, bf16[16,128,128]{2,1,0:T(8,128)(2,1)S(1)}, u32[]{:S(2)}, u32[]{:S(2)}) collective-permute-start(bf16[16,128,128]{2,1,0:T(8,128)(2,1)} %get-tuple-element.69), channel_id=1, source_target_pairs={{0,4},{1,5},{2,6},{3,7},{4,0},{5,1},{6,2},{7,3},{8,12},{9,13},{10,... | collective-permute-start | bytes 1572872 | tf_op jit(solution)/shard_map/ppermute | solution.py:396
  68.6 14.2 %collective-permute-start.19 = (bf16[8,128,128]{2,1,0:T(8,128)(2,1)}, bf16[8,128,128]{2,1,0:T(8,128)(2,1)S(1)}, u32[]{:S(2)}, u32[]{:S(2)}) collective-permute-start(bf16[8,128,128]{2,1,0:T(8,128)(2,1)} %get-tuple-element.70), channel_id=1, source_target_pairs={{0,1},{1,0},{2,3},{3,2},{4,5},{5,4},{6,7},{7,6},{8,9},{9,8},{10,11... | collective-permute-start | bytes 786440 | tf_op jit(solution)/shard_map/ppermute | solution.py:396
  68.7 14.2 %collective-permute-start.20 = (bf16[8,128,128]{2,1,0:T(8,128)(2,1)}, bf16[8,128,128]{2,1,0:T(8,128)(2,1)S(1)}, u32[]{:S(2)}, u32[]{:S(2)}) collective-permute-start(bf16[8,128,128]{2,1,0:T(8,128)(2,1)} %get-tuple-element.71), channel_id=1, source_target_pairs={{0,3},{1,2},{2,1},{3,0},{4,7},{5,6},{6,5},{7,4},{8,11},{9,10},{10,... | collective-permute-start | bytes 786440 | tf_op jit(solution)/shard_map/ppermute | solution.py:396
  79.6 5.8 %collective-permute-start.21 = (bf16[4,128,128]{2,1,0:T(8,128)(2,1)}, bf16[4,128,128]{2,1,0:T(8,128)(2,1)S(1)}, u32[]{:S(2)}, u32[]{:S(2)}) collective-permute-start(bf16[4,128,128]{2,1,0:T(8,128)(2,1)} %get-tuple-element.78), channel_id=1, source_target_pairs={{0,1},{1,0},{2,3},{3,2},{4,5},{5,4},{6,7},{7,6},{8,9},{9,8},{10,11... | collective-permute-start | bytes 393224 | tf_op jit(solution)/shard_map/ppermute | solution.py:396
  80.2 6.8 %collective-permute-start.22 = (bf16[4,128,128]{2,1,0:T(8,128)(2,1)}, bf16[4,128,128]{2,1,0:T(8,128)(2,1)S(1)}, u32[]{:S(2)}, u32[]{:S(2)}) collective-permute-start(bf16[4,128,128]{2,1,0:T(8,128)(2,1)} %get-tuple-element.79), channel_id=1, source_target_pairs={{0,3},{1,2},{2,1},{3,0},{4,7},{5,6},{6,5},{7,4},{8,11},{9,10},{10,... | collective-permute-start | bytes 393224 | tf_op jit(solution)/shard_map/ppermute | solution.py:396
  90.5 10.3 %collective-permute-start.24 = (bf16[12,128,128]{2,1,0:T(8,128)(2,1)}, bf16[12,128,128]{2,1,0:T(8,128)(2,1)S(1)}, u32[]{:S(2)}, u32[]{:S(2)}) collective-permute-start(bf16[12,128,128]{2,1,0:T(8,128)(2,1)} %get-tuple-element.81), channel_id=1, source_target_pairs={{0,1},{1,0},{2,3},{3,2},{4,5},{5,4},{6,7},{7,6},{8,9},{9,8},{10,11... | collective-permute-start | bytes 1179656 | tf_op jit(solution)/shard_map/ppermute | solution.py:396
  90.7 11.3 %collective-permute-start.25 = (bf16[12,128,128]{2,1,0:T(8,128)(2,1)}, bf16[12,128,128]{2,1,0:T(8,128)(2,1)S(1)}, u32[]{:S(2)}, u32[]{:S(2)}) collective-permute-start(bf16[12,128,128]{2,1,0:T(8,128)(2,1)} %get-tuple-element.82), channel_id=1, source_target_pairs={{0,3},{1,2},{2,1},{3,0},{4,7},{5,6},{6,5},{7,4},{8,11},{9,10},{10,... | collective-permute-start | bytes 1179656 | tf_op jit(solution)/shard_map/ppermute | solution.py:396
  92.9 6.9 %collective-permute-start.23 = (bf16[8,128,128]{2,1,0:T(8,128)(2,1)}, bf16[8,128,128]{2,1,0:T(8,128)(2,1)S(1)}, u32[]{:S(2)}, u32[]{:S(2)}) collective-permute-start(bf16[8,128,128]{2,1,0:T(8,128)(2,1)} %get-tuple-element.80), channel_id=1, source_target_pairs={{0,4},{1,5},{2,6},{3,7},{4,0},{5,1},{6,2},{7,3},{8,12},{9,13},{10,... | collective-permute-start | bytes 786440 | tf_op jit(solution)/shard_map/ppermute | solution.py:396
  (20 other events, 59.2 us)

commit v4 on v3

--- a/solution.py
+++ b/solution.py
@@ -28,15 +28,15 @@
 KEPT = (((0, 0), (0, 1), (0, 2), (0, 3)), ((0, 0), (0, 3), (1, 0), (1, 3)), ((0, 0), (0, 1), (1, 0), (1, 1)))
 PAIRS = ((1, 0), (0, 1), (0, 3))
 PARTS_12 = (
-    ((1, (1, 0), 0, 2), (1, (1, 3), 0, 2), (2, (1, 0), 0, 2), (2, (1, 1), 0, 2)),
-    ((2, (0, 1), 2, 2), (2, (1, 1), 2, 2)),
-    ((1, (0, 3), 2, 2), (1, (1, 3), 2, 2)),
+    ((1, (1, 0), 0, 1), (1, (1, 3), 0, 1), (2, (1, 0), 0, 1), (2, (1, 1), 0, 1)),
+    ((2, (0, 1), 1, 3), (2, (1, 1), 1, 3)),
+    ((1, (0, 3), 1, 3), (1, (1, 3), 1, 3)),
     ((1, (0, 0), 0, 4),),
-    ((1, (0, 3), 0, 2),),
-    ((1, (1, 0), 2, 2),),
+    ((1, (0, 3), 0, 1),),
+    ((1, (1, 0), 1, 3),),
     ((2, (0, 0), 0, 4),),
-    ((2, (0, 1), 0, 2),),
-    ((2, (1, 0), 2, 2),),
+    ((2, (0, 1), 0, 1),),
+    ((2, (1, 0), 1, 3),),
 )
 PARTS_0 = (
     ((0, (0, 2), 0, 2),),
@@ -182,89 +182,155 @@
     )()
 
 
+def spread(rows, right):
+    diagonal = ((iota((16, 256), 0) & 7) == (iota((16, 256), 1) & 7)).astype(F32).astype(BF16)
+    left = dot(rows, right, ((1,), (1,))).astype(BF16)
+    return (left.reshape(-1, 16, 256) * diagonal[None]).reshape(left.shape)
+
+
+def some(x, third):
+    at = [PLACES.index(place) * 64 for place in KEPT[third]]
+    return jnp.concatenate([x[i : i + 64] for i in at], axis=0)
+
+
+def both_parts(both, who, ref, half, steps):
+    for s in range(steps):
+        for t in range(2):
+            at = s * 512 + t * 256
+            x = ref[at : at + 256, :]
+            both[s, who, half * 2 + t] = jnp.concatenate([x, swap_parts(x)], axis=1)
+
+
+def quarters(refs, held, sems):
+    return [
+        [
+            pltpu.make_async_copy(
+                ref.at[pl.ds(hi * 4, 4)], held.at[i, pl.ds(hi * 4, 4)], sems.at[hi, i]
+            )
+            for i, ref in enumerate(refs)
+        ]
+        for hi in range(4)
+    ]
+
+
+def own_kernel(steps, pick_hbm, a_hbm, b_hbm, *rest):
+    sources, outs = rest[:3], rest[3:6]
+    pick, senders, held, both, stacked, sems, late_sems, out_sems = rest[6:]
+    core = lax.axis_index("chan") & 1
+    early = [
+        pltpu.make_async_copy(src, dst, sems.at[i])
+        for i, (src, dst) in enumerate(
+            [(a_hbm, senders.at[0]), (b_hbm, senders.at[1]), (pick_hbm, pick)]
+        )
+    ]
+    late = quarters(sources, held, late_sems)
+    for copy in early + [copy for group in late for copy in group]:
+        copy.start()
+    for half in range(2):
+        early[half].wait()
+        both_parts(both, 0, senders.at[half], half, steps)
+    early[2].wait()
+    writes = []
+    for hi in range(4):
+        for copy in late[hi]:
+            copy.wait()
+        for lo in range(4):
+            block = hi * 4 + (((lo >> 1) ^ core) << 1) + (lo & 1)
+            own = [spread(pick[hi], both[s, 0, lo]) for s in range(steps)]
+            for third in range(3):
+                left = jnp.concatenate([some(x, third) for x in own], axis=0)
+                out = dot(left, held[third, block]).astype(BF16)
+                stacked[third, :, :, block] = out.reshape(steps, 16, 16, 128)
+        for third in range(3):
+            at = pl.ds(hi * 4, 4)
+            write = pltpu.make_async_copy(
+                stacked.at[third, :, :, at], outs[third].at[:, :, at], out_sems.at[hi, third]
+            )
+            write.start()
+            writes.append(write)
+    for write in writes:
+        write.wait()
+
+
+def correlate_own(pick, senders, receivers):
+    steps = senders[0].shape[0] // 512
+    hbm = pl.BlockSpec(memory_space=pl.ANY)
+    shape = (steps, 16, FB, 16, 128)
+    return pl.pallas_call(
+        functools.partial(own_kernel, steps),
+        out_shape=[jax.ShapeDtypeStruct(shape, BF16)] * 3,
+        in_specs=[hbm] * 6,
+        out_specs=[hbm] * 3,
+        scratch_shapes=[
+            pltpu.VMEM(pick.shape, BF16),
+            pltpu.VMEM((2,) + senders[0].shape, BF16),
+            pltpu.VMEM((3, FB, 256, 128), BF16),
+            pltpu.VMEM((steps, 1, 4, 256, 256), BF16),
+            pltpu.VMEM((3,) + shape, BF16),
+            pltpu.SemaphoreType.DMA((3,)),
+            pltpu.SemaphoreType.DMA((4, 3)),
+            pltpu.SemaphoreType.DMA((4, 3)),
+        ],
+        compiler_params=pltpu.CompilerParams(vmem_limit_bytes=24 * MB),
+        cost_estimate=pl.CostEstimate(flops=10**6, bytes_accessed=10**6, transcendentals=0),
+        name="correlate_own",
+    )(pick, *senders, *receivers)
+
+
 def correlate_kernel(thirds, steps, parts, *rest):
     nt = len(thirds)
     rest = list(rest)
-    ins = [rest.pop(0) for _ in range(4 + 4 * nt)]
+    ins = [rest.pop(0) for _ in range(2 + 2 * nt)]
+    partners = [rest.pop(0) for _ in range(nt)]
+    sums = [rest.pop(0) for _ in range(nt)]
     outs = [rest.pop(0) for _ in parts]
     results = [rest.pop(0) for _ in parts]
-    pick, lag_ref, senders, held, both, stacked, sems, out_sems = rest
+    pick, lag_ref, senders, held, summed, both, stacked, sems, late_sems, out_sems = rest
     core = lax.axis_index("chan") & 1
-    targets = [pick, lag_ref] + [senders.at[i] for i in range(2 + 2 * nt)]
+    targets = [pick, lag_ref] + [senders.at[i] for i in range(2 * nt)]
+    targets += [summed.at[i] for i in range(nt)]
     early = [
         pltpu.make_async_copy(src, dst, sems.at[i])
-        for i, (src, dst) in enumerate(zip(ins, targets))
+        for i, (src, dst) in enumerate(zip(ins + sums, targets))
     ]
-    sources = ins[len(early) :]
-    late = [
-        [
-            pltpu.make_async_copy(
-                ref.at[pl.ds(hi * 4, 4)],
-                held.at[i, pl.ds(hi * 4, 4)],
-                sems.at[len(early) + hi * 2 * nt + i],
-            )
-            for i, ref in enumerate(sources)
-        ]
-        for hi in range(4)
-    ]
-    for copy in early[2:] + early[:2]:
+    late = quarters(partners, held, late_sems)
+    last = [early[1]] + early[2 + 2 * nt :]
+    for copy in early[2 : 2 + 2 * nt] + early[:1] + [c for group in late for c in group] + last:
         copy.start()
-    for some in late:
-        for copy in some:
-            copy.start()
-    diagonal = ((iota((16, 256), 0) & 7) == (iota((16, 256), 1) & 7)).astype(F32).astype(BF16)
-    rows_of = sorted({place for t in thirds for place in KEPT[t]})
-
-    def spread(rows, right):
-        left = dot(rows, right, ((1,), (1,))).astype(BF16)
-        return (left.reshape(-1, 16, 256) * diagonal[None]).reshape(left.shape)
-
-    def some(x, order, third):
-        at = [order.index(place) * 64 for place in KEPT[third]]
-        return jnp.concatenate([x[i : i + 64] for i in at], axis=0)
-
-    for who in range(1 + nt):
+    for who in range(nt):
         for half in range(2):
             early[2 + who * 2 + half].wait()
-            for s in range(steps):
-                for t in range(2):
-                    at = s * 512 + t * 256
-                    x = senders[who * 2 + half, at : at + 256, :]
-                    both[s, who, half * 2 + t] = jnp.concatenate([x, swap_parts(x)], axis=1)
+            both_parts(both, who, senders.at[who * 2 + half], half, steps)
     early[0].wait()
     for hi in range(4):
         for copy in late[hi]:
             copy.wait()
         rows = pick[hi]
-        mine = jnp.concatenate(
-            [rows[PLACES.index(p) * 64 : PLACES.index(p) * 64 + 64] for p in rows_of], axis=0
-        )
         for lo in range(4):
             block = hi * 4 + (((lo >> 1) ^ core) << 1) + (lo & 1)
-            own = [spread(mine, both[s, 0, lo]) for s in range(steps)]
             for i, third in enumerate(thirds):
-                left = []
-                for s in range(steps):
-                    other = spread(some(rows, PLACES, third), both[s, 1 + i, lo])
-                    left.append(jnp.concatenate([some(own[s], rows_of, third), other], axis=1))
-                left = jnp.concatenate(left, axis=0)
-                right = jnp.concatenate([held[i, block], held[nt + i, block]], axis=0)
-                out = dot(left, right).astype(BF16).reshape(steps, 16, 16, 128)
-                for s in range(steps):
-                    stacked[s, i, :, block] = out[s]
-    early[1].wait()
-    lag = lag_ref[...]
+                left = [spread(some(rows, third), both[s, i, lo]) for s in range(steps)]
+                out = dot(jnp.concatenate(left, axis=0), held[i, block]).astype(BF16)
+                stacked[i, :, :, block] = out.reshape(steps, 16, 16, 128)
+    for copy in last:
+        copy.wait()
+    lag = jnp.concatenate([lag_ref[...], lag_ref[...]], axis=1)
     writes = []
     for p, (part, result, out) in enumerate(zip(parts, results, outs)):
-        for s in range(steps):
-            place = s * (out.shape[0] // steps)
-            for third, where, first, amount in part:
-                i, at = thirds.index(third), KEPT[third].index(where) * 4 + first
-                for r in range(0, amount, 2):
-                    x = [stacked[s, i, at + r + k].reshape(256, 128) for k in range(2)]
-                    y = dot(lag, jnp.concatenate(x, axis=1)).astype(BF16)
-                    result[place + r], result[place + r + 1] = y[:, :128], y[:, 128:]
-                place += amount
+        wanted = [
+            (s, thirds.index(third), KEPT[third].index(where) * 4 + first + r)
+            for s in range(steps)
+            for third, where, first, amount in part
+            for r in range(amount)
+        ]
+        for k in range(0, len(wanted), 2):
+            x = [
+                jnp.concatenate([ref[i, s, row].reshape(256, 128) for ref in (summed, stacked)])
+                for s, i, row in wanted[k : k + 2]
+            ]
+            y = dot(lag, jnp.concatenate(x, axis=1)).astype(BF16)
+            for j in range(len(x)):
+                result[k + j] = y[:, j * 128 : (j + 1) * 128]
         write = pltpu.make_async_copy(result, out, out_sems.at[p])
         write.start()
         writes.append(write)
@@ -272,11 +338,11 @@
         write.wait()
 
 
-def correlate(thirds, parts, pick, lags, senders, receivers, partners, limit=60):
+def correlate(thirds, parts, pick, lags, senders, partners, sums):
     steps, nt = senders[0].shape[0] // 512, len(thirds)
     hbm = pl.BlockSpec(memory_space=pl.ANY)
     sizes = [sum(piece[3] for piece in part) * steps for part in parts]
-    ins = [pick, lags, *senders, *receivers, *partners]
+    ins = [pick, lags, *senders, *partners, *sums]
     return pl.pallas_call(
         functools.partial(correlate_kernel, thirds, steps, parts),
         out_shape=[jax.ShapeDtypeStruct((n, NLAG, 128), BF16) for n in sizes],
@@ -286,17 +352,26 @@
         + [
             pltpu.VMEM(pick.shape, BF16),
             pltpu.VMEM(lags.shape, BF16),
-            pltpu.VMEM((2 + 2 * nt,) + senders[0].shape, BF16),
-            pltpu.VMEM((2 * nt, FB, 256, 128), BF16),
-            pltpu.VMEM((steps, 1 + nt, 4, 256, 256), BF16),
-            pltpu.VMEM((steps, nt, 16, FB, 16, 128), BF16),
-            pltpu.SemaphoreType.DMA((4 + 2 * nt + 8 * nt,)),
+            pltpu.VMEM((2 * nt,) + senders[0].shape, BF16),
+            pltpu.VMEM((nt, FB, 256, 128), BF16),
+            pltpu.VMEM((nt,) + sums[0].shape, BF16),
+            pltpu.VMEM((steps, nt, 4, 256, 256), BF16),
+            pltpu.VMEM((nt,) + sums[0].shape, BF16),
+            pltpu.SemaphoreType.DMA((2 + 3 * nt,)),
+            pltpu.SemaphoreType.DMA((4, nt)),
             pltpu.SemaphoreType.DMA((len(sizes),)),
         ],
-        compiler_params=pltpu.CompilerParams(vmem_limit_bytes=limit * MB),
+        compiler_params=pltpu.CompilerParams(vmem_limit_bytes=24 * MB),
         cost_estimate=pl.CostEstimate(flops=10**6, bytes_accessed=10**6, transcendentals=0),
         name="correlate",
     )(*ins)
+
+
+def by_step(refs):
+    for s in range(STEPS):
+        yield [
+            ref.at[pl.ds(s * (ref.shape[0] // STEPS), ref.shape[0] // STEPS)] for ref in refs
+        ]
 
 
 def finish_kernel(*refs):
@@ -309,28 +384,18 @@
             first = first + x.astype(F32)
         return first.T
 
-    for s in range(STEPS):
-        rows = [ref.shape[0] // STEPS for ref in ins]
-        g0, k1, k2, y1, xa1, xb1, y2, xa2, xb2 = [
-            ref.at[pl.ds(s * n, n)] for ref, n in zip(ins, rows)
-        ]
-
-        def put(r, third, value, s=s):
-            out[r, s, third * 128 : (third + 1) * 128, :] = value
-
-        @pl.when(half == 0)
-        def _():
-            for r in range(2):
-                put(r, 0, total(g0[r], xa2[r], xb2[r]))
-                put(r, 1, total(k1[r], y1[r], xb2[4 + r]))
-                put(r, 2, total(k2[r], y1[4 + r], xa2[4 + r]))
-
-        @pl.when(half == 1)
-        def _():
-            for r in range(2):
-                put(r, 0, total(g0[2 + r], xa2[2 + r], xb2[2 + r]))
-                put(r, 1, total(k1[2 + r], xb1[r], y2[r]))
-                put(r, 2, total(k2[2 + r], xa1[r], y2[2 + r]))
+    for s, (g0, k1, k2, y1, xa1, xb1, y2, xa2, xb2) in enumerate(by_step(ins)):
+        for h in range(2):
+
+            @pl.when(half == h)
+            def _():
+                for j in range(2):
+                    r = 2 * h + j
+                    one, two = (y1[0], xb2[4]) if r == 0 else (xb1[r - 1], y2[r - 1])
+                    three, four = (y1[2], xa2[4]) if r == 0 else (xa1[r - 1], y2[2 + r])
+                    out[j, s, :128, :] = total(g0[r], xa2[r], xb2[r])
+                    out[j, s, 128:256, :] = total(k1[r], one, two)
+                    out[j, s, 256:, :] = total(k2[r], three, four)
 
 
 def finish(ins, channels):
@@ -343,40 +408,46 @@
         out_shape=jax.ShapeDtypeStruct((4, STEPS, channels, NLAG), F32),
         in_specs=[whole(x) for x in ins],
         out_specs=pl.BlockSpec((2, STEPS, channels, NLAG), lambda h: (h, 0, 0, 0)),
-        compiler_params=pltpu.CompilerParams(vmem_limit_bytes=60 * MB),
+        compiler_params=pltpu.CompilerParams(vmem_limit_bytes=FIN * MB),
         name="finish",
     )(*ins)
 
 
-def merge_kernel(*refs):
-    rows = [ref.shape[0] // STEPS for ref in refs]
-
-    def add(x, y):
-        return (x.astype(F32) + y.astype(F32)).astype(BF16)
-
-    for s in range(STEPS):
-        g1, g3, k13, k10, k21, k20, y, xa, xb, ua, ub, y2, xa2, xb2 = [
-            ref.at[pl.ds(s * n, n)] for ref, n in zip(refs, rows)
-        ]
+FIN = 16
+
+
+def add(x, y):
+    return (x.astype(F32) + y.astype(F32)).astype(BF16)
+
+
+def merge_thirds_kernel(*refs):
+    for k13, k10, k21, k20, y, xa, xb, y2, m21, m13 in by_step(refs):
+        for r in range(3):
+            y2[r] = add(k10[r], xb[3 + r])
+            y2[3 + r] = add(k20[r], xa[3 + r])
+        m21[0] = add(k21[0], y[3])
+        m13[0] = add(k13[0], y[1])
+
+
+def merge_ring_kernel(*refs):
+    for g1, g3, ua, ub, m21, m13, xa2, xb2 in by_step(refs):
         for r in range(2):
-            y2[r] = add(k10[r], xb[2 + r])
-            y2[2 + r] = add(k20[r], xa[2 + r])
             xa2[r] = g1[r]
             xa2[2 + r] = add(g1[2 + r], ub[r])
-            xa2[4 + r] = add(k21[r], y[6 + r])
             xb2[r] = add(g3[r], ua[r])
             xb2[2 + r] = g3[2 + r]
-            xb2[4 + r] = add(k13[r], y[2 + r])
-
-
-def merge(ins, sizes):
+        xa2[4] = m21[0]
+        xb2[4] = m13[0]
+
+
+def merge(kernel, ins, sizes):
     vmem = pl.BlockSpec(memory_space=pltpu.VMEM)
     return pl.pallas_call(
-        merge_kernel,
-        out_shape=[jax.ShapeDtypeStruct((n,) + ins[0].shape[1:], BF16) for n in sizes],
+        kernel,
+        out_shape=[jax.ShapeDtypeStruct((n * STEPS,) + ins[0].shape[1:], BF16) for n in sizes],
         in_specs=[vmem] * len(ins),
         out_specs=[vmem] * len(sizes),
-        compiler_params=pltpu.CompilerParams(vmem_limit_bytes=60 * MB),
+        compiler_params=pltpu.CompilerParams(vmem_limit_bytes=FIN * MB),
         name="merge",
     )(*ins)
 
@@ -398,28 +469,32 @@
     r0, r1, r2, keep0, keep1, send0, send1 = spectra(traces, channel_mask, source_blocks, table)
     p1, p2 = win_swap(r1, PAIRS[1]), win_swap(r2, PAIRS[2])
     part0, part1 = keep0 + chan_swap(send0, 1), keep1 + chan_swap(send1, 1)
-    part0, part1 = part0 + chan_swap(part0, 8), part1 + chan_swap(part1, 8)
     pick = pick_rows()
-    part0, part1, r0, pick = lax.optimization_barrier((part0, part1, r0, pick))
-    p0 = win_swap(r0, PAIRS[0])
-
-    for one, other in ((2, 6), (6, 2)):
+    for one, other in ((8, 2), (2, 8), (6, 6)):
         part0, part1 = part0 + chan_swap(part0, one), part1 + chan_swap(part1, other)
+        if one == 8:
+            part1, pick = lax.optimization_barrier((part1, pick))
+        if other == 8:
+            part0, part1, r0 = lax.optimization_barrier((part0, part1, r0))
+            p0 = win_swap(r0, PAIRS[0])
     part0, part1, p1, p2 = lax.optimization_barrier((part0, part1, p1, p2))
     part = jnp.concatenate([part0, part1])
-    own, *found = [part] + [win_swap(part, pair) for pair in (PAIRS[1], PAIRS[2], PAIRS[0])]
-    own = (own, chan_swap(own, 1))
-    from_a, from_b = [(half, chan_swap(half, 1)) for half in found[:2]]
+    from_a, from_b, from_y = [win_swap(part, pair) for pair in (PAIRS[1], PAIRS[2], PAIRS[0])]
+    s0, s1, s2 = correlate_own(pick, (part, chan_swap(part, 1)), (r0, r1, r2))
+    from_a, from_b, s0, s1, s2 = lax.optimization_barrier((from_a, from_b, s0, s1, s2))
+    senders = [x for half in (from_a, from_b) for x in (half, chan_swap(half, 1))]
     y1, xa1, xb1, k1, k13, k10, k2, k21, k20 = correlate(
-        (1, 2), PARTS_12, pick, lags, own + from_a + from_b, (r1, r2), (p1, p2)
+        (1, 2), PARTS_12, pick, lags, senders, (p1, p2), (s1, s2)
     )
-    own, from_y, p0, y1, xa1, xb1 = lax.optimization_barrier((own, found[2], p0, y1, xa1, xb1))
-    from_y = (from_y, chan_swap(from_y, 1))
+    from_y, p0, y1, xa1, xb1 = lax.optimization_barrier((from_y, p0, y1, xa1, xb1))
     y1, xa1, xb1 = win_swap(y1, (1, 0)), win_swap(xa1, (0, 1)), win_swap(xb1, (0, 3))
-    ua, ub, g0, g1, g3 = correlate((0,), PARTS_0, pick, lags, own + from_y, (r0,), (p0,))
+    senders = [from_y, chan_swap(from_y, 1)]
+    ua, ub, g0, g1, g3 = correlate((0,), PARTS_0, pick, lags, senders, (p0,), (s0,))
     ua, ub = win_swap(ua, (0, 1)), win_swap(ub, (0, 3))
-    y2, xa2, xb2 = merge([g1, g3, k13, k10, k21, k20, y1, xa1, xb1, ua, ub], [8, 12, 12])
-    y2, xa2, xb2 = win_swap(y2, (1, 0)), win_swap(xa2, (0, 1)), win_swap(xb2, (0, 3))
+    y2, m21, m13 = merge(merge_thirds_kernel, [k13, k10, k21, k20, y1, xa1, xb1], [6, 1, 1])
+    y2 = win_swap(y2, (1, 0))
+    xa2, xb2 = merge(merge_ring_kernel, [g1, g3, ua, ub, m21, m13], [5, 5])
+    xa2, xb2 = win_swap(xa2, (0, 1)), win_swap(xb2, (0, 3))
     return finish([g0, k1, k2, y1, xa1, xb1, y2, xa2, xb2], channels)
 
 

time: 106 us -> 93.7 us (0.88)
  waiting for transfers between devices: 37.8 us -> 25.7 us
  local copies, waits for them, and re-layouts: 3.64 us -> 0.05 us
  starting transfers between devices: 24.7 us -> 28.1 us
  Pallas kernels: 37.7 us -> 36.3 us
    ppermute x14, waiting for transfers between devices: 19 us -> 12.9 us  [win_swap(): return lax.ppermute(x, 'win', [(i, i ^ bits) for i in range(8)])]
    ppermute x12, waiting for transfers between devices: 18.7 us -> 12.8 us  [chan_swap(): return lax.ppermute(x, 'chan', [(i, i ^ bits) for i in range(16)])]
    pallas_call x1 -> x3, Pallas kernels: 2.66 us -> 8.06 us  [the longest x1 7.87 us: correlate_own(): pl.pallas_call(functools.partial(own_kernel, steps), out_shape=[jax.Shape...]
    pallas_call x2, Pallas kernels: 22.2 us -> 17.2 us  [correlate(): pl.pallas_call(functools.partial(correlate_kernel, thirds, steps, parts),...]
    unnamed x37 -> x11, local copies, waits for them, and re-layouts: 3.62 us -> 0.03 us
    ppermute x12, starting transfers between devices: 8.62 us -> 12 us  [chan_swap(): return lax.ppermute(x, 'chan', [(i, i ^ bits) for i in range(16)])]
    pallas_call x1, Pallas kernels: 3.36 us -> 1.59 us  [finish(): pl.pallas_call(finish_kernel, grid=(2,), out_shape=jax.ShapeDtypeStruct((...]
  transfers between devices with their start and end apart: 26 -> 26, of which waited for: 16 -> 15; matrix products, arithmetic and copies ran while one was open for 2% -> 3% of each run, Pallas kernels for 22% -> 28%
where the time goes in v4:
time: 93.7 us; the launch traced here: 93.5 us
  Pallas kernels  36.3 us (39%)
  starting transfers between devices  28.1 us (30%)
  waiting for transfers between devices  25.7 us (27%)
  other arithmetic  3.17 us (3%)
    pallas_call x2, Pallas kernels, correlate(): pl.pallas_call(functools.partial(correlate_kernel, thirds, steps, parts),...  17.2 us
    ppermute x14, starting transfers between devices, win_swap(): return lax.ppermute(x, 'win', [(i, i ^ bits) for i in range(8)])  16.1 us
    ppermute x14, waiting for transfers between devices, win_swap(): return lax.ppermute(x, 'win', [(i, i ^ bits) for i in range(8)])  12.9 us
    ppermute x12, waiting for transfers between devices, chan_swap(): return lax.ppermute(x, 'chan', [(i, i ^ bits) for i in range(16)])  12.8 us
    ppermute x12, starting transfers between devices, chan_swap(): return lax.ppermute(x, 'chan', [(i, i ^ bits) for i in range(16)])  12 us
    pallas_call x1, Pallas kernels, spectra(): pl.pallas_call(spectra_kernel, grid=(count // chunk,), out_shape=[third]...  8.28 us
    pallas_call x1, Pallas kernels, correlate_own(): pl.pallas_call(functools.partial(own_kernel, steps), out_shape=[jax.Shape...  7.87 us
    add x2, other arithmetic, on_device(): part0, part1 = (keep0 + chan_swap(send0, 1), keep1 + chan_swap(send1, 1))  2.03 us
  transfers between devices with their start and end apart: 26, of which 15 were waited for; matrix products, arithmetic and copies ran while one was open for 3% of the time, Pallas kernels for 28%

profile of v4, /device:TPU:0, one launch (start us, length us, event | category | flops | bytes accessed | tf_op | source)
XLA Modules:
  0.0 93.5 jit_solution(12171288412479828406)
XLA Ops:
  0.0 8.3 %spectra.1 = (bf16[16,256,128]{2,1,0:T(8,128)(2,1)}, bf16[16,256,128]{2,1,0:T(8,128)(2,1)}, bf16[16,256,128]{2,1,0:T(8,128)(2,1)}, bf16[512,128]{1,0:T(8,128)(2,...) custom-call(s32[2,4]{1,0:T(2,128)} %blocks_ref.1, ...), custom_call_target="tpu_custom_call" | custom-call | flops 1000000000 | bytes 10000000 | tf_op jit(solution)/shard_map/spectra/pallas_call | solution.py:140
  8.3 1.6 %collective-permute-start.8 = (bf16[16,256,128]{2,1,0:T(8,128)(2,1)}, bf16[16,256,128]{2,1,0:T(8,128)(2,1)}, u32[]{:S(2)}, u32[]{:S(2)}) collective-permute-start(bf16[16,256,128]{2,1,0:T(8,128)(2,1)} %get-tuple-element.62.rest_1_), channel_id=1, source_target_pairs={{0,1},{1,0},{2,3},{3,2},{4,5},{5,4},{6,7},{7,6},{8,9},{9,8},{10,11... | collective-permute-start | bytes 3145736 | tf_op jit(solution)/shard_map/ppermute | solution.py:467
  9.9 2.1 %collective-permute-start.9 = (bf16[16,256,128]{2,1,0:T(8,128)(2,1)}, bf16[16,256,128]{2,1,0:T(8,128)(2,1)}, u32[]{:S(2)}, u32[]{:S(2)}) collective-permute-start(bf16[16,256,128]{2,1,0:T(8,128)(2,1)} %get-tuple-element.63.rest_2_), channel_id=1, source_target_pairs={{0,3},{1,2},{2,1},{3,0},{4,7},{5,6},{6,5},{7,4},{8,11},{9,10},{10,... | collective-permute-start | bytes 3145736 | tf_op jit(solution)/shard_map/ppermute | solution.py:467
  14.5 2.0 %collective-permute-start.1 = (bf16[512,128]{1,0:T(8,128)(2,1)S(1)}, bf16[512,128]{1,0:T(8,128)(2,1)S(1)}, u32[]{:S(2)}, u32[]{:S(2)}) collective-permute-start(bf16[512,128]{1,0:T(8,128)(2,1)S(1)} %add.24), channel_id=1, source_target_pairs={{0,16},{8,24},{16,0},{24,8},{32,48},{40,56},{48,32},{56,40},{64,80... | collective-permute-start | bytes 393224 | tf_op jit(solution)/shard_map/ppermute | solution.py:463
  17.6 3.3 %collective-permute-start.3 = (bf16[512,128]{1,0:T(8,128)(2,1)S(1)}, bf16[512,128]{1,0:T(8,128)(2,1)}, u32[]{:S(2)}, u32[]{:S(2)}) collective-permute-start(bf16[512,128]{1,0:T(8,128)(2,1)S(1)} %add.26), channel_id=1, source_target_pairs={{0,64},{8,72},{16,80},{24,88},{32,96},{40,104},{48,112},{56,120},{... | collective-permute-start | bytes 393224 | tf_op jit(solution)/shard_map/ppermute | solution.py:463
  20.9 1.2 %pick_rows.1.pick_hbm.rest_0_ = bf16[4,448,256]{2,1,0:T(8,128)(2,1)} custom-call(), custom_call_target="tpu_custom_call" | custom-call | flops 1000000 | bytes 1000000 | tf_op jit(solution)/shard_map/pick_rows/pallas_call | solution.py:176
  22.1 1.5 %collective-permute-start.5 = (bf16[512,128]{1,0:T(8,128)(2,1)S(1)}, bf16[512,128]{1,0:T(8,128)(2,1)S(1)}, u32[]{:S(2)}, u32[]{:S(2)}) collective-permute-start(bf16[512,128]{1,0:T(8,128)(2,1)S(1)} %add.25), channel_id=1, source_target_pairs={{0,64},{8,72},{16,80},{24,88},{32,96},{40,104},{48,112},{56,120},{... | collective-permute-start | bytes 393224 | tf_op jit(solution)/shard_map/ppermute | solution.py:463
  26.4 2.3 %collective-permute-done.5 = bf16[512,128]{1,0:T(8,128)(2,1)S(1)} collective-permute-done((bf16[512,128]{1,0:T(8,128)(2,1)S(1)}, bf16[512,128]{1,0:T(8,128)(2,1)S(1)}, u32[]{:S(2)}, u32[]{:S(2)}) %collective-permute-start.5) | collective-permute-done | bytes 131104 | tf_op jit(solution)/shard_map/ppermute | solution.py:463
  28.7 1.8 %collective-permute-done.4 = bf16[512,128]{1,0:T(8,128)(2,1)S(1)} collective-permute-done((bf16[512,128]{1,0:T(8,128)(2,1)S(1)}, bf16[512,128]{1,0:T(8,128)(2,1)S(1)}, u32[]{:S(2)}, u32[]{:S(2)}) %collective-permute-start.4) | collective-permute-done | bytes 131104 | tf_op jit(solution)/shard_map/ppermute | solution.py:463
  30.6 1.7 %collective-permute-start.11 = (bf16[16,256,128]{2,1,0:T(8,128)(2,1)S(1)}, bf16[16,256,128]{2,1,0:T(8,128)(2,1)S(1)}, u32[]{:S(2)}, u32[]{:S(2)}) collective-permute-start(bf16[16,256,128]{2,1,0:T(8,128)(2,1)S(1)} %copy-done.1), channel_id=1, source_target_pairs={{0,4},{1,5},{2,6},{3,7},{4,0},{5,1},{6,2},{7,3},{8,12},{9,13},{10,... | collective-permute-start | bytes 3145736 | tf_op jit(solution)/shard_map/ppermute | solution.py:467
  32.3 2.5 %collective-permute-start.7 = (bf16[512,128]{1,0:T(8,128)(2,1)S(1)}, bf16[512,128]{1,0:T(8,128)(2,1)S(1)}, u32[]{:S(2)}, u32[]{:S(2)}) collective-permute-start(bf16[512,128]{1,0:T(8,128)(2,1)S(1)} %add.29), channel_id=1, source_target_pairs={{0,48},{8,56},{16,32},{24,40},{32,16},{40,24},{48,0},{56,8},{64,11... | collective-permute-start | bytes 393224 | tf_op jit(solution)/shard_map/ppermute | solution.py:463
  35.5 3.6 %collective-permute-done.7 = bf16[512,128]{1,0:T(8,128)(2,1)S(1)} collective-permute-done((bf16[512,128]{1,0:T(8,128)(2,1)S(1)}, bf16[512,128]{1,0:T(8,128)(2,1)S(1)}, u32[]{:S(2)}, u32[]{:S(2)}) %collective-permute-start.7) | collective-permute-done | bytes 131104 | tf_op jit(solution)/shard_map/ppermute | solution.py:463
  39.1 1.8 %collective-permute-done.6 = bf16[512,128]{1,0:T(8,128)(2,1)S(1)} collective-permute-done((bf16[512,128]{1,0:T(8,128)(2,1)S(1)}, bf16[512,128]{1,0:T(8,128)(2,1)S(1)}, u32[]{:S(2)}, u32[]{:S(2)}) %collective-permute-start.6) | collective-permute-done | bytes 131104 | tf_op jit(solution)/shard_map/ppermute | solution.py:463
  42.7 7.9 %correlate_own.1 = (bf16[2,16,16,16,128]{4,3,2,1,0:T(8,128)(2,1)S(1)}, bf16[2,16,16,16,128]{4,3,2,1,0:T(8,128)(2,1)S(1)}, bf16[2,16,16,16,128]{4,3,2,1,0:T(8,128)(2,1)S(1)}) custom-call(bf16[4,448,256]{2,1,0:T(8,128)(2,1)S(1)} %copy-done, bf16[1024,128]{1,0:T(8,128)(2,1)S(1)} %constant_dynamic-update-slice_fusion.a_hbm, ...), custom_call_target="tpu_custom_call" | custom-call | flops 1000000 | bytes 1000000 | tf_op jit(solution)/shard_map/correlate_own/pallas_call | solution.py:259
  53.3 11.1 %correlate.2 = (bf16[8,128,128]{2,1,0:T(8,128)(2,1)S(1)}, bf16[12,128,128]{2,1,0:T(8,128)(2,1)S(1)}, bf16[12,128,128]{2,1,0:T(8,128)(2,1)S(1)}, bf16[8,128,128]{...) custom-call(bf16[4,448,256]{2,1,0:T(8,128)(2,1)S(1)} %copy-done, ...), custom_call_target="tpu_custom_call" | custom-call | flops 1000000 | bytes 1000000 | tf_op jit(solution)/shard_map/correlate/pallas_call | solution.py:346
  64.9 2.1 %collective-permute-start.20 = (bf16[12,128,128]{2,1,0:T(8,128)(2,1)S(1)}, bf16[12,128,128]{2,1,0:T(8,128)(2,1)S(1)}, u32[]{:S(2)}, u32[]{:S(2)}) collective-permute-start(bf16[12,128,128]{2,1,0:T(8,128)(2,1)S(1)} %get-tuple-element.87), channel_id=1, source_target_pairs={{0,3},{1,2},{2,1},{3,0},{4,7},{5,6},{6,5},{7,4},{8,11},{9,10},{10,... | collective-permute-start | bytes 1179656 | tf_op jit(solution)/shard_map/ppermute | solution.py:467
  68.6 6.1 %correlate.3 = (bf16[4,128,128]{2,1,0:T(8,128)(2,1)S(1)}, bf16[4,128,128]{2,1,0:T(8,128)(2,1)S(1)}, bf16[8,128,128]{2,1,0:T(8,128)(2,1)S(1)}, bf16[8,128,128]{2,1,0:T(8,128)(2,1)S(1)}, bf16[8,128,128]{2,1,0:T(8,128)(2,1)S(1)}) custom-call(bf16[4,448,256]{2,1,0:T(8,128)(2,1)S(1)} %copy-done, bf16[128,256]{1,0:T(8,128)(2,1)S(1)} %copy-done.4, ...), custom_call_target="tpu_custom_call" | custom-call | flops 1000000 | bytes 1000000 | tf_op jit(solution)/shard_map/correlate/pallas_call | solution.py:346
  75.3 1.6 %collective-permute-start.23 = (bf16[4,128,128]{2,1,0:T(8,128)(2,1)S(1)}, bf16[4,128,128]{2,1,0:T(8,128)(2,1)S(1)}, u32[]{:S(2)}, u32[]{:S(2)}) collective-permute-start(bf16[4,128,128]{2,1,0:T(8,128)(2,1)S(1)} %get-tuple-element.96), channel_id=1, source_target_pairs={{0,3},{1,2},{2,1},{3,0},{4,7},{5,6},{6,5},{7,4},{8,11},{9,10},{10,... | collective-permute-start | bytes 393224 | tf_op jit(solution)/shard_map/ppermute | solution.py:467
  78.1 2.2 %collective-permute-done.22.refs_2_ = bf16[4,128,128]{2,1,0:T(8,128)(2,1)S(1)} collective-permute-done((bf16[4,128,128]{2,1,0:T(8,128)(2,1)S(1)}, bf16[4,128,128]{2,1,0:T(8,128)(2,1)S(1)}, u32[]{:S(2)}, u32[]{:S(2)}) %collective-permute-start.22) | collective-permute-done | bytes 131104 | tf_op jit(solution)/shard_map/ppermute | solution.py:467
  80.3 1.5 %collective-permute-done.23.refs_3_ = bf16[4,128,128]{2,1,0:T(8,128)(2,1)S(1)} collective-permute-done((bf16[4,128,128]{2,1,0:T(8,128)(2,1)S(1)}, bf16[4,128,128]{2,1,0:T(8,128)(2,1)S(1)}, u32[]{:S(2)}, u32[]{:S(2)}) %collective-permute-start.23) | collective-permute-done | bytes 131104 | tf_op jit(solution)/shard_map/ppermute | solution.py:467
  82.2 1.5 %collective-permute-start.25 = (bf16[10,128,128]{2,1,0:T(8,128)(2,1)S(1)}, bf16[10,128,128]{2,1,0:T(8,128)(2,1)S(1)}, u32[]{:S(2)}, u32[]{:S(2)}) collective-permute-start(bf16[10,128,128]{2,1,0:T(8,128)(2,1)S(1)} %get-tuple-element.100), channel_id=1, source_target_pairs={{0,3},{1,2},{2,1},{3,0},{4,7},{5,6},{6,5},{7,4},{8,11},{9,10},{10,... | collective-permute-start | bytes 983048 | tf_op jit(solution)/shard_map/ppermute | solution.py:467
  83.6 6.9 %collective-permute-done.24.refs_7_ = bf16[10,128,128]{2,1,0:T(8,128)(2,1)S(1)} collective-permute-done((bf16[10,128,128]{2,1,0:T(8,128)(2,1)S(1)}, bf16[10,128,128]{2,1,0:T(8,128)(2,1)S(1)}, u32[]{:S(2)}, u32[]{:S(2)}) %collective-permute-start.24) | collective-permute-done | bytes 327712 | tf_op jit(solution)/shard_map/ppermute | solution.py:467
  90.6 1.3 %collective-permute-done.25.refs_8_ = bf16[10,128,128]{2,1,0:T(8,128)(2,1)S(1)} collective-permute-done((bf16[10,128,128]{2,1,0:T(8,128)(2,1)S(1)}, bf16[10,128,128]{2,1,0:T(8,128)(2,1)S(1)}, u32[]{:S(2)}, u32[]{:S(2)}) %collective-permute-start.25) | collective-permute-done | bytes 327712 | tf_op jit(solution)/shard_map/ppermute | solution.py:467
  91.9 1.6 %finish.1 = f32[4,2,384,128]{3,2,1,0:T(8,128)} custom-call(bf16[8,128,128]{2,1,0:T(8,128)(2,1)S(1)} %get-tuple-element.82.refs_0_, bf16[8,128,128]{2,1,0:T(8,128)(2,1)S(1)} %get-tuple-element.83.refs_1_, bf16[8,128,128]{2,1,0:T(8,128)(2,1)S(1)} %get-tuple-element.84.refs_2_, bf16[8,128,128]{2,1,0:T(8,128)(2,1)S(1)} %collective-permute-done.18.refs_4_.refs_3_, ...), custom_call_target="tpu_custom_call" | custom-call | tf_op jit(solution)/shard_map/finish/pallas_call | solution.py:405
  (56 shorter events, 15.9 us)
Async XLA Ops:
  8.3 32.7 %collective-permute-start.8 = (bf16[16,256,128]{2,1,0:T(8,128)(2,1)}, bf16[16,256,128]{2,1,0:T(8,128)(2,1)}, u32[]{:S(2)}, u32[]{:S(2)}) collective-permute-start(bf16[16,256,128]{2,1,0:T(8,128)(2,1)} %get-tuple-element.62.rest_1_), channel_id=1, source_target_pairs={{0,1},{1,0},{2,3},{3,2},{4,5},{5,4},{6,7},{7,6},{8,9},{9,8},{10,11... | collective-permute-start | bytes 3145736 | tf_op jit(solution)/shard_map/ppermute | solution.py:467
  9.9 31.1 %collective-permute-start.9 = (bf16[16,256,128]{2,1,0:T(8,128)(2,1)}, bf16[16,256,128]{2,1,0:T(8,128)(2,1)}, u32[]{:S(2)}, u32[]{:S(2)}) collective-permute-start(bf16[16,256,128]{2,1,0:T(8,128)(2,1)} %get-tuple-element.63.rest_2_), channel_id=1, source_target_pairs={{0,3},{1,2},{2,1},{3,0},{4,7},{5,6},{6,5},{7,4},{8,11},{9,10},{10,... | collective-permute-start | bytes 3145736 | tf_op jit(solution)/shard_map/ppermute | solution.py:467
  12.0 1.6 %collective-permute-start = (bf16[512,128]{1,0:T(8,128)(2,1)}, bf16[512,128]{1,0:T(8,128)(2,1)S(1)}, u32[]{:S(2)}, u32[]{:S(2)}) collective-permute-start(bf16[512,128]{1,0:T(8,128)(2,1)} %get-tuple-element.54), channel_id=1, source_target_pairs={{0,8},{8,0},{16,24},{24,16},{32,40},{40,32},{48,56},{56,48},{64,72... | collective-permute-start | bytes 393224 | tf_op jit(solution)/shard_map/ppermute | solution.py:463
  12.0 4.5 %collective-permute-start.2 = (bf16[512,128]{1,0:T(8,128)(2,1)}, bf16[512,128]{1,0:T(8,128)(2,1)S(1)}, u32[]{:S(2)}, u32[]{:S(2)}) collective-permute-start(bf16[512,128]{1,0:T(8,128)(2,1)} %get-tuple-element.57), channel_id=1, source_target_pairs={{0,8},{8,0},{16,24},{24,16},{32,40},{40,32},{48,56},{56,48},{64,72... | collective-permute-start | bytes 393224 | tf_op jit(solution)/shard_map/ppermute | solution.py:463
  14.5 7.5 %collective-permute-start.1 = (bf16[512,128]{1,0:T(8,128)(2,1)S(1)}, bf16[512,128]{1,0:T(8,128)(2,1)S(1)}, u32[]{:S(2)}, u32[]{:S(2)}) collective-permute-start(bf16[512,128]{1,0:T(8,128)(2,1)S(1)} %add.24), channel_id=1, source_target_pairs={{0,16},{8,24},{16,0},{24,8},{32,48},{40,56},{48,32},{56,40},{64,80... | collective-permute-start | bytes 393224 | tf_op jit(solution)/shard_map/ppermute | solution.py:463
  17.6 7.0 %collective-permute-start.3 = (bf16[512,128]{1,0:T(8,128)(2,1)S(1)}, bf16[512,128]{1,0:T(8,128)(2,1)}, u32[]{:S(2)}, u32[]{:S(2)}) collective-permute-start(bf16[512,128]{1,0:T(8,128)(2,1)S(1)} %add.26), channel_id=1, source_target_pairs={{0,64},{8,72},{16,80},{24,88},{32,96},{40,104},{48,112},{56,120},{... | collective-permute-start | bytes 393224 | tf_op jit(solution)/shard_map/ppermute | solution.py:463
  22.1 6.6 %collective-permute-start.5 = (bf16[512,128]{1,0:T(8,128)(2,1)S(1)}, bf16[512,128]{1,0:T(8,128)(2,1)S(1)}, u32[]{:S(2)}, u32[]{:S(2)}) collective-permute-start(bf16[512,128]{1,0:T(8,128)(2,1)S(1)} %add.25), channel_id=1, source_target_pairs={{0,64},{8,72},{16,80},{24,88},{32,96},{40,104},{48,112},{56,120},{... | collective-permute-start | bytes 393224 | tf_op jit(solution)/shard_map/ppermute | solution.py:463
  25.5 5.0 %collective-permute-start.4 = (bf16[512,128]{1,0:T(8,128)(2,1)S(1)}, bf16[512,128]{1,0:T(8,128)(2,1)S(1)}, u32[]{:S(2)}, u32[]{:S(2)}) collective-permute-start(bf16[512,128]{1,0:T(8,128)(2,1)S(1)} %add.27), channel_id=1, source_target_pairs={{0,16},{8,24},{16,0},{24,8},{32,48},{40,56},{48,32},{56,40},{64,80... | collective-permute-start | bytes 393224 | tf_op jit(solution)/shard_map/ppermute | solution.py:463
  30.6 33.9 %collective-permute-start.11 = (bf16[16,256,128]{2,1,0:T(8,128)(2,1)S(1)}, bf16[16,256,128]{2,1,0:T(8,128)(2,1)S(1)}, u32[]{:S(2)}, u32[]{:S(2)}) collective-permute-start(bf16[16,256,128]{2,1,0:T(8,128)(2,1)S(1)} %copy-done.1), channel_id=1, source_target_pairs={{0,4},{1,5},{2,6},{3,7},{4,0},{5,1},{6,2},{7,3},{8,12},{9,13},{10,... | collective-permute-start | bytes 3145736 | tf_op jit(solution)/shard_map/ppermute | solution.py:467
  32.3 6.8 %collective-permute-start.7 = (bf16[512,128]{1,0:T(8,128)(2,1)S(1)}, bf16[512,128]{1,0:T(8,128)(2,1)S(1)}, u32[]{:S(2)}, u32[]{:S(2)}) collective-permute-start(bf16[512,128]{1,0:T(8,128)(2,1)S(1)} %add.29), channel_id=1, source_target_pairs={{0,48},{8,56},{16,32},{24,40},{32,16},{40,24},{48,0},{56,8},{64,11... | collective-permute-start | bytes 393224 | tf_op jit(solution)/shard_map/ppermute | solution.py:463
  34.8 6.2 %collective-permute-start.6 = (bf16[512,128]{1,0:T(8,128)(2,1)S(1)}, bf16[512,128]{1,0:T(8,128)(2,1)S(1)}, u32[]{:S(2)}, u32[]{:S(2)}) collective-permute-start(bf16[512,128]{1,0:T(8,128)(2,1)S(1)} %add.28), channel_id=1, source_target_pairs={{0,48},{8,56},{16,32},{24,40},{32,16},{40,24},{48,0},{56,8},{64,11... | collective-permute-start | bytes 393224 | tf_op jit(solution)/shard_map/ppermute | solution.py:463
  41.1 1.6 %collective-permute-start.14 = (bf16[1024,128]{1,0:T(8,128)(2,1)S(1)}, bf16[1024,128]{1,0:T(8,128)(2,1)S(1)}, u32[]{:S(2)}, u32[]{:S(2)}) collective-permute-start(bf16[1024,128]{1,0:T(8,128)(2,1)S(1)} %constant_dynamic-update-slice_fusion.a_hbm), channel_id=1, source_target_pairs={{0,8},{8,0},{16,24},{24,16},{32,40},{40,32},{48,56},{56,48},{64,72... | collective-permute-start | bytes 786440 | tf_op jit(solution)/shard_map/ppermute | solution.py:463
  41.2 9.4 %collective-permute-start.12 = (bf16[1024,128]{1,0:T(8,128)(2,1)S(1)}, bf16[1024,128]{1,0:T(8,128)(2,1)S(1)}, u32[]{:S(2)}, u32[]{:S(2)}) collective-permute-start(bf16[1024,128]{1,0:T(8,128)(2,1)S(1)} %constant_dynamic-update-slice_fusion.a_hbm), channel_id=1, source_target_pairs={{0,1},{1,0},{2,3},{3,2},{4,5},{5,4},{6,7},{7,6},{8,9},{9,8},{10,11... | collective-permute-start | bytes 786440 | tf_op jit(solution)/shard_map/ppermute | solution.py:467
  41.9 9.6 %collective-permute-start.13 = (bf16[1024,128]{1,0:T(8,128)(2,1)S(1)}, bf16[1024,128]{1,0:T(8,128)(2,1)S(1)}, u32[]{:S(2)}, u32[]{:S(2)}) collective-permute-start(bf16[1024,128]{1,0:T(8,128)(2,1)S(1)} %constant_dynamic-update-slice_fusion.a_hbm), channel_id=1, source_target_pairs={{0,3},{1,2},{2,1},{3,0},{4,7},{5,6},{6,5},{7,4},{8,11},{9,10},{10,... | collective-permute-start | bytes 786440 | tf_op jit(solution)/shard_map/ppermute | solution.py:467
  51.4 1.9 %collective-permute-start.16 = (bf16[1024,128]{1,0:T(8,128)(2,1)S(1)}, bf16[1024,128]{1,0:T(8,128)(2,1)S(1)}, u32[]{:S(2)}, u32[]{:S(2)}) collective-permute-start(bf16[1024,128]{1,0:T(8,128)(2,1)S(1)} %collective-permute-done.13.rest_4_), channel_id=1, source_target_pairs={{0,8},{8,0},{16,24},{24,16},{32,40},{40,32},{48,56},{56,48},{64,72... | collective-permute-start | bytes 786440 | tf_op jit(solution)/shard_map/ppermute | solution.py:463
  51.9 12.5 %collective-permute-start.10 = (bf16[1024,128]{1,0:T(8,128)(2,1)S(1)}, bf16[1024,128]{1,0:T(8,128)(2,1)S(1)}, u32[]{:S(2)}, u32[]{:S(2)}) collective-permute-start(bf16[1024,128]{1,0:T(8,128)(2,1)S(1)} %constant_dynamic-update-slice_fusion.a_hbm), channel_id=1, source_target_pairs={{0,4},{1,5},{2,6},{3,7},{4,0},{5,1},{6,2},{7,3},{8,12},{9,13},{10,... | collective-permute-start | bytes 786440 | tf_op jit(solution)/shard_map/ppermute | solution.py:467
  64.5 12.4 %collective-permute-start.19 = (bf16[12,128,128]{2,1,0:T(8,128)(2,1)S(1)}, bf16[12,128,128]{2,1,0:T(8,128)(2,1)S(1)}, u32[]{:S(2)}, u32[]{:S(2)}) collective-permute-start(bf16[12,128,128]{2,1,0:T(8,128)(2,1)S(1)} %get-tuple-element.86), channel_id=1, source_target_pairs={{0,1},{1,0},{2,3},{3,2},{4,5},{5,4},{6,7},{7,6},{8,9},{9,8},{10,11... | collective-permute-start | bytes 1179656 | tf_op jit(solution)/shard_map/ppermute | solution.py:467
  64.9 12.1 %collective-permute-start.20 = (bf16[12,128,128]{2,1,0:T(8,128)(2,1)S(1)}, bf16[12,128,128]{2,1,0:T(8,128)(2,1)S(1)}, u32[]{:S(2)}, u32[]{:S(2)}) collective-permute-start(bf16[12,128,128]{2,1,0:T(8,128)(2,1)S(1)} %get-tuple-element.87), channel_id=1, source_target_pairs={{0,3},{1,2},{2,1},{3,0},{4,7},{5,6},{6,5},{7,4},{8,11},{9,10},{10,... | collective-permute-start | bytes 1179656 | tf_op jit(solution)/shard_map/ppermute | solution.py:467
  67.0 9.9 %collective-permute-start.18 = (bf16[8,128,128]{2,1,0:T(8,128)(2,1)S(1)}, bf16[8,128,128]{2,1,0:T(8,128)(2,1)S(1)}, u32[]{:S(2)}, u32[]{:S(2)}) collective-permute-start(bf16[8,128,128]{2,1,0:T(8,128)(2,1)S(1)} %get-tuple-element.85), channel_id=1, source_target_pairs={{0,4},{1,5},{2,6},{3,7},{4,0},{5,1},{6,2},{7,3},{8,12},{9,13},{10,... | collective-permute-start | bytes 786440 | tf_op jit(solution)/shard_map/ppermute | solution.py:467
  74.7 5.6 %collective-permute-start.22 = (bf16[4,128,128]{2,1,0:T(8,128)(2,1)S(1)}, bf16[4,128,128]{2,1,0:T(8,128)(2,1)S(1)}, u32[]{:S(2)}, u32[]{:S(2)}) collective-permute-start(bf16[4,128,128]{2,1,0:T(8,128)(2,1)S(1)} %get-tuple-element.95), channel_id=1, source_target_pairs={{0,1},{1,0},{2,3},{3,2},{4,5},{5,4},{6,7},{7,6},{8,9},{9,8},{10,11... | collective-permute-start | bytes 393224 | tf_op jit(solution)/shard_map/ppermute | solution.py:467
  75.3 6.5 %collective-permute-start.23 = (bf16[4,128,128]{2,1,0:T(8,128)(2,1)S(1)}, bf16[4,128,128]{2,1,0:T(8,128)(2,1)S(1)}, u32[]{:S(2)}, u32[]{:S(2)}) collective-permute-start(bf16[4,128,128]{2,1,0:T(8,128)(2,1)S(1)} %get-tuple-element.96), channel_id=1, source_target_pairs={{0,3},{1,2},{2,1},{3,0},{4,7},{5,6},{6,5},{7,4},{8,11},{9,10},{10,... | collective-permute-start | bytes 393224 | tf_op jit(solution)/shard_map/ppermute | solution.py:467
  77.2 14.7 %collective-permute-start.21 = (bf16[12,128,128]{2,1,0:T(8,128)(2,1)S(1)}, bf16[12,128,128]{2,1,0:T(8,128)(2,1)S(1)}, u32[]{:S(2)}, u32[]{:S(2)}) collective-permute-start(bf16[12,128,128]{2,1,0:T(8,128)(2,1)S(1)} %get-tuple-element.92), channel_id=1, source_target_pairs={{0,4},{1,5},{2,6},{3,7},{4,0},{5,1},{6,2},{7,3},{8,12},{9,13},{10,... | collective-permute-start | bytes 1179656 | tf_op jit(solution)/shard_map/ppermute | solution.py:467
  81.9 8.7 %collective-permute-start.24 = (bf16[10,128,128]{2,1,0:T(8,128)(2,1)S(1)}, bf16[10,128,128]{2,1,0:T(8,128)(2,1)S(1)}, u32[]{:S(2)}, u32[]{:S(2)}) collective-permute-start(bf16[10,128,128]{2,1,0:T(8,128)(2,1)S(1)} %get-tuple-element.99), channel_id=1, source_target_pairs={{0,1},{1,0},{2,3},{3,2},{4,5},{5,4},{6,7},{7,6},{8,9},{9,8},{10,11... | collective-permute-start | bytes 983048 | tf_op jit(solution)/shard_map/ppermute | solution.py:467
  82.2 9.7 %collective-permute-start.25 = (bf16[10,128,128]{2,1,0:T(8,128)(2,1)S(1)}, bf16[10,128,128]{2,1,0:T(8,128)(2,1)S(1)}, u32[]{:S(2)}, u32[]{:S(2)}) collective-permute-start(bf16[10,128,128]{2,1,0:T(8,128)(2,1)S(1)} %get-tuple-element.100), channel_id=1, source_target_pairs={{0,3},{1,2},{2,1},{3,0},{4,7},{5,6},{6,5},{7,4},{8,11},{9,10},{10,... | collective-permute-start | bytes 983048 | tf_op jit(solution)/shard_map/ppermute | solution.py:467
  (7 other events, 110.7 us)

commit v5 on v4

v5 whole, which is shorter than its diff:
```python
import functools
import math

import jax
import jax.numpy as jnp
import ml_dtypes
import numpy as np
from jax import lax
from jax.experimental import pallas as pl
from jax.experimental.pallas import tpu as pltpu
from jax.sharding import PartitionSpec as P

NF = 128
F_LO = 8
NLAG = 128
VSB = 8
NSRC = 4
STEPS = 2
WATER_LEVEL = 0.05
TINY_ENERGY = 1e-06

FB = 16
BF16 = jnp.bfloat16
F32 = jnp.float32
MB = 2**20

PLACES = ((0, 0), (0, 1), (0, 2), (0, 3), (1, 0), (1, 1), (1, 3))
KEPT = (((0, 0), (0, 1), (0, 2), (0, 3)), ((0, 0), (0, 3), (1, 0), (1, 3)), ((0, 0), (0, 1), (1, 0), (1, 1)))
PAIRS = ((1, 0), (0, 1), (0, 3))
PARTS_12 = (
    ((1, (1, 0), 0, 1), (1, (1, 3), 0, 1), (2, (1, 0), 0, 1), (2, (1, 1), 0, 1)),
    ((2, (0, 1), 1, 3), (2, (1, 1), 1, 3)),
    ((1, (0, 3), 1, 3), (1, (1, 3), 1, 3)),
    ((1, (0, 0), 0, 4),),
    ((1, (0, 3), 0, 1),),
    ((1, (1, 0), 1, 3),),
    ((2, (0, 0), 0, 4),),
    ((2, (0, 1), 0, 1),),
    ((2, (1, 0), 1, 3),),
)
PARTS_0 = (
    ((0, (0, 2), 0, 2),),
    ((0, (0, 2), 2, 2),),
    ((0, (0, 0), 0, 4),),
    ((0, (0, 1), 0, 4),),
    ((0, (0, 3), 0, 4),),
)


def band_rows():
    row = np.arange(2 * NF)
    return F_LO + (row // 16) * 8 + row % 8, (row // 8) % 2


def dft_rows(length):
    bins, part = band_rows()
    t = np.arange(length)
    angle = (t[None, :] * bins[:, None] % length) * (2.0 * math.pi / length)
    taper = 0.5 - 0.5 * np.cos((t + 0.5) * (2.0 * math.pi / length))
    table = np.where(part[:, None] == 0, np.cos(angle), -np.sin(angle)) * taper[None, :]
    return table.astype(np.float32).astype(ml_dtypes.bfloat16)


def lag_rows(length, scale):
    bins, part = band_rows()
    shift = np.arange(NLAG) - NLAG // 2
    angle = (shift[:, None] * bins[None, :] % length) * (2.0 * math.pi / length)
    table = np.where(part[None, :] == 0, np.cos(angle), -np.sin(angle))
    table = table.astype(np.float32).astype(ml_dtypes.bfloat16)
    return (table.astype(np.float32) * scale).astype(ml_dtypes.bfloat16)


def dot(a, b, dims=((1,), (0,))):
    return lax.dot_general(a, b, (dims, ((), ())), preferred_element_type=F32)


def iota(shape, dim):
    return lax.broadcasted_iota(jnp.int32, shape, dim)


def whiten_rows(z, live):
    lanes = z.shape[-1]
    z = z.reshape(FB, 2, 8, lanes)
    re, im = z[:, 0], z[:, 1]
    energy = re * re + im * im
    mean = jnp.sum(jnp.sum(energy, axis=0), axis=0, keepdims=True) * (1.0 / NF)
    factor = lax.rsqrt(energy + WATER_LEVEL * mean[None] + TINY_ENERGY) * live[None]
    out = jnp.concatenate([(re * factor)[:, None], (im * factor)[:, None]], axis=1)
    return out.reshape(FB, 16, lanes).astype(BF16)


def spectra_kernel(blocks_ref, traces_ref, table_ref, mask_ref, *rest):
    thirds, parts, (xbuf, held, select, sems, out_sems) = rest[:3], rest[3:7], rest[7:]
    keep0, keep1, send0, send1 = parts
    count, channels = xbuf.shape[0], xbuf.shape[1]
    turns = sems.shape[0]
    chunk = count // turns
    copies = [
        pltpu.make_async_copy(
            traces_ref.at[pl.ds(i * chunk, chunk)], xbuf.at[pl.ds(i * chunk, chunk)], sems.at[i]
        )
        for i in range(turns)
    ]
    for copy in copies:
        copy.start()
    chan = lax.axis_index("chan")
    core = chan & 1
    per_device = channels // VSB
    col = iota((1, 256), 1)
    col_block = (col >> 7) * NSRC + ((col & 31) >> 3)
    want = jnp.full((1, 256), -1, jnp.int32)
    for b in range(STEPS * NSRC):
        block = blocks_ref[b // NSRC, b % NSRC]
        holder = block // per_device
        first = jnp.where(holder == chan, (block - holder * per_device) * VSB, -1000)
        want = jnp.where(col_block == b, first + (col & 7), want)
    row = iota((channels, 256), 0)
    for hi in range(4):
        wanted = jnp.where(((col >> 5) & 3) == hi, want, -1)
        select[hi * channels : (hi + 1) * channels, :] = (row == wanted).astype(F32).astype(BF16)
    live = mask_ref[...].astype(F32)[None]
    writes = []
    for i in range(turns):
        copies[i].wait()
        for n in range(i * chunk, (i + 1) * chunk):
            w = whiten_rows(dot(table_ref[...], xbuf[n], ((1,), (1,))), live)
            for third in range(3):
                held[third, :, n * 16 : (n + 1) * 16, :] = w[:, :, third * 128 : (third + 1) * 128]
        if i % 2 == 1:
            at = pl.ds((i - 1) * chunk * 16, 2 * chunk * 16)
            for third in range(3):
                write = pltpu.make_async_copy(
                    held.at[third, :, at], thirds[third].at[:, at], out_sems.at[i // 2, third]
                )
                write.start()
                writes.append(write)
    for half, pair in ((core, (keep0, keep1)), (1 - core, (send0, send1))):
        for t in range(2):
            low = half * 2 + t
            left = [held[third, hi * 4 + low] for hi in range(4) for third in range(3)]
            out = dot(jnp.concatenate(left, axis=1), select[...]).astype(BF16)
            pair[0][t * 256 : (t + 1) * 256, :] = out[:, :128]
            pair[1][t * 256 : (t + 1) * 256, :] = out[:, 128:]
    for write in writes:
        write.wait()


def spectra(traces, mask, blocks, table):
    count, channels, length = traces.shape
    vmem, hbm = pl.BlockSpec(memory_space=pltpu.VMEM), pl.BlockSpec(memory_space=pl.ANY)
    third = jax.ShapeDtypeStruct((FB, count * 16, channels // 3), BF16)
    shape = jax.ShapeDtypeStruct((512, 128), BF16)
    return pl.pallas_call(
        spectra_kernel,
        out_shape=[third] * 3 + [shape] * 4,
        in_specs=[pl.BlockSpec(memory_space=pltpu.SMEM), hbm, vmem, vmem],
        out_specs=[hbm] * 3 + [vmem] * 4,
        scratch_shapes=[
            pltpu.VMEM(traces.shape, BF16),
            pltpu.VMEM((3,) + third.shape, BF16),
            pltpu.VMEM((4 * channels, 256), BF16),
            pltpu.SemaphoreType.DMA((8,)),
            pltpu.SemaphoreType.DMA((4, 3)),
        ],
        compiler_params=pltpu.CompilerParams(vmem_limit_bytes=60 * MB),
        cost_estimate=pl.CostEstimate(flops=10**9, bytes_accessed=10**7, transcendentals=0),
        name="spectra",
    )(blocks, traces, table, mask)


def swap_parts(x):
    y = x.astype(F32).reshape(16, 2, 8, x.shape[-1])
    y = jnp.concatenate([-y[:, 1:2], y[:, 0:1]], axis=1)
    return y.reshape(256, x.shape[-1]).astype(BF16)


def pick_kernel(pick, pick_sent):
    win = lax.axis_index("win")
    my_y, my_x = win >> 2, win & 3
    for g, (ey, ex) in enumerate(PLACES):
        row, col = iota((64, 256), 0), iota((64, 256), 1)
        source = ((((my_y ^ ey) * 4) + (my_x ^ ex)) << 2) + (row >> 4)
        key = (((row >> 3) & 1) << 7) + source
        for hi in range(4):
            pick[hi, g * 64 : (g + 1) * 64, :] = (col == key + hi * 32).astype(F32).astype(BF16)
    row, col = iota((256, 256), 0), iota((256, 256), 1)
    key = (((row >> 3) & 1) << 7) + (row >> 4)
    for t in range(2):
        for hi in range(4):
            at = t * 4 + hi
            pick_sent[at] = (col == key + at * 16).astype(F32).astype(BF16)


def pick_rows():
    vmem = pl.BlockSpec(memory_space=pltpu.VMEM)
    shapes = (4, 64 * len(PLACES), 256), (8, 256, 256)
    return pl.pallas_call(
        pick_kernel,
        out_shape=[jax.ShapeDtypeStruct(shape, BF16) for shape in shapes],
        out_specs=[vmem] * 2,
        cost_estimate=pl.CostEstimate(flops=10**6, bytes_accessed=10**6, transcendentals=0),
        name="pick_rows",
    )()


def narrow_kernel(*refs):
    ins, outs = refs[:STEPS], refs[STEPS:]
    win = lax.axis_index("win")
    my_y, my_x = win >> 2, win & 3
    row, col = iota((256, 128), 0), iota((1, 128), 1)
    for third, out in enumerate(outs):
        want = jnp.zeros((1, 128), jnp.int32)
        for p, (ey, ex) in enumerate(KEPT[third]):
            at_y, at_x = my_y ^ PAIRS[third][0] ^ ey, my_x ^ PAIRS[third][1] ^ ex
            want = jnp.where(((col >> 2) & 3) == p, (at_y * 4 + at_x) * 4, want)
        select = (row == want + (col & 3) + (col >> 4) * 32).astype(F32).astype(BF16)
        for s, x in enumerate(ins):
            x = jnp.concatenate([x[:256, :], x[256:, :]], axis=1)
            out[s * 256 : (s + 1) * 256, :] = dot(x, select).astype(BF16)


def narrow(parts):
    vmem = pl.BlockSpec(memory_space=pltpu.VMEM)
    return pl.pallas_call(
        narrow_kernel,
        out_shape=[jax.ShapeDtypeStruct((256 * STEPS, 128), BF16)] * 3,
        in_specs=[vmem] * STEPS,
        out_specs=[vmem] * 3,
        compiler_params=pltpu.CompilerParams(vmem_limit_bytes=16 * MB),
        cost_estimate=pl.CostEstimate(flops=10**6, bytes_accessed=10**6, transcendentals=0),
        name="narrow",
    )(*parts)


def spread(rows, right):
    diagonal = ((iota((16, 256), 0) & 7) == (iota((16, 256), 1) & 7)).astype(F32).astype(BF16)
    left = dot(rows, right, ((1,), (1,))).astype(BF16)
    return (left.reshape(-1, 16, 256) * diagonal[None]).reshape(left.shape)


def some(x, third):
    at = [PLACES.index(place) * 64 for place in KEPT[third]]
    return jnp.concatenate([x[i : i + 64] for i in at], axis=0)


def both_parts(both, who, ref, half, steps):
    for place, s in enumerate(steps):
        for t in range(2):
            at = s * 512 + t * 256
            x = ref[at : at + 256, :]
            both[place, who, half * 2 + t] = jnp.concatenate([x, swap_parts(x)], axis=1)


def own_kernel(steps, pick, a, b, *rest):
    sources, outs, both = rest[:3], rest[3:6], rest[6]
    core = lax.axis_index("chan") & 1
    for half, ref in enumerate((a, b)):
        both_parts(both, 0, ref, half, range(steps))
    for hi in range(4):
        for lo in range(4):
            block = hi * 4 + (((lo >> 1) ^ core) << 1) + (lo & 1)
            own = [spread(pick[hi], both[s, 0, lo]) for s in range(steps)]
            for third in range(3):
                left = jnp.concatenate([some(x, third) for x in own], axis=0)
                out = dot(left, sources[third][block]).astype(BF16)
                outs[third][:, :, block] = out.reshape(steps, 16, 16, 128)


def correlate_own(pick, senders, receivers):
    steps = senders[0].shape[0] // 512
    vmem = pl.BlockSpec(memory_space=pltpu.VMEM)
    shape = (steps, 16, FB, 16, 128)
    return pl.pallas_call(
        functools.partial(own_kernel, steps),
        out_shape=[jax.ShapeDtypeStruct(shape, BF16)] * 3,
        in_specs=[vmem] * 6,
        out_specs=[vmem] * 3,
        scratch_shapes=[pltpu.VMEM((steps, 1, 4, 256, 256), BF16)],
        compiler_params=pltpu.CompilerParams(vmem_limit_bytes=24 * MB),
        cost_estimate=pl.CostEstimate(flops=10**6, bytes_accessed=10**6, transcendentals=0),
        name="correlate_own",
    )(pick, *senders, *receivers)


def correlate_kernel(thirds, steps, parts, pick, lag_ref, *rest):
    nt = len(thirds)
    senders, partners, sums = rest[: 2 * nt], rest[2 * nt : 3 * nt], rest[3 * nt : 4 * nt]
    outs, (both, stacked) = rest[4 * nt : 4 * nt + len(parts)], rest[4 * nt + len(parts) :]
    core = lax.axis_index("chan") & 1
    for who in range(nt):
        for half in range(2):
            for place, s in enumerate(steps):
                x = senders[who * 2 + half][s * 256 : (s + 1) * 256, :]
                both[place, who, half] = jnp.concatenate([x, swap_parts(x)], axis=1)
    for hi in range(4):
        for lo in range(4):
            rows = pick[(lo & 1) * 4 + hi]
            block = hi * 4 + (((lo >> 1) ^ core) << 1) + (lo & 1)
            for i, third in enumerate(thirds):
                left = [spread(rows, both[s, i, lo >> 1]) for s in range(len(steps))]
                out = dot(jnp.concatenate(left, axis=0), partners[i][block]).astype(BF16)
                stacked[i, :, :, block] = out.reshape(len(steps), 16, 16, 128)
    lag = jnp.concatenate([lag_ref[...], lag_ref[...]], axis=1)
    for part, out in zip(parts, outs):
        wanted = [
            (s, thirds.index(third), KEPT[third].index(where) * 4 + first + r)
            for s in range(len(steps))
            for third, where, first, amount in part
            for r in range(amount)
        ]
        for k in range(0, len(wanted), 2):
            x = [
                jnp.concatenate(
                    [sums[i][steps[s], row].reshape(256, 128), stacked[i, s, row].reshape(256, 128)]
                )
                for s, i, row in wanted[k : k + 2]
            ]
            y = dot(lag, jnp.concatenate(x, axis=1)).astype(BF16)
            for j in range(len(x)):
                out[k + j] = y[:, j * 128 : (j + 1) * 128]


def correlate(thirds, parts, steps, pick, lags, senders, partners, sums):
    nt, count = len(thirds), len(steps)
    vmem = pl.BlockSpec(memory_space=pltpu.VMEM)
    sizes = [sum(piece[3] for piece in part) * count for part in parts]
    ins = [pick, lags, *senders, *partners, *sums]
    return pl.pallas_call(
        functools.partial(correlate_kernel, thirds, steps, parts),
        out_shape=[jax.ShapeDtypeStruct((n, NLAG, 128), BF16) for n in sizes],
        in_specs=[vmem] * len(ins),
        out_specs=[vmem] * len(sizes),
        scratch_shapes=[
            pltpu.VMEM((count, nt, 2, 256, 256), BF16),
            pltpu.VMEM((nt, count) + sums[0].shape[1:], BF16),
        ],
        compiler_params=pltpu.CompilerParams(vmem_limit_bytes=24 * MB),
        cost_estimate=pl.CostEstimate(flops=10**6, bytes_accessed=10**6, transcendentals=0),
        name="correlate",
    )(*ins)


def by_step(refs):
    for s in range(STEPS):
        rows = [ref.shape[0] // STEPS for ref in refs]
        yield [ref.at[pl.ds(s * n, n)] for ref, n in zip(refs, rows)]


def finish_kernel(*refs):
    ins, out = refs[:-1], refs[-1]
    half = pl.program_id(0)

    def total(*xs):
        first = xs[0].astype(F32)
        for x in xs[1:]:
            first = first + x.astype(F32)
        return first.T

    for s, (k1, k2, y1, xa1, xb1, g0, y2, xa2, xb2, ma, mb) in enumerate(by_step(ins)):
        for h in range(2):

            @pl.when(half == h)
            def _():
                for j in range(2):
                    r = 2 * h + j
                    one, two = (y1[0], mb[0]) if r == 0 else (xb1[r - 1], y2[r - 1])
                    three, four = (y1[2], ma[0]) if r == 0 else (xa1[r - 1], y2[2 + r])
                    out[j, s, :128, :] = total(g0[r], xa2[r], xb2[r])
                    out[j, s, 128:256, :] = total(k1[r], one, two)
                    out[j, s, 256:, :] = total(k2[r], three, four)


def finish(ins, channels):
    def whole(x):
        return pl.BlockSpec(x.shape, lambda h: (0, 0, 0))

    return pl.pallas_call(
        finish_kernel,
        grid=(2,),
        out_shape=jax.ShapeDtypeStruct((4, STEPS, channels, NLAG), F32),
        in_specs=[whole(x) for x in ins],
        out_specs=pl.BlockSpec((2, STEPS, channels, NLAG), lambda h: (h, 0, 0, 0)),
        compiler_params=pltpu.CompilerParams(vmem_limit_bytes=16 * MB),
        name="finish",
    )(*ins)


def add(x, y):
    return (x.astype(F32) + y.astype(F32)).astype(BF16)


def merge_once_kernel(*refs):
    for k13, k21, y, ma, mb in by_step(refs):
        ma[0] = add(k21[0], y[3])
        mb[0] = add(k13[0], y[1])


def merge_thirds_kernel(*refs):
    for k10, k20, xa, xb, y2 in by_step(refs):
        for r in range(3):
            y2[r] = add(k10[r], xb[3 + r])
            y2[3 + r] = add(k20[r], xa[3 + r])


def merge_ring_kernel(*refs):
    for g1, g3, ua, ub, xa2, xb2 in by_step(refs):
        for r in range(2):
            xa2[r] = g1[r]
            xa2[2 + r] = add(g1[2 + r], ub[r])
            xb2[r] = add(g3[r], ua[r])
            xb2[2 + r] = g3[2 + r]


def merge(kernel, ins, sizes):
    vmem = pl.BlockSpec(memory_space=pltpu.VMEM)
    return pl.pallas_call(
        kernel,
        out_shape=[jax.ShapeDtypeStruct((n * STEPS,) + ins[0].shape[1:], BF16) for n in sizes],
        in_specs=[vmem] * len(ins),
        out_specs=[vmem] * len(sizes),
        compiler_params=pltpu.CompilerParams(vmem_limit_bytes=16 * MB),
        name="merge",
    )(*ins)


def on_device(traces, channel_mask, source_blocks):
    windows, segments, channels, length = traces.shape
    traces = traces.reshape(windows * segments, channels, length)
    table = jnp.asarray(dft_rows(length))
    scale = 1.0 / (windows * lax.axis_size("win") * segments)
    lags = jnp.asarray(lag_rows(length, scale))

    def chan_swap(x, bits):
        return lax.ppermute(x, "chan", [(i, i ^ bits) for i in range(16)])

    def win_swap(x, pair):
        bits = pair[0] * 4 + pair[1]
        return lax.ppermute(x, "win", [(i, i ^ bits) for i in range(8)])

    r0, r1, r2, keep0, keep1, send0, send1 = spectra(traces, channel_mask, source_blocks, table)
    p1, p2 = win_swap(r1, PAIRS[1]), win_swap(r2, PAIRS[2])
    part0, part1 = keep0 + chan_swap(send0, 1), keep1 + chan_swap(send1, 1)
    pick, pick_sent = pick_rows()
    for one, other in ((8, 2), (2, 8), (6, 6)):
        part0, part1 = part0 + chan_swap(part0, one), part1 + chan_swap(part1, other)
        if other == 8:
            part0, part1, r0, pick, pick_sent = lax.optimization_barrier(
                (part0, part1, r0, pick, pick_sent)
            )
            p0 = win_swap(r0, PAIRS[0])
    part0, part1, p1, p2 = lax.optimization_barrier((part0, part1, p1, p2))
    part = jnp.concatenate([part0, part1])
    to_y, to_a, to_b = narrow([part0, part1])
    from_a, from_b = win_swap(to_a, PAIRS[1]), win_swap(to_b, PAIRS[2])
    from_y = win_swap(to_y, PAIRS[0])
    s0, s1, s2 = correlate_own(pick, (part, chan_swap(part, 1)), (r0, r1, r2))
    from_a, from_b, s0, s1, s2 = lax.optimization_barrier((from_a, from_b, s0, s1, s2))
    senders = [x for half in (from_a, from_b) for x in (half, chan_swap(half, 1))]
    y, xa, xb, k1, k13, k10, k2, k21, k20 = correlate(
        (1, 2), PARTS_12, (0, 1), pick_sent, lags, senders, (p1, p2), (s1, s2)
    )
    from_y, p0, y, xa, xb = lax.optimization_barrier((from_y, p0, y, xa, xb))
    y1, xa1, xb1 = win_swap(y, (1, 0)), win_swap(xa, (0, 1)), win_swap(xb, (0, 3))
    senders = [from_y, chan_swap(from_y, 1)]
    ua, ub, g0, g1, g3 = correlate((0,), PARTS_0, (0, 1), pick_sent, lags, senders, (p0,), (s0,))
    ua, ub = win_swap(ua, (0, 1)), win_swap(ub, (0, 3))
    ma, mb = merge(merge_once_kernel, [k13, k21, y1], [1, 1])
    xa1, xb1, ma, mb = lax.optimization_barrier((xa1, xb1, ma, mb))
    (y2,) = merge(merge_thirds_kernel, [k10, k20, xa1, xb1], [6])
    y2 = win_swap(y2, (1, 0))
    ma, mb = win_swap(ma, (0, 1)), win_swap(mb, (0, 3))
    xa2, xb2 = merge(merge_ring_kernel, [g1, g3, ua, ub], [4, 4])
    xa2, xb2 = win_swap(xa2, (0, 1)), win_swap(xb2, (0, 3))
    return finish([k1, k2, y1, xa1, xb1, g0, y2, xa2, xb2, ma, mb], channels)


def solution(mesh):
    in_specs = (P("win", None, "chan", None), P("chan"), P())
    out_specs = P("win", None, "chan", None)
    return jax.shard_map(
        on_device, mesh=mesh, in_specs=in_specs, out_specs=out_specs, check_vma=False
    )
```

time: 93.7 us -> 85.5 us (0.912)
  Pallas kernels: 36.3 us -> 26.6 us
  starting transfers between devices: 28.1 us -> 33.8 us
  waiting for transfers between devices: 25.7 us -> 20.5 us
  local copies, waits for them, and re-layouts: 0.05 us -> 1.22 us
    pallas_call x2, Pallas kernels: 17.2 us -> 9.27 us  [correlate(): pl.pallas_call(functools.partial(correlate_kernel, thirds, steps, parts),...]
    ppermute x14 -> x16, starting transfers between devices: 16.1 us -> 20.1 us  [win_swap(): return lax.ppermute(x, 'win', [(i, i ^ bits) for i in range(8)])]
    ppermute x14 -> x16, waiting for transfers between devices: 12.9 us -> 9.73 us  [win_swap(): return lax.ppermute(x, 'win', [(i, i ^ bits) for i in range(8)])]
    pallas_call x1, Pallas kernels: 7.87 us -> 5.49 us  [correlate_own(): pl.pallas_call(functools.partial(own_kernel, steps), out_shape=[jax.Shape...]
    ppermute x12, waiting for transfers between devices: 12.8 us -> 10.8 us  [chan_swap(): return lax.ppermute(x, 'chan', [(i, i ^ bits) for i in range(16)])]
    ppermute x12, starting transfers between devices: 12 us -> 13.7 us  [chan_swap(): return lax.ppermute(x, 'chan', [(i, i ^ bits) for i in range(16)])]
    unnamed x11 -> x13, local copies, waits for them, and re-layouts: 0.03 us -> 1.2 us
    pallas_call x2 -> x3, Pallas kernels: 9.45 us -> 10 us  [the longest x1 8.19 us: spectra(): pl.pallas_call(spectra_kernel, out_shape=[third] * 3 + [shape] * 4, in_sp...]
  transfers between devices with their start and end apart: 26 -> 28, of which waited for: 15 -> 13; matrix products, arithmetic and copies ran while one was open for 3% -> 4% of each run, Pallas kernels for 28% -> 20%
where the time goes in v5:
time: 85.5 us; the launch traced here: 85.3 us
  starting transfers between devices  33.8 us (40%)
  Pallas kernels  26.6 us (31%)
  waiting for transfers between devices  20.5 us (24%)
  other arithmetic  3.02 us (4%)
  local copies, waits for them, and re-layouts  1.22 us (1%)
    ppermute x16, starting transfers between devices, win_swap(): return lax.ppermute(x, 'win', [(i, i ^ bits) for i in range(8)])  20.1 us
    ppermute x12, starting transfers between devices, chan_swap(): return lax.ppermute(x, 'chan', [(i, i ^ bits) for i in range(16)])  13.7 us
    ppermute x12, waiting for transfers between devices, chan_swap(): return lax.ppermute(x, 'chan', [(i, i ^ bits) for i in range(16)])  10.8 us
    ppermute x16, waiting for transfers between devices, win_swap(): return lax.ppermute(x, 'win', [(i, i ^ bits) for i in range(8)])  9.73 us
    pallas_call x2, Pallas kernels, correlate(): pl.pallas_call(functools.partial(correlate_kernel, thirds, steps, parts),...  9.27 us
    pallas_call x1, Pallas kernels, spectra(): pl.pallas_call(spectra_kernel, out_shape=[third] * 3 + [shape] * 4, in_sp...  8.19 us
    pallas_call x1, Pallas kernels, correlate_own(): pl.pallas_call(functools.partial(own_kernel, steps), out_shape=[jax.Shape...  5.49 us
    add x2, other arithmetic, on_device(): part0, part1 = (keep0 + chan_swap(send0, 1), keep1 + chan_swap(send1, 1))  1.89 us
  transfers between devices with their start and end apart: 28, of which 13 were waited for; matrix products, arithmetic and copies ran while one was open for 4% of the time, Pallas kernels for 20%

profile of v5, /device:TPU:0, one launch (start us, length us, event | category | flops | bytes accessed | tf_op | source)
XLA Modules:
  0.0 85.3 jit_solution(7750653740790015099)
XLA Ops:
  0.0 8.2 %spectra.1 = (bf16[16,256,128]{2,1,0:T(8,128)(2,1)}, bf16[16,256,128]{2,1,0:T(8,128)(2,1)}, bf16[16,256,128]{2,1,0:T(8,128)(2,1)}, bf16[512,128]{1,0:T(8,128)(2,...) custom-call(s32[2,4]{1,0:T(2,128)} %blocks_ref.1, ...), custom_call_target="tpu_custom_call" | custom-call | flops 1000000000 | bytes 10000000 | tf_op jit(solution)/shard_map/spectra/pallas_call | solution.py:153
  8.2 1.7 %collective-permute-start.8 = (bf16[16,256,128]{2,1,0:T(8,128)(2,1)}, bf16[16,256,128]{2,1,0:T(8,128)(2,1)S(1)}, u32[]{:S(2)}, u32[]{:S(2)}) collective-permute-start(bf16[16,256,128]{2,1,0:T(8,128)(2,1)} %get-tuple-element.71.rest_1_), channel_id=1, source_target_pairs={{0,1},{1,0},{2,3},{3,2},{4,5},{5,4},{6,7},{7,6},{8,9},{9,8},{10,11... | collective-permute-start | bytes 3145736 | tf_op jit(solution)/shard_map/ppermute | solution.py:438
  9.9 2.1 %collective-permute-start.9 = (bf16[16,256,128]{2,1,0:T(8,128)(2,1)}, bf16[16,256,128]{2,1,0:T(8,128)(2,1)S(1)}, u32[]{:S(2)}, u32[]{:S(2)}) collective-permute-start(bf16[16,256,128]{2,1,0:T(8,128)(2,1)} %get-tuple-element.72.rest_2_), channel_id=1, source_target_pairs={{0,3},{1,2},{2,1},{3,0},{4,7},{5,6},{6,5},{7,4},{8,11},{9,10},{10,... | collective-permute-start | bytes 3145736 | tf_op jit(solution)/shard_map/ppermute | solution.py:438
  14.5 2.0 %collective-permute-start.4 = (bf16[512,128]{1,0:T(8,128)(2,1)S(1)}, bf16[512,128]{1,0:T(8,128)(2,1)S(1)}, u32[]{:S(2)}, u32[]{:S(2)}) collective-permute-start(bf16[512,128]{1,0:T(8,128)(2,1)S(1)} %add.27), channel_id=1, source_target_pairs={{0,16},{8,24},{16,0},{24,8},{32,48},{40,56},{48,32},{56,40},{64,80... | collective-permute-start | bytes 393224 | tf_op jit(solution)/shard_map/ppermute | solution.py:434
  17.4 3.3 %collective-permute-start.1 = (bf16[512,128]{1,0:T(8,128)(2,1)S(1)}, bf16[512,128]{1,0:T(8,128)(2,1)S(1)}, u32[]{:S(2)}, u32[]{:S(2)}) collective-permute-start(bf16[512,128]{1,0:T(8,128)(2,1)S(1)} %add.24), channel_id=1, source_target_pairs={{0,64},{8,72},{16,80},{24,88},{32,96},{40,104},{48,112},{56,120},{... | collective-permute-start | bytes 393224 | tf_op jit(solution)/shard_map/ppermute | solution.py:434
  20.7 2.9 %collective-permute-start.5 = (bf16[512,128]{1,0:T(8,128)(2,1)S(1)}, bf16[512,128]{1,0:T(8,128)(2,1)S(1)}, u32[]{:S(2)}, u32[]{:S(2)}) collective-permute-start(bf16[512,128]{1,0:T(8,128)(2,1)S(1)} %add.28), channel_id=1, source_target_pairs={{0,64},{8,72},{16,80},{24,88},{32,96},{40,104},{48,112},{56,120},{... | collective-permute-start | bytes 393224 | tf_op jit(solution)/shard_map/ppermute | solution.py:434
  25.5 1.5 %pick_rows.1 = (bf16[4,448,256]{2,1,0:T(8,128)(2,1)}, bf16[8,256,256]{2,1,0:T(8,128)(2,1)}) custom-call(), custom_call_target="tpu_custom_call" | custom-call | flops 1000000 | bytes 1000000 | tf_op jit(solution)/shard_map/pick_rows/pallas_call | solution.py:197
  27.4 2.1 %collective-permute-done.2 = bf16[512,128]{1,0:T(8,128)(2,1)} collective-permute-done((bf16[512,128]{1,0:T(8,128)(2,1)S(1)}, bf16[512,128]{1,0:T(8,128)(2,1)}, u32[]{:S(2)}, u32[]{:S(2)}) %collective-permute-start.2) | collective-permute-done | bytes 131104 | tf_op jit(solution)/shard_map/ppermute | solution.py:434
  30.4 1.9 %collective-permute-start.16 = (bf16[16,256,128]{2,1,0:T(8,128)(2,1)S(1)}, bf16[16,256,128]{2,1,0:T(8,128)(2,1)S(1)}, u32[]{:S(2)}, u32[]{:S(2)}) collective-permute-start(bf16[16,256,128]{2,1,0:T(8,128)(2,1)S(1)} %copy-done.1), channel_id=1, source_target_pairs={{0,4},{1,5},{2,6},{3,7},{4,0},{5,1},{6,2},{7,3},{8,12},{9,13},{10,... | collective-permute-start | bytes 3145736 | tf_op jit(solution)/shard_map/ppermute | solution.py:438
  32.3 2.3 %collective-permute-start.7 = (bf16[512,128]{1,0:T(8,128)(2,1)S(1)}, bf16[512,128]{1,0:T(8,128)(2,1)S(1)}, u32[]{:S(2)}, u32[]{:S(2)}) collective-permute-start(bf16[512,128]{1,0:T(8,128)(2,1)S(1)} %add.29), channel_id=1, source_target_pairs={{0,48},{8,56},{16,32},{24,40},{32,16},{40,24},{48,0},{56,8},{64,11... | collective-permute-start | bytes 393224 | tf_op jit(solution)/shard_map/ppermute | solution.py:434
  35.5 3.2 %collective-permute-done.7 = bf16[512,128]{1,0:T(8,128)(2,1)S(1)} collective-permute-done((bf16[512,128]{1,0:T(8,128)(2,1)S(1)}, bf16[512,128]{1,0:T(8,128)(2,1)S(1)}, u32[]{:S(2)}, u32[]{:S(2)}) %collective-permute-start.7) | collective-permute-done | bytes 131104 | tf_op jit(solution)/shard_map/ppermute | solution.py:434
  38.7 2.0 %collective-permute-done.6 = bf16[512,128]{1,0:T(8,128)(2,1)S(1)} collective-permute-done((bf16[512,128]{1,0:T(8,128)(2,1)S(1)}, bf16[512,128]{1,0:T(8,128)(2,1)S(1)}, u32[]{:S(2)}, u32[]{:S(2)}) %collective-permute-start.6) | collective-permute-done | bytes 131104 | tf_op jit(solution)/shard_map/ppermute | solution.py:434
  44.1 5.5 %correlate_own.1 = (bf16[2,16,16,16,128]{4,3,2,1,0:T(8,128)(2,1)S(1)}, bf16[2,16,16,16,128]{4,3,2,1,0:T(8,128)(2,1)S(1)}, bf16[2,16,16,16,128]{4,3,2,1,0:T(8,128)(2,1)S(1)}) custom-call(bf16[4,448,256]{2,1,0:T(8,128)(2,1)S(1)} %copy-done.4, bf16[1024,128]{1,0:T(8,128)(2,1)S(1)} %constant_dynamic-update-slice_fusion.a, ...), custom_call_target="tpu_custom_call" | custom-call | flops 1000000 | bytes 1000000 | tf_op jit(solution)/shard_map/correlate_own/pallas_call | solution.py:273
  51.3 6.0 %correlate.2 = (bf16[8,128,128]{2,1,0:T(8,128)(2,1)S(1)}, bf16[12,128,128]{2,1,0:T(8,128)(2,1)S(1)}, bf16[12,128,128]{2,1,0:T(8,128)(2,1)S(1)}, bf16[8,128,128]{...) custom-call(bf16[8,256,256]{2,1,0:T(8,128)(2,1)S(1)} %copy-done, ...), custom_call_target="tpu_custom_call" | custom-call | flops 1000000 | bytes 1000000 | tf_op jit(solution)/shard_map/correlate/pallas_call | solution.py:328
  58.5 2.1 %collective-permute-start.19 = (bf16[12,128,128]{2,1,0:T(8,128)(2,1)S(1)}, bf16[12,128,128]{2,1,0:T(8,128)(2,1)S(1)}, u32[]{:S(2)}, u32[]{:S(2)}) collective-permute-start(bf16[12,128,128]{2,1,0:T(8,128)(2,1)S(1)} %get-tuple-element.96), channel_id=1, source_target_pairs={{0,3},{1,2},{2,1},{3,0},{4,7},{5,6},{6,5},{7,4},{8,11},{9,10},{10,... | collective-permute-start | bytes 1179656 | tf_op jit(solution)/shard_map/ppermute | solution.py:438
  61.6 1.3 %collective-permute-done.20.rest_1_ = bf16[512,128]{1,0:T(8,128)(2,1)S(1)} collective-permute-done((bf16[512,128]{1,0:T(8,128)(2,1)S(1)}, bf16[512,128]{1,0:T(8,128)(2,1)S(1)}, u32[]{:S(2)}, u32[]{:S(2)}) %collective-permute-start.20) | collective-permute-done | bytes 131104 | tf_op jit(solution)/shard_map/ppermute | solution.py:434
  63.0 3.3 %correlate.3 = (bf16[4,128,128]{2,1,0:T(8,128)(2,1)S(1)}, bf16[4,128,128]{2,1,0:T(8,128)(2,1)S(1)}, bf16[8,128,128]{2,1,0:T(8,128)(2,1)S(1)}, bf16[8,128,128]{2,1,0:T(8,128)(2,1)S(1)}, bf16[8,128,128]{2,1,0:T(8,128)(2,1)S(1)}) custom-call(bf16[8,256,256]{2,1,0:T(8,128)(2,1)S(1)} %copy-done, bf16[128,256]{1,0:T(8,128)(2,1)S(1)} %copy-done.5, ...), custom_call_target="tpu_custom_call" | custom-call | flops 1000000 | bytes 1000000 | tf_op jit(solution)/shard_map/correlate/pallas_call | solution.py:328
  68.6 2.1 %collective-permute-done.19.refs_3_.refs_4_ = bf16[12,128,128]{2,1,0:T(8,128)(2,1)S(1)} collective-permute-done((bf16[12,128,128]{2,1,0:T(8,128)(2,1)S(1)}, bf16[12,128,128]{2,1,0:T(8,128)(2,1)S(1)}, u32[]{:S(2)}, u32[]{:S(2)}) %collective-permute-start.19) | collective-permute-done | bytes 393248 | tf_op jit(solution)/shard_map/ppermute | solution.py:438
  72.1 1.4 %collective-permute-done.23.refs_3_ = bf16[4,128,128]{2,1,0:T(8,128)(2,1)S(1)} collective-permute-done((bf16[4,128,128]{2,1,0:T(8,128)(2,1)S(1)}, bf16[4,128,128]{2,1,0:T(8,128)(2,1)S(1)}, u32[]{:S(2)}, u32[]{:S(2)}) %collective-permute-start.23) | collective-permute-done | bytes 131104 | tf_op jit(solution)/shard_map/ppermute | solution.py:438
  73.8 2.1 %collective-permute-start.25 = (bf16[8,128,128]{2,1,0:T(8,128)(2,1)S(1)}, bf16[8,128,128]{2,1,0:T(8,128)(2,1)S(1)}, u32[]{:S(2)}, u32[]{:S(2)}) collective-permute-start(bf16[8,128,128]{2,1,0:T(8,128)(2,1)S(1)} %get-tuple-element.114), channel_id=1, source_target_pairs={{0,3},{1,2},{2,1},{3,0},{4,7},{5,6},{6,5},{7,4},{8,11},{9,10},{10,... | collective-permute-start | bytes 786440 | tf_op jit(solution)/shard_map/ppermute | solution.py:438
  75.8 1.3 %collective-permute-start.26 = (bf16[2,128,128]{2,1,0:T(8,128)(2,1)S(1)}, bf16[2,128,128]{2,1,0:T(8,128)(2,1)S(1)}, u32[]{:S(2)}, u32[]{:S(2)}) collective-permute-start(bf16[2,128,128]{2,1,0:T(8,128)(2,1)S(1)} %get-tuple-element.115), channel_id=1, source_target_pairs={{0,1},{1,0},{2,3},{3,2},{4,5},{5,4},{6,7},{7,6},{8,9},{9,8},{10,11... | collective-permute-start | bytes 196616 | tf_op jit(solution)/shard_map/ppermute | solution.py:438
  78.3 4.1 %collective-permute-done.26.refs_9_ = bf16[2,128,128]{2,1,0:T(8,128)(2,1)S(1)} collective-permute-done((bf16[2,128,128]{2,1,0:T(8,128)(2,1)S(1)}, bf16[2,128,128]{2,1,0:T(8,128)(2,1)S(1)}, u32[]{:S(2)}, u32[]{:S(2)}) %collective-permute-start.26) | collective-permute-done | bytes 65568 | tf_op jit(solution)/shard_map/ppermute | solution.py:438
  82.4 1.3 %collective-permute-done.27.refs_10_ = bf16[2,128,128]{2,1,0:T(8,128)(2,1)S(1)} collective-permute-done((bf16[2,128,128]{2,1,0:T(8,128)(2,1)S(1)}, bf16[2,128,128]{2,1,0:T(8,128)(2,1)S(1)}, u32[]{:S(2)}, u32[]{:S(2)}) %collective-permute-start.27) | collective-permute-done | bytes 65568 | tf_op jit(solution)/shard_map/ppermute | solution.py:438
  83.7 1.6 %finish.1 = f32[4,2,384,128]{3,2,1,0:T(8,128)} custom-call(bf16[8,128,128]{2,1,0:T(8,128)(2,1)S(1)} %get-tuple-element.88.refs_0_, bf16[8,128,128]{2,1,0:T(8,128)(2,1)S(1)} %get-tuple-element.89.refs_1_, bf16[8,128,128]{2,1,0:T(8,128)(2,1)S(1)} %collective-permute-done.17.refs_2_, bf16[12,128,128]{2,1,0:T(8,128)(2,1)S(1)} %collective-permute-done.18.refs_2_.refs_3_, ...), custom_call_target="tpu_custom_call" | custom-call | tf_op jit(solution)/shard_map/finish/pallas_call | solution.py:377
  (64 shorter events, 20.0 us)
Async XLA Ops:
  8.2 32.6 %collective-permute-start.8 = (bf16[16,256,128]{2,1,0:T(8,128)(2,1)}, bf16[16,256,128]{2,1,0:T(8,128)(2,1)S(1)}, u32[]{:S(2)}, u32[]{:S(2)}) collective-permute-start(bf16[16,256,128]{2,1,0:T(8,128)(2,1)} %get-tuple-element.71.rest_1_), channel_id=1, source_target_pairs={{0,1},{1,0},{2,3},{3,2},{4,5},{5,4},{6,7},{7,6},{8,9},{9,8},{10,11... | collective-permute-start | bytes 3145736 | tf_op jit(solution)/shard_map/ppermute | solution.py:438
  9.9 31.0 %collective-permute-start.9 = (bf16[16,256,128]{2,1,0:T(8,128)(2,1)}, bf16[16,256,128]{2,1,0:T(8,128)(2,1)S(1)}, u32[]{:S(2)}, u32[]{:S(2)}) collective-permute-start(bf16[16,256,128]{2,1,0:T(8,128)(2,1)} %get-tuple-element.72.rest_2_), channel_id=1, source_target_pairs={{0,3},{1,2},{2,1},{3,0},{4,7},{5,6},{6,5},{7,4},{8,11},{9,10},{10,... | collective-permute-start | bytes 3145736 | tf_op jit(solution)/shard_map/ppermute | solution.py:438
  12.0 4.5 %collective-permute-start = (bf16[512,128]{1,0:T(8,128)(2,1)}, bf16[512,128]{1,0:T(8,128)(2,1)S(1)}, u32[]{:S(2)}, u32[]{:S(2)}) collective-permute-start(bf16[512,128]{1,0:T(8,128)(2,1)} %get-tuple-element.62), channel_id=1, source_target_pairs={{0,8},{8,0},{16,24},{24,16},{32,40},{40,32},{48,56},{56,48},{64,72... | collective-permute-start | bytes 393224 | tf_op jit(solution)/shard_map/ppermute | solution.py:434
  14.5 6.2 %collective-permute-start.4 = (bf16[512,128]{1,0:T(8,128)(2,1)S(1)}, bf16[512,128]{1,0:T(8,128)(2,1)S(1)}, u32[]{:S(2)}, u32[]{:S(2)}) collective-permute-start(bf16[512,128]{1,0:T(8,128)(2,1)S(1)} %add.27), channel_id=1, source_target_pairs={{0,16},{8,24},{16,0},{24,8},{32,48},{40,56},{48,32},{56,40},{64,80... | collective-permute-start | bytes 393224 | tf_op jit(solution)/shard_map/ppermute | solution.py:434
  17.4 6.9 %collective-permute-start.1 = (bf16[512,128]{1,0:T(8,128)(2,1)S(1)}, bf16[512,128]{1,0:T(8,128)(2,1)S(1)}, u32[]{:S(2)}, u32[]{:S(2)}) collective-permute-start(bf16[512,128]{1,0:T(8,128)(2,1)S(1)} %add.24), channel_id=1, source_target_pairs={{0,64},{8,72},{16,80},{24,88},{32,96},{40,104},{48,112},{56,120},{... | collective-permute-start | bytes 393224 | tf_op jit(solution)/shard_map/ppermute | solution.py:434
  20.7 6.6 %collective-permute-start.5 = (bf16[512,128]{1,0:T(8,128)(2,1)S(1)}, bf16[512,128]{1,0:T(8,128)(2,1)S(1)}, u32[]{:S(2)}, u32[]{:S(2)}) collective-permute-start(bf16[512,128]{1,0:T(8,128)(2,1)S(1)} %add.28), channel_id=1, source_target_pairs={{0,64},{8,72},{16,80},{24,88},{32,96},{40,104},{48,112},{56,120},{... | collective-permute-start | bytes 393224 | tf_op jit(solution)/shard_map/ppermute | solution.py:434
  24.3 5.2 %collective-permute-start.2 = (bf16[512,128]{1,0:T(8,128)(2,1)S(1)}, bf16[512,128]{1,0:T(8,128)(2,1)}, u32[]{:S(2)}, u32[]{:S(2)}) collective-permute-start(bf16[512,128]{1,0:T(8,128)(2,1)S(1)} %add.25), channel_id=1, source_target_pairs={{0,16},{8,24},{16,0},{24,8},{32,48},{40,56},{48,32},{56,40},{64,80... | collective-permute-start | bytes 393224 | tf_op jit(solution)/shard_map/ppermute | solution.py:434
  30.4 26.9 %collective-permute-start.16 = (bf16[16,256,128]{2,1,0:T(8,128)(2,1)S(1)}, bf16[16,256,128]{2,1,0:T(8,128)(2,1)S(1)}, u32[]{:S(2)}, u32[]{:S(2)}) collective-permute-start(bf16[16,256,128]{2,1,0:T(8,128)(2,1)S(1)} %copy-done.1), channel_id=1, source_target_pairs={{0,4},{1,5},{2,6},{3,7},{4,0},{5,1},{6,2},{7,3},{8,12},{9,13},{10,... | collective-permute-start | bytes 3145736 | tf_op jit(solution)/shard_map/ppermute | solution.py:438
  32.3 6.4 %collective-permute-start.7 = (bf16[512,128]{1,0:T(8,128)(2,1)S(1)}, bf16[512,128]{1,0:T(8,128)(2,1)S(1)}, u32[]{:S(2)}, u32[]{:S(2)}) collective-permute-start(bf16[512,128]{1,0:T(8,128)(2,1)S(1)} %add.29), channel_id=1, source_target_pairs={{0,48},{8,56},{16,32},{24,40},{32,16},{40,24},{48,0},{56,8},{64,11... | collective-permute-start | bytes 393224 | tf_op jit(solution)/shard_map/ppermute | solution.py:434
  34.6 6.2 %collective-permute-start.6 = (bf16[512,128]{1,0:T(8,128)(2,1)S(1)}, bf16[512,128]{1,0:T(8,128)(2,1)S(1)}, u32[]{:S(2)}, u32[]{:S(2)}) collective-permute-start(bf16[512,128]{1,0:T(8,128)(2,1)S(1)} %add.26), channel_id=1, source_target_pairs={{0,48},{8,56},{16,32},{24,40},{32,16},{40,24},{48,0},{56,8},{64,11... | collective-permute-start | bytes 393224 | tf_op jit(solution)/shard_map/ppermute | solution.py:434
  40.9 2.0 %collective-permute-start.12 = (bf16[1024,128]{1,0:T(8,128)(2,1)S(1)}, bf16[1024,128]{1,0:T(8,128)(2,1)S(1)}, u32[]{:S(2)}, u32[]{:S(2)}) collective-permute-start(bf16[1024,128]{1,0:T(8,128)(2,1)S(1)} %constant_dynamic-update-slice_fusion.a), channel_id=1, source_target_pairs={{0,8},{8,0},{16,24},{24,16},{32,40},{40,32},{48,56},{56,48},{64,72... | collective-permute-start | bytes 786440 | tf_op jit(solution)/shard_map/ppermute | solution.py:434
  41.4 8.2 %collective-permute-start.10 = (bf16[512,128]{1,0:T(8,128)(2,1)S(1)}, bf16[512,128]{1,0:T(8,128)(2,1)S(1)}, u32[]{:S(2)}, u32[]{:S(2)}) collective-permute-start(bf16[512,128]{1,0:T(8,128)(2,1)S(1)} %get-tuple-element.75), channel_id=1, source_target_pairs={{0,1},{1,0},{2,3},{3,2},{4,5},{5,4},{6,7},{7,6},{8,9},{9,8},{10,11... | collective-permute-start | bytes 393224 | tf_op jit(solution)/shard_map/ppermute | solution.py:438
  42.0 7.5 %collective-permute-start.11 = (bf16[512,128]{1,0:T(8,128)(2,1)S(1)}, bf16[512,128]{1,0:T(8,128)(2,1)S(1)}, u32[]{:S(2)}, u32[]{:S(2)}) collective-permute-start(bf16[512,128]{1,0:T(8,128)(2,1)S(1)} %get-tuple-element.76), channel_id=1, source_target_pairs={{0,3},{1,2},{2,1},{3,0},{4,7},{5,6},{6,5},{7,4},{8,11},{9,10},{10,... | collective-permute-start | bytes 393224 | tf_op jit(solution)/shard_map/ppermute | solution.py:438
  50.2 7.1 %collective-permute-start.15 = (bf16[512,128]{1,0:T(8,128)(2,1)S(1)}, bf16[512,128]{1,0:T(8,128)(2,1)S(1)}, u32[]{:S(2)}, u32[]{:S(2)}) collective-permute-start(bf16[512,128]{1,0:T(8,128)(2,1)S(1)} %get-tuple-element.90), channel_id=1, source_target_pairs={{0,4},{1,5},{2,6},{3,7},{4,0},{5,1},{6,2},{7,3},{8,12},{9,13},{10,... | collective-permute-start | bytes 393224 | tf_op jit(solution)/shard_map/ppermute | solution.py:438
  57.3 11.3 %collective-permute-start.18 = (bf16[12,128,128]{2,1,0:T(8,128)(2,1)S(1)}, bf16[12,128,128]{2,1,0:T(8,128)(2,1)S(1)}, u32[]{:S(2)}, u32[]{:S(2)}) collective-permute-start(bf16[12,128,128]{2,1,0:T(8,128)(2,1)S(1)} %get-tuple-element.95), channel_id=1, source_target_pairs={{0,1},{1,0},{2,3},{3,2},{4,5},{5,4},{6,7},{7,6},{8,9},{9,8},{10,11... | collective-permute-start | bytes 1179656 | tf_op jit(solution)/shard_map/ppermute | solution.py:438
  58.5 12.2 %collective-permute-start.19 = (bf16[12,128,128]{2,1,0:T(8,128)(2,1)S(1)}, bf16[12,128,128]{2,1,0:T(8,128)(2,1)S(1)}, u32[]{:S(2)}, u32[]{:S(2)}) collective-permute-start(bf16[12,128,128]{2,1,0:T(8,128)(2,1)S(1)} %get-tuple-element.96), channel_id=1, source_target_pairs={{0,3},{1,2},{2,1},{3,0},{4,7},{5,6},{6,5},{7,4},{8,11},{9,10},{10,... | collective-permute-start | bytes 1179656 | tf_op jit(solution)/shard_map/ppermute | solution.py:438
  60.6 7.9 %collective-permute-start.17 = (bf16[8,128,128]{2,1,0:T(8,128)(2,1)S(1)}, bf16[8,128,128]{2,1,0:T(8,128)(2,1)S(1)}, u32[]{:S(2)}, u32[]{:S(2)}) collective-permute-start(bf16[8,128,128]{2,1,0:T(8,128)(2,1)S(1)} %get-tuple-element.94), channel_id=1, source_target_pairs={{0,4},{1,5},{2,6},{3,7},{4,0},{5,1},{6,2},{7,3},{8,12},{9,13},{10,... | collective-permute-start | bytes 786440 | tf_op jit(solution)/shard_map/ppermute | solution.py:438
  66.3 5.8 %collective-permute-start.22 = (bf16[4,128,128]{2,1,0:T(8,128)(2,1)S(1)}, bf16[4,128,128]{2,1,0:T(8,128)(2,1)S(1)}, u32[]{:S(2)}, u32[]{:S(2)}) collective-permute-start(bf16[4,128,128]{2,1,0:T(8,128)(2,1)S(1)} %get-tuple-element.111), channel_id=1, source_target_pairs={{0,1},{1,0},{2,3},{3,2},{4,5},{5,4},{6,7},{7,6},{8,9},{9,8},{10,11... | collective-permute-start | bytes 393224 | tf_op jit(solution)/shard_map/ppermute | solution.py:438
  66.9 6.6 %collective-permute-start.23 = (bf16[4,128,128]{2,1,0:T(8,128)(2,1)S(1)}, bf16[4,128,128]{2,1,0:T(8,128)(2,1)S(1)}, u32[]{:S(2)}, u32[]{:S(2)}) collective-permute-start(bf16[4,128,128]{2,1,0:T(8,128)(2,1)S(1)} %get-tuple-element.112), channel_id=1, source_target_pairs={{0,3},{1,2},{2,1},{3,0},{4,7},{5,6},{6,5},{7,4},{8,11},{9,10},{10,... | collective-permute-start | bytes 393224 | tf_op jit(solution)/shard_map/ppermute | solution.py:438
  70.8 12.9 %collective-permute-start.21 = (bf16[12,128,128]{2,1,0:T(8,128)(2,1)S(1)}, bf16[12,128,128]{2,1,0:T(8,128)(2,1)S(1)}, u32[]{:S(2)}, u32[]{:S(2)}) collective-permute-start(bf16[12,128,128]{2,1,0:T(8,128)(2,1)S(1)} %merge.4), channel_id=1, source_target_pairs={{0,4},{1,5},{2,6},{3,7},{4,0},{5,1},{6,2},{7,3},{8,12},{9,13},{10,... | collective-permute-start | bytes 1179656 | tf_op jit(solution)/shard_map/ppermute | solution.py:438
  73.6 10.1 %collective-permute-start.24 = (bf16[8,128,128]{2,1,0:T(8,128)(2,1)S(1)}, bf16[8,128,128]{2,1,0:T(8,128)(2,1)S(1)}, u32[]{:S(2)}, u32[]{:S(2)}) collective-permute-start(bf16[8,128,128]{2,1,0:T(8,128)(2,1)S(1)} %get-tuple-element.113), channel_id=1, source_target_pairs={{0,1},{1,0},{2,3},{3,2},{4,5},{5,4},{6,7},{7,6},{8,9},{9,8},{10,11... | collective-permute-start | bytes 786440 | tf_op jit(solution)/shard_map/ppermute | solution.py:438
  73.8 9.9 %collective-permute-start.25 = (bf16[8,128,128]{2,1,0:T(8,128)(2,1)S(1)}, bf16[8,128,128]{2,1,0:T(8,128)(2,1)S(1)}, u32[]{:S(2)}, u32[]{:S(2)}) collective-permute-start(bf16[8,128,128]{2,1,0:T(8,128)(2,1)S(1)} %get-tuple-element.114), channel_id=1, source_target_pairs={{0,3},{1,2},{2,1},{3,0},{4,7},{5,6},{6,5},{7,4},{8,11},{9,10},{10,... | collective-permute-start | bytes 786440 | tf_op jit(solution)/shard_map/ppermute | solution.py:438
  75.8 6.5 %collective-permute-start.26 = (bf16[2,128,128]{2,1,0:T(8,128)(2,1)S(1)}, bf16[2,128,128]{2,1,0:T(8,128)(2,1)S(1)}, u32[]{:S(2)}, u32[]{:S(2)}) collective-permute-start(bf16[2,128,128]{2,1,0:T(8,128)(2,1)S(1)} %get-tuple-element.115), channel_id=1, source_target_pairs={{0,1},{1,0},{2,3},{3,2},{4,5},{5,4},{6,7},{7,6},{8,9},{9,8},{10,11... | collective-permute-start | bytes 196616 | tf_op jit(solution)/shard_map/ppermute | solution.py:438
  77.2 6.5 %collective-permute-start.27 = (bf16[2,128,128]{2,1,0:T(8,128)(2,1)S(1)}, bf16[2,128,128]{2,1,0:T(8,128)(2,1)S(1)}, u32[]{:S(2)}, u32[]{:S(2)}) collective-permute-start(bf16[2,128,128]{2,1,0:T(8,128)(2,1)S(1)} %get-tuple-element.116), channel_id=1, source_target_pairs={{0,3},{1,2},{2,1},{3,0},{4,7},{5,6},{6,5},{7,4},{8,11},{9,10},{10,... | collective-permute-start | bytes 196616 | tf_op jit(solution)/shard_map/ppermute | solution.py:438
  (10 other events, 77.7 us)

commit v6 on v5

--- a/solution.py
+++ b/solution.py
@@ -21,6 +21,7 @@
 
 FB = 16
 BF16 = jnp.bfloat16
+TURNS = 4
 F32 = jnp.float32
 MB = 2**20
 
@@ -95,14 +96,19 @@
     count, channels = xbuf.shape[0], xbuf.shape[1]
     turns = sems.shape[0]
     chunk = count // turns
-    copies = [
-        pltpu.make_async_copy(
-            traces_ref.at[pl.ds(i * chunk, chunk)], xbuf.at[pl.ds(i * chunk, chunk)], sems.at[i]
+
+    def read(i):
+        at = pl.ds(i * chunk, chunk)
+        return pltpu.make_async_copy(traces_ref.at[at], xbuf.at[at], sems.at[i])
+
+    def write(i, third):
+        at = pl.ds(pl.multiple_of(i * chunk * 16, 16), chunk * 16)
+        return pltpu.make_async_copy(
+            held.at[third, :, at], thirds[third].at[:, at], out_sems.at[i, third]
         )
-        for i in range(turns)
-    ]
-    for copy in copies:
-        copy.start()
+
+    for i in range(turns):
+        read(i).start()
     chan = lax.axis_index("chan")
     core = chan & 1
     per_device = channels // VSB
@@ -119,21 +125,20 @@
         wanted = jnp.where(((col >> 5) & 3) == hi, want, -1)
         select[hi * channels : (hi + 1) * channels, :] = (row == wanted).astype(F32).astype(BF16)
     live = mask_ref[...].astype(F32)[None]
-    writes = []
-    for i in range(turns):
-        copies[i].wait()
-        for n in range(i * chunk, (i + 1) * chunk):
+
+    def turn(i, carry):
+        read(i).wait()
+        for k in range(chunk):
+            n = i * chunk + k
             w = whiten_rows(dot(table_ref[...], xbuf[n], ((1,), (1,))), live)
+            at = pl.ds(pl.multiple_of(n * 16, 16), 16)
             for third in range(3):
-                held[third, :, n * 16 : (n + 1) * 16, :] = w[:, :, third * 128 : (third + 1) * 128]
-        if i % 2 == 1:
-            at = pl.ds((i - 1) * chunk * 16, 2 * chunk * 16)
-            for third in range(3):
-                write = pltpu.make_async_copy(
-                    held.at[third, :, at], thirds[third].at[:, at], out_sems.at[i // 2, third]
-                )
-                write.start()
-                writes.append(write)
+                held[third, :, at, :] = w[:, :, third * 128 : (third + 1) * 128]
+        for third in range(3):
+            write(i, third).start()
+        return carry
+
+    lax.fori_loop(0, turns, turn, 0)
     for half, pair in ((core, (keep0, keep1)), (1 - core, (send0, send1))):
         for t in range(2):
             low = half * 2 + t
@@ -141,8 +146,9 @@
             out = dot(jnp.concatenate(left, axis=1), select[...]).astype(BF16)
             pair[0][t * 256 : (t + 1) * 256, :] = out[:, :128]
             pair[1][t * 256 : (t + 1) * 256, :] = out[:, 128:]
-    for write in writes:
-        write.wait()
+    for i in range(turns):
+        for third in range(3):
+            write(i, third).wait()
 
 
 def spectra(traces, mask, blocks, table):
@@ -159,8 +165,8 @@
             pltpu.VMEM(traces.shape, BF16),
             pltpu.VMEM((3,) + third.shape, BF16),
             pltpu.VMEM((4 * channels, 256), BF16),
-            pltpu.SemaphoreType.DMA((8,)),
-            pltpu.SemaphoreType.DMA((4, 3)),
+            pltpu.SemaphoreType.DMA((TURNS,)),
+            pltpu.SemaphoreType.DMA((TURNS, 3)),
         ],
         compiler_params=pltpu.CompilerParams(vmem_limit_bytes=60 * MB),
         cost_estimate=pl.CostEstimate(flops=10**9, bytes_accessed=10**7, transcendentals=0),
@@ -198,6 +204,7 @@
         pick_kernel,
         out_shape=[jax.ShapeDtypeStruct(shape, BF16) for shape in shapes],
         out_specs=[vmem] * 2,
+        compiler_params=pltpu.CompilerParams(vmem_limit_bytes=16 * MB),
         cost_estimate=pl.CostEstimate(flops=10**6, bytes_accessed=10**6, transcendentals=0),
         name="pick_rows",
     )()
@@ -298,9 +305,12 @@
             block = hi * 4 + (((lo >> 1) ^ core) << 1) + (lo & 1)
             for i, third in enumerate(thirds):
                 left = [spread(rows, both[s, i, lo >> 1]) for s in range(len(steps))]
-                out = dot(jnp.concatenate(left, axis=0), partners[i][block]).astype(BF16)
-                stacked[i, :, :, block] = out.reshape(len(steps), 16, 16, 128)
-    lag = jnp.concatenate([lag_ref[...], lag_ref[...]], axis=1)
+                out = dot(jnp.concatenate(left, axis=0), partners[i][block])
+                out = out.reshape(len(steps), 16, 16, 128)
+                for place, s in enumerate(steps):
+                    both_groups = out[place] + sums[i][s, :, block].astype(F32)
+                    stacked[i, place, :, block] = both_groups.astype(BF16)
+    lag = lag_ref[...]
     for part, out in zip(parts, outs):
         wanted = [
             (s, thirds.index(third), KEPT[third].index(where) * 4 + first + r)
@@ -309,12 +319,7 @@
             for r in range(amount)
         ]
         for k in range(0, len(wanted), 2):
-            x = [
-                jnp.concatenate(
-                    [sums[i][steps[s], row].reshape(256, 128), stacked[i, s, row].reshape(256, 128)]
-                )
-                for s, i, row in wanted[k : k + 2]
-            ]
+            x = [stacked[i, s, row].reshape(256, 128) for s, i, row in wanted[k : k + 2]]
             y = dot(lag, jnp.concatenate(x, axis=1)).astype(BF16)
             for j in range(len(x)):
                 out[k + j] = y[:, j * 128 : (j + 1) * 128]

time: 85.5 us -> 82.2 us (0.961)
  Pallas kernels: 26.6 us -> 24.1 us
  local copies, waits for them, and re-layouts: 1.22 us -> 0.05 us
  other arithmetic: 3.02 us -> 2.11 us
    unnamed x13 -> x9, local copies, waits for them, and re-layouts: 1.2 us -> 0.03 us
    pallas_call x1, Pallas kernels: 1.47 us -> 0.41 us  [pick_rows(): pl.pallas_call(pick_kernel, out_shape=[jax.ShapeDtypeStruct(shape, BF16)...]
    ppermute x12, waiting for transfers between devices: 10.8 us -> 11.8 us  [chan_swap(): return lax.ppermute(x, 'chan', [(i, i ^ bits) for i in range(16)])]
    add x3, other arithmetic: 1.02 us -> 0.11 us  [on_device(): part0 + chan_swap(part0, one)]
  transfers between devices with their start and end apart: 28 -> 28, of which waited for: 13 -> 14; matrix products, arithmetic and copies ran while one was open for 4% -> 3% of each run, Pallas kernels for 20% -> 18%
where the time goes in v6:
time: 82.2 us; the launch traced here: 82.1 us
  starting transfers between devices  34.3 us (42%)
  Pallas kernels  24.1 us (29%)
  waiting for transfers between devices  21.3 us (26%)
  other arithmetic  2.11 us (3%)
    ppermute x16, starting transfers between devices, win_swap(): return lax.ppermute(x, 'win', [(i, i ^ bits) for i in range(8)])  20.7 us
    ppermute x12, starting transfers between devices, chan_swap(): return lax.ppermute(x, 'chan', [(i, i ^ bits) for i in range(16)])  13.6 us
    ppermute x12, waiting for transfers between devices, chan_swap(): return lax.ppermute(x, 'chan', [(i, i ^ bits) for i in range(16)])  11.8 us
    ppermute x16, waiting for transfers between devices, win_swap(): return lax.ppermute(x, 'win', [(i, i ^ bits) for i in range(8)])  9.58 us
    pallas_call x2, Pallas kernels, correlate(): pl.pallas_call(functools.partial(correlate_kernel, thirds, steps, parts),...  8.53 us
    pallas_call x1, Pallas kernels, spectra(): pl.pallas_call(spectra_kernel, out_shape=[third] * 3 + [shape] * 4, in_sp...  7.47 us
    pallas_call x1, Pallas kernels, correlate_own(): pl.pallas_call(functools.partial(own_kernel, steps), out_shape=[jax.Shape...  5.49 us
    add x2, other arithmetic, on_device(): part0, part1 = (keep0 + chan_swap(send0, 1), keep1 + chan_swap(send1, 1))  1.88 us
  transfers between devices with their start and end apart: 28, of which 14 were waited for; matrix products, arithmetic and copies ran while one was open for 3% of the time, Pallas kernels for 18%

profile of v6, /device:TPU:0, one launch (start us, length us, event | category | flops | bytes accessed | tf_op | source)
XLA Modules:
  0.0 82.1 jit_solution(13714311233255042177)
XLA Ops:
  0.0 7.5 %spectra.1 = (bf16[16,256,128]{2,1,0:T(8,128)(2,1)}, bf16[16,256,128]{2,1,0:T(8,128)(2,1)}, bf16[16,256,128]{2,1,0:T(8,128)(2,1)}, bf16[512,128]{1,0:T(8,128)(2,...) custom-call(s32[2,4]{1,0:T(2,128)} %blocks_ref.1, ...), custom_call_target="tpu_custom_call" | custom-call | flops 1000000000 | bytes 10000000 | tf_op jit(solution)/shard_map/spectra/pallas_call | solution.py:159
  7.5 1.7 %collective-permute-start.8 = (bf16[16,256,128]{2,1,0:T(8,128)(2,1)}, bf16[16,256,128]{2,1,0:T(8,128)(2,1)S(1)}, u32[]{:S(2)}, u32[]{:S(2)}) collective-permute-start(bf16[16,256,128]{2,1,0:T(8,128)(2,1)} %get-tuple-element.71.rest_1_), channel_id=1, source_target_pairs={{0,1},{1,0},{2,3},{3,2},{4,5},{5,4},{6,7},{7,6},{8,9},{9,8},{10,11... | collective-permute-start | bytes 3145736 | tf_op jit(solution)/shard_map/ppermute | solution.py:443
  9.2 2.1 %collective-permute-start.9 = (bf16[16,256,128]{2,1,0:T(8,128)(2,1)}, bf16[16,256,128]{2,1,0:T(8,128)(2,1)S(1)}, u32[]{:S(2)}, u32[]{:S(2)}) collective-permute-start(bf16[16,256,128]{2,1,0:T(8,128)(2,1)} %get-tuple-element.72.rest_2_), channel_id=1, source_target_pairs={{0,3},{1,2},{2,1},{3,0},{4,7},{5,6},{6,5},{7,4},{8,11},{9,10},{10,... | collective-permute-start | bytes 3145736 | tf_op jit(solution)/shard_map/ppermute | solution.py:443
  13.8 2.0 %collective-permute-start.4 = (bf16[512,128]{1,0:T(8,128)(2,1)S(1)}, bf16[512,128]{1,0:T(8,128)(2,1)S(1)}, u32[]{:S(2)}, u32[]{:S(2)}) collective-permute-start(bf16[512,128]{1,0:T(8,128)(2,1)S(1)} %add.27), channel_id=1, source_target_pairs={{0,16},{8,24},{16,0},{24,8},{32,48},{40,56},{48,32},{56,40},{64,80... | collective-permute-start | bytes 393224 | tf_op jit(solution)/shard_map/ppermute | solution.py:439
  16.7 3.3 %collective-permute-start.1 = (bf16[512,128]{1,0:T(8,128)(2,1)S(1)}, bf16[512,128]{1,0:T(8,128)(2,1)S(1)}, u32[]{:S(2)}, u32[]{:S(2)}) collective-permute-start(bf16[512,128]{1,0:T(8,128)(2,1)S(1)} %add.24), channel_id=1, source_target_pairs={{0,64},{8,72},{16,80},{24,88},{32,96},{40,104},{48,112},{56,120},{... | collective-permute-start | bytes 393224 | tf_op jit(solution)/shard_map/ppermute | solution.py:439
  20.0 2.9 %collective-permute-start.5 = (bf16[512,128]{1,0:T(8,128)(2,1)S(1)}, bf16[512,128]{1,0:T(8,128)(2,1)S(1)}, u32[]{:S(2)}, u32[]{:S(2)}) collective-permute-start(bf16[512,128]{1,0:T(8,128)(2,1)S(1)} %add.28), channel_id=1, source_target_pairs={{0,64},{8,72},{16,80},{24,88},{32,96},{40,104},{48,112},{56,120},{... | collective-permute-start | bytes 393224 | tf_op jit(solution)/shard_map/ppermute | solution.py:439
  25.2 1.4 %collective-permute-done.5 = bf16[512,128]{1,0:T(8,128)(2,1)S(1)} collective-permute-done((bf16[512,128]{1,0:T(8,128)(2,1)S(1)}, bf16[512,128]{1,0:T(8,128)(2,1)S(1)}, u32[]{:S(2)}, u32[]{:S(2)}) %collective-permute-start.5) | collective-permute-done | bytes 131104 | tf_op jit(solution)/shard_map/ppermute | solution.py:439
  26.7 2.0 %collective-permute-done.2 = bf16[512,128]{1,0:T(8,128)(2,1)S(1)} collective-permute-done((bf16[512,128]{1,0:T(8,128)(2,1)S(1)}, bf16[512,128]{1,0:T(8,128)(2,1)S(1)}, u32[]{:S(2)}, u32[]{:S(2)}) %collective-permute-start.2) | collective-permute-done | bytes 131104 | tf_op jit(solution)/shard_map/ppermute | solution.py:439
  28.7 1.8 %collective-permute-start.16 = (bf16[16,256,128]{2,1,0:T(8,128)(2,1)S(1)}, bf16[16,256,128]{2,1,0:T(8,128)(2,1)S(1)}, u32[]{:S(2)}, u32[]{:S(2)}) collective-permute-start(bf16[16,256,128]{2,1,0:T(8,128)(2,1)S(1)} %copy-done), channel_id=1, source_target_pairs={{0,4},{1,5},{2,6},{3,7},{4,0},{5,1},{6,2},{7,3},{8,12},{9,13},{10,... | collective-permute-start | bytes 3145736 | tf_op jit(solution)/shard_map/ppermute | solution.py:443
  30.6 2.3 %collective-permute-start.7 = (bf16[512,128]{1,0:T(8,128)(2,1)S(1)}, bf16[512,128]{1,0:T(8,128)(2,1)S(1)}, u32[]{:S(2)}, u32[]{:S(2)}) collective-permute-start(bf16[512,128]{1,0:T(8,128)(2,1)S(1)} %add.29), channel_id=1, source_target_pairs={{0,48},{8,56},{16,32},{24,40},{32,16},{40,24},{48,0},{56,8},{64,11... | collective-permute-start | bytes 393224 | tf_op jit(solution)/shard_map/ppermute | solution.py:439
  33.8 3.3 %collective-permute-done.7 = bf16[512,128]{1,0:T(8,128)(2,1)S(1)} collective-permute-done((bf16[512,128]{1,0:T(8,128)(2,1)S(1)}, bf16[512,128]{1,0:T(8,128)(2,1)S(1)}, u32[]{:S(2)}, u32[]{:S(2)}) %collective-permute-start.7) | collective-permute-done | bytes 131104 | tf_op jit(solution)/shard_map/ppermute | solution.py:439
  37.1 1.9 %collective-permute-done.6 = bf16[512,128]{1,0:T(8,128)(2,1)S(1)} collective-permute-done((bf16[512,128]{1,0:T(8,128)(2,1)S(1)}, bf16[512,128]{1,0:T(8,128)(2,1)S(1)}, u32[]{:S(2)}, u32[]{:S(2)}) %collective-permute-start.6) | collective-permute-done | bytes 131104 | tf_op jit(solution)/shard_map/ppermute | solution.py:439
  41.2 5.5 %correlate_own.1 = (bf16[2,16,16,16,128]{4,3,2,1,0:T(8,128)(2,1)S(1)}, bf16[2,16,16,16,128]{4,3,2,1,0:T(8,128)(2,1)S(1)}, bf16[2,16,16,16,128]{4,3,2,1,0:T(8,128)(2,1)S(1)}) custom-call(bf16[4,448,256]{2,1,0:T(8,128)(2,1)S(1)} %get-tuple-element.77.pick, bf16[1024,128]{1,0:T(8,128)(2,1)S(1)} %constant_dynamic-update-slice_fusion.a, ...), custom_call_target="tpu_custom_call" | custom-call | flops 1000000 | bytes 1000000 | tf_op jit(solution)/shard_map/correlate_own/pallas_call | solution.py:280
  48.8 5.5 %correlate.2 = (bf16[8,128,128]{2,1,0:T(8,128)(2,1)S(1)}, bf16[12,128,128]{2,1,0:T(8,128)(2,1)S(1)}, bf16[12,128,128]{2,1,0:T(8,128)(2,1)S(1)}, bf16[8,128,128]{...) custom-call(bf16[8,256,256]{2,1,0:T(8,128)(2,1)S(1)} %get-tuple-elem, ...), custom_call_target="tpu_custom_call" | custom-call | flops 1000000 | bytes 1000000 | tf_op jit(solution)/shard_map/correlate/pallas_call | solution.py:333
  55.4 1.8 %collective-permute-start.19 = (bf16[12,128,128]{2,1,0:T(8,128)(2,1)S(1)}, bf16[12,128,128]{2,1,0:T(8,128)(2,1)S(1)}, u32[]{:S(2)}, u32[]{:S(2)}) collective-permute-start(bf16[12,128,128]{2,1,0:T(8,128)(2,1)S(1)} %get-tuple-element.96), channel_id=1, source_target_pairs={{0,3},{1,2},{2,1},{3,0},{4,7},{5,6},{6,5},{7,4},{8,11},{9,10},{10,... | collective-permute-start | bytes 1179656 | tf_op jit(solution)/shard_map/ppermute | solution.py:443
  58.3 1.3 %collective-permute-done.20.rest_1_ = bf16[512,128]{1,0:T(8,128)(2,1)S(1)} collective-permute-done((bf16[512,128]{1,0:T(8,128)(2,1)S(1)}, bf16[512,128]{1,0:T(8,128)(2,1)S(1)}, u32[]{:S(2)}, u32[]{:S(2)}) %collective-permute-start.20) | collective-permute-done | bytes 131104 | tf_op jit(solution)/shard_map/ppermute | solution.py:439
  59.6 3.0 %correlate.3 = (bf16[4,128,128]{2,1,0:T(8,128)(2,1)S(1)}, bf16[4,128,128]{2,1,0:T(8,128)(2,1)S(1)}, bf16[8,128,128]{2,1,0:T(8,128)(2,1)S(1)}, bf16[8,128,128]{2,1,0:T(8,128)(2,1)S(1)}, bf16[8,128,128]{2,1,0:T(8,128)(2,1)S(1)}) custom-call(bf16[8,256,256]{2,1,0:T(8,128)(2,1)S(1)} %get-tuple-element.68.pick, bf16[128,256]{1,0:T(8,128)(2,1)S(1)} %copy-done.3, ...), custom_call_target="tpu_custom_call" | custom-call | flops 1000000 | bytes 1000000 | tf_op jit(solution)/shard_map/correlate/pallas_call | solution.py:333
  63.4 2.1 %collective-permute-start.23 = (bf16[4,128,128]{2,1,0:T(8,128)(2,1)S(1)}, bf16[4,128,128]{2,1,0:T(8,128)(2,1)S(1)}, u32[]{:S(2)}, u32[]{:S(2)}) collective-permute-start(bf16[4,128,128]{2,1,0:T(8,128)(2,1)S(1)} %get-tuple-element.112), channel_id=1, source_target_pairs={{0,3},{1,2},{2,1},{3,0},{4,7},{5,6},{6,5},{7,4},{8,11},{9,10},{10,... | collective-permute-start | bytes 393224 | tf_op jit(solution)/shard_map/ppermute | solution.py:443
  65.8 1.7 %collective-permute-done.19.refs_3_.refs_4_ = bf16[12,128,128]{2,1,0:T(8,128)(2,1)S(1)} collective-permute-done((bf16[12,128,128]{2,1,0:T(8,128)(2,1)S(1)}, bf16[12,128,128]{2,1,0:T(8,128)(2,1)S(1)}, u32[]{:S(2)}, u32[]{:S(2)}) %collective-permute-start.19) | collective-permute-done | bytes 393248 | tf_op jit(solution)/shard_map/ppermute | solution.py:443
  67.6 1.4 %collective-permute-start.21 = (bf16[12,128,128]{2,1,0:T(8,128)(2,1)S(1)}, bf16[12,128,128]{2,1,0:T(8,128)(2,1)S(1)}, u32[]{:S(2)}, u32[]{:S(2)}) collective-permute-start(bf16[12,128,128]{2,1,0:T(8,128)(2,1)S(1)} %merge.4), channel_id=1, source_target_pairs={{0,4},{1,5},{2,6},{3,7},{4,0},{5,1},{6,2},{7,3},{8,12},{9,13},{10,... | collective-permute-start | bytes 1179656 | tf_op jit(solution)/shard_map/ppermute | solution.py:443
  70.3 2.1 %collective-permute-start.25 = (bf16[8,128,128]{2,1,0:T(8,128)(2,1)S(1)}, bf16[8,128,128]{2,1,0:T(8,128)(2,1)S(1)}, u32[]{:S(2)}, u32[]{:S(2)}) collective-permute-start(bf16[8,128,128]{2,1,0:T(8,128)(2,1)S(1)} %get-tuple-element.114), channel_id=1, source_target_pairs={{0,3},{1,2},{2,1},{3,0},{4,7},{5,6},{6,5},{7,4},{8,11},{9,10},{10,... | collective-permute-start | bytes 786440 | tf_op jit(solution)/shard_map/ppermute | solution.py:443
  72.5 1.3 %collective-permute-start.26 = (bf16[2,128,128]{2,1,0:T(8,128)(2,1)S(1)}, bf16[2,128,128]{2,1,0:T(8,128)(2,1)S(1)}, u32[]{:S(2)}, u32[]{:S(2)}) collective-permute-start(bf16[2,128,128]{2,1,0:T(8,128)(2,1)S(1)} %get-tuple-element.115), channel_id=1, source_target_pairs={{0,1},{1,0},{2,3},{3,2},{4,5},{5,4},{6,7},{7,6},{8,9},{9,8},{10,11... | collective-permute-start | bytes 196616 | tf_op jit(solution)/shard_map/ppermute | solution.py:443
  74.9 4.2 %collective-permute-done.26.refs_9_ = bf16[2,128,128]{2,1,0:T(8,128)(2,1)S(1)} collective-permute-done((bf16[2,128,128]{2,1,0:T(8,128)(2,1)S(1)}, bf16[2,128,128]{2,1,0:T(8,128)(2,1)S(1)}, u32[]{:S(2)}, u32[]{:S(2)}) %collective-permute-start.26) | collective-permute-done | bytes 65568 | tf_op jit(solution)/shard_map/ppermute | solution.py:443
  80.4 1.6 %finish.1 = f32[4,2,384,128]{3,2,1,0:T(8,128)} custom-call(bf16[8,128,128]{2,1,0:T(8,128)(2,1)S(1)} %get-tuple-element.88.refs_0_, bf16[8,128,128]{2,1,0:T(8,128)(2,1)S(1)} %get-tuple-element.89.refs_1_, bf16[8,128,128]{2,1,0:T(8,128)(2,1)S(1)} %collective-permute-done.17.refs_2_, bf16[12,128,128]{2,1,0:T(8,128)(2,1)S(1)} %collective-permute-done.18.refs_2_.refs_3_, ...), custom_call_target="tpu_custom_call" | custom-call | tf_op jit(solution)/shard_map/finish/pallas_call | solution.py:382
  (60 shorter events, 18.0 us)
Async XLA Ops:
  7.5 31.6 %collective-permute-start.8 = (bf16[16,256,128]{2,1,0:T(8,128)(2,1)}, bf16[16,256,128]{2,1,0:T(8,128)(2,1)S(1)}, u32[]{:S(2)}, u32[]{:S(2)}) collective-permute-start(bf16[16,256,128]{2,1,0:T(8,128)(2,1)} %get-tuple-element.71.rest_1_), channel_id=1, source_target_pairs={{0,1},{1,0},{2,3},{3,2},{4,5},{5,4},{6,7},{7,6},{8,9},{9,8},{10,11... | collective-permute-start | bytes 3145736 | tf_op jit(solution)/shard_map/ppermute | solution.py:443
  9.2 30.0 %collective-permute-start.9 = (bf16[16,256,128]{2,1,0:T(8,128)(2,1)}, bf16[16,256,128]{2,1,0:T(8,128)(2,1)S(1)}, u32[]{:S(2)}, u32[]{:S(2)}) collective-permute-start(bf16[16,256,128]{2,1,0:T(8,128)(2,1)} %get-tuple-element.72.rest_2_), channel_id=1, source_target_pairs={{0,3},{1,2},{2,1},{3,0},{4,7},{5,6},{6,5},{7,4},{8,11},{9,10},{10,... | collective-permute-start | bytes 3145736 | tf_op jit(solution)/shard_map/ppermute | solution.py:443
  11.3 4.5 %collective-permute-start = (bf16[512,128]{1,0:T(8,128)(2,1)}, bf16[512,128]{1,0:T(8,128)(2,1)S(1)}, u32[]{:S(2)}, u32[]{:S(2)}) collective-permute-start(bf16[512,128]{1,0:T(8,128)(2,1)} %get-tuple-element.62), channel_id=1, source_target_pairs={{0,8},{8,0},{16,24},{24,16},{32,40},{40,32},{48,56},{56,48},{64,72... | collective-permute-start | bytes 393224 | tf_op jit(solution)/shard_map/ppermute | solution.py:439
  13.8 6.2 %collective-permute-start.4 = (bf16[512,128]{1,0:T(8,128)(2,1)S(1)}, bf16[512,128]{1,0:T(8,128)(2,1)S(1)}, u32[]{:S(2)}, u32[]{:S(2)}) collective-permute-start(bf16[512,128]{1,0:T(8,128)(2,1)S(1)} %add.27), channel_id=1, source_target_pairs={{0,16},{8,24},{16,0},{24,8},{32,48},{40,56},{48,32},{56,40},{64,80... | collective-permute-start | bytes 393224 | tf_op jit(solution)/shard_map/ppermute | solution.py:439
  16.7 6.9 %collective-permute-start.1 = (bf16[512,128]{1,0:T(8,128)(2,1)S(1)}, bf16[512,128]{1,0:T(8,128)(2,1)S(1)}, u32[]{:S(2)}, u32[]{:S(2)}) collective-permute-start(bf16[512,128]{1,0:T(8,128)(2,1)S(1)} %add.24), channel_id=1, source_target_pairs={{0,64},{8,72},{16,80},{24,88},{32,96},{40,104},{48,112},{56,120},{... | collective-permute-start | bytes 393224 | tf_op jit(solution)/shard_map/ppermute | solution.py:439
  20.0 6.6 %collective-permute-start.5 = (bf16[512,128]{1,0:T(8,128)(2,1)S(1)}, bf16[512,128]{1,0:T(8,128)(2,1)S(1)}, u32[]{:S(2)}, u32[]{:S(2)}) collective-permute-start(bf16[512,128]{1,0:T(8,128)(2,1)S(1)} %add.28), channel_id=1, source_target_pairs={{0,64},{8,72},{16,80},{24,88},{32,96},{40,104},{48,112},{56,120},{... | collective-permute-start | bytes 393224 | tf_op jit(solution)/shard_map/ppermute | solution.py:439
  23.6 5.0 %collective-permute-start.2 = (bf16[512,128]{1,0:T(8,128)(2,1)S(1)}, bf16[512,128]{1,0:T(8,128)(2,1)S(1)}, u32[]{:S(2)}, u32[]{:S(2)}) collective-permute-start(bf16[512,128]{1,0:T(8,128)(2,1)S(1)} %add.25), channel_id=1, source_target_pairs={{0,16},{8,24},{16,0},{24,8},{32,48},{40,56},{48,32},{56,40},{64,80... | collective-permute-start | bytes 393224 | tf_op jit(solution)/shard_map/ppermute | solution.py:439
  28.7 26.1 %collective-permute-start.16 = (bf16[16,256,128]{2,1,0:T(8,128)(2,1)S(1)}, bf16[16,256,128]{2,1,0:T(8,128)(2,1)S(1)}, u32[]{:S(2)}, u32[]{:S(2)}) collective-permute-start(bf16[16,256,128]{2,1,0:T(8,128)(2,1)S(1)} %copy-done), channel_id=1, source_target_pairs={{0,4},{1,5},{2,6},{3,7},{4,0},{5,1},{6,2},{7,3},{8,12},{9,13},{10,... | collective-permute-start | bytes 3145736 | tf_op jit(solution)/shard_map/ppermute | solution.py:443
  30.6 6.5 %collective-permute-start.7 = (bf16[512,128]{1,0:T(8,128)(2,1)S(1)}, bf16[512,128]{1,0:T(8,128)(2,1)S(1)}, u32[]{:S(2)}, u32[]{:S(2)}) collective-permute-start(bf16[512,128]{1,0:T(8,128)(2,1)S(1)} %add.29), channel_id=1, source_target_pairs={{0,48},{8,56},{16,32},{24,40},{32,16},{40,24},{48,0},{56,8},{64,11... | collective-permute-start | bytes 393224 | tf_op jit(solution)/shard_map/ppermute | solution.py:439
  32.9 6.2 %collective-permute-start.6 = (bf16[512,128]{1,0:T(8,128)(2,1)S(1)}, bf16[512,128]{1,0:T(8,128)(2,1)S(1)}, u32[]{:S(2)}, u32[]{:S(2)}) collective-permute-start(bf16[512,128]{1,0:T(8,128)(2,1)S(1)} %add.26), channel_id=1, source_target_pairs={{0,48},{8,56},{16,32},{24,40},{32,16},{40,24},{48,0},{56,8},{64,11... | collective-permute-start | bytes 393224 | tf_op jit(solution)/shard_map/ppermute | solution.py:439
  39.2 2.0 %collective-permute-start.12 = (bf16[1024,128]{1,0:T(8,128)(2,1)S(1)}, bf16[1024,128]{1,0:T(8,128)(2,1)S(1)}, u32[]{:S(2)}, u32[]{:S(2)}) collective-permute-start(bf16[1024,128]{1,0:T(8,128)(2,1)S(1)} %constant_dynamic-update-slice_fusion.a), channel_id=1, source_target_pairs={{0,8},{8,0},{16,24},{24,16},{32,40},{40,32},{48,56},{56,48},{64,72... | collective-permute-start | bytes 786440 | tf_op jit(solution)/shard_map/ppermute | solution.py:439
  39.6 7.0 %collective-permute-start.10 = (bf16[512,128]{1,0:T(8,128)(2,1)S(1)}, bf16[512,128]{1,0:T(8,128)(2,1)S(1)}, u32[]{:S(2)}, u32[]{:S(2)}) collective-permute-start(bf16[512,128]{1,0:T(8,128)(2,1)S(1)} %get-tuple-element.75), channel_id=1, source_target_pairs={{0,1},{1,0},{2,3},{3,2},{4,5},{5,4},{6,7},{7,6},{8,9},{9,8},{10,11... | collective-permute-start | bytes 393224 | tf_op jit(solution)/shard_map/ppermute | solution.py:443
  40.3 6.8 %collective-permute-start.11 = (bf16[512,128]{1,0:T(8,128)(2,1)S(1)}, bf16[512,128]{1,0:T(8,128)(2,1)S(1)}, u32[]{:S(2)}, u32[]{:S(2)}) collective-permute-start(bf16[512,128]{1,0:T(8,128)(2,1)S(1)} %get-tuple-element.76), channel_id=1, source_target_pairs={{0,3},{1,2},{2,1},{3,0},{4,7},{5,6},{6,5},{7,4},{8,11},{9,10},{10,... | collective-permute-start | bytes 393224 | tf_op jit(solution)/shard_map/ppermute | solution.py:443
  47.7 7.2 %collective-permute-start.15 = (bf16[512,128]{1,0:T(8,128)(2,1)S(1)}, bf16[512,128]{1,0:T(8,128)(2,1)S(1)}, u32[]{:S(2)}, u32[]{:S(2)}) collective-permute-start(bf16[512,128]{1,0:T(8,128)(2,1)S(1)} %get-tuple-element.90), channel_id=1, source_target_pairs={{0,4},{1,5},{2,6},{3,7},{4,0},{5,1},{6,2},{7,3},{8,12},{9,13},{10,... | collective-permute-start | bytes 393224 | tf_op jit(solution)/shard_map/ppermute | solution.py:443
  54.8 10.9 %collective-permute-start.18 = (bf16[12,128,128]{2,1,0:T(8,128)(2,1)S(1)}, bf16[12,128,128]{2,1,0:T(8,128)(2,1)S(1)}, u32[]{:S(2)}, u32[]{:S(2)}) collective-permute-start(bf16[12,128,128]{2,1,0:T(8,128)(2,1)S(1)} %get-tuple-element.95), channel_id=1, source_target_pairs={{0,1},{1,0},{2,3},{3,2},{4,5},{5,4},{6,7},{7,6},{8,9},{9,8},{10,11... | collective-permute-start | bytes 1179656 | tf_op jit(solution)/shard_map/ppermute | solution.py:443
  55.4 12.1 %collective-permute-start.19 = (bf16[12,128,128]{2,1,0:T(8,128)(2,1)S(1)}, bf16[12,128,128]{2,1,0:T(8,128)(2,1)S(1)}, u32[]{:S(2)}, u32[]{:S(2)}) collective-permute-start(bf16[12,128,128]{2,1,0:T(8,128)(2,1)S(1)} %get-tuple-element.96), channel_id=1, source_target_pairs={{0,3},{1,2},{2,1},{3,0},{4,7},{5,6},{6,5},{7,4},{8,11},{9,10},{10,... | collective-permute-start | bytes 1179656 | tf_op jit(solution)/shard_map/ppermute | solution.py:443
  57.2 8.3 %collective-permute-start.17 = (bf16[8,128,128]{2,1,0:T(8,128)(2,1)S(1)}, bf16[8,128,128]{2,1,0:T(8,128)(2,1)S(1)}, u32[]{:S(2)}, u32[]{:S(2)}) collective-permute-start(bf16[8,128,128]{2,1,0:T(8,128)(2,1)S(1)} %get-tuple-element.94), channel_id=1, source_target_pairs={{0,4},{1,5},{2,6},{3,7},{4,0},{5,1},{6,2},{7,3},{8,12},{9,13},{10,... | collective-permute-start | bytes 786440 | tf_op jit(solution)/shard_map/ppermute | solution.py:443
  62.6 6.3 %collective-permute-start.22 = (bf16[4,128,128]{2,1,0:T(8,128)(2,1)S(1)}, bf16[4,128,128]{2,1,0:T(8,128)(2,1)S(1)}, u32[]{:S(2)}, u32[]{:S(2)}) collective-permute-start(bf16[4,128,128]{2,1,0:T(8,128)(2,1)S(1)} %get-tuple-element.111), channel_id=1, source_target_pairs={{0,1},{1,0},{2,3},{3,2},{4,5},{5,4},{6,7},{7,6},{8,9},{9,8},{10,11... | collective-permute-start | bytes 393224 | tf_op jit(solution)/shard_map/ppermute | solution.py:443
  63.4 6.7 %collective-permute-start.23 = (bf16[4,128,128]{2,1,0:T(8,128)(2,1)S(1)}, bf16[4,128,128]{2,1,0:T(8,128)(2,1)S(1)}, u32[]{:S(2)}, u32[]{:S(2)}) collective-permute-start(bf16[4,128,128]{2,1,0:T(8,128)(2,1)S(1)} %get-tuple-element.112), channel_id=1, source_target_pairs={{0,3},{1,2},{2,1},{3,0},{4,7},{5,6},{6,5},{7,4},{8,11},{9,10},{10,... | collective-permute-start | bytes 393224 | tf_op jit(solution)/shard_map/ppermute | solution.py:443
  67.6 12.9 %collective-permute-start.21 = (bf16[12,128,128]{2,1,0:T(8,128)(2,1)S(1)}, bf16[12,128,128]{2,1,0:T(8,128)(2,1)S(1)}, u32[]{:S(2)}, u32[]{:S(2)}) collective-permute-start(bf16[12,128,128]{2,1,0:T(8,128)(2,1)S(1)} %merge.4), channel_id=1, source_target_pairs={{0,4},{1,5},{2,6},{3,7},{4,0},{5,1},{6,2},{7,3},{8,12},{9,13},{10,... | collective-permute-start | bytes 1179656 | tf_op jit(solution)/shard_map/ppermute | solution.py:443
  70.2 10.2 %collective-permute-start.24 = (bf16[8,128,128]{2,1,0:T(8,128)(2,1)S(1)}, bf16[8,128,128]{2,1,0:T(8,128)(2,1)S(1)}, u32[]{:S(2)}, u32[]{:S(2)}) collective-permute-start(bf16[8,128,128]{2,1,0:T(8,128)(2,1)S(1)} %get-tuple-element.113), channel_id=1, source_target_pairs={{0,1},{1,0},{2,3},{3,2},{4,5},{5,4},{6,7},{7,6},{8,9},{9,8},{10,11... | collective-permute-start | bytes 786440 | tf_op jit(solution)/shard_map/ppermute | solution.py:443
  70.3 10.1 %collective-permute-start.25 = (bf16[8,128,128]{2,1,0:T(8,128)(2,1)S(1)}, bf16[8,128,128]{2,1,0:T(8,128)(2,1)S(1)}, u32[]{:S(2)}, u32[]{:S(2)}) collective-permute-start(bf16[8,128,128]{2,1,0:T(8,128)(2,1)S(1)} %get-tuple-element.114), channel_id=1, source_target_pairs={{0,3},{1,2},{2,1},{3,0},{4,7},{5,6},{6,5},{7,4},{8,11},{9,10},{10,... | collective-permute-start | bytes 786440 | tf_op jit(solution)/shard_map/ppermute | solution.py:443
  72.5 6.7 %collective-permute-start.26 = (bf16[2,128,128]{2,1,0:T(8,128)(2,1)S(1)}, bf16[2,128,128]{2,1,0:T(8,128)(2,1)S(1)}, u32[]{:S(2)}, u32[]{:S(2)}) collective-permute-start(bf16[2,128,128]{2,1,0:T(8,128)(2,1)S(1)} %get-tuple-element.115), channel_id=1, source_target_pairs={{0,1},{1,0},{2,3},{3,2},{4,5},{5,4},{6,7},{7,6},{8,9},{9,8},{10,11... | collective-permute-start | bytes 196616 | tf_op jit(solution)/shard_map/ppermute | solution.py:443
  73.8 6.6 %collective-permute-start.27 = (bf16[2,128,128]{2,1,0:T(8,128)(2,1)S(1)}, bf16[2,128,128]{2,1,0:T(8,128)(2,1)S(1)}, u32[]{:S(2)}, u32[]{:S(2)}) collective-permute-start(bf16[2,128,128]{2,1,0:T(8,128)(2,1)S(1)} %get-tuple-element.116), channel_id=1, source_target_pairs={{0,3},{1,2},{2,1},{3,0},{4,7},{5,6},{6,5},{7,4},{8,11},{9,10},{10,... | collective-permute-start | bytes 196616 | tf_op jit(solution)/shard_map/ppermute | solution.py:443
  (8 other events, 103.2 us)

commit v7 on v6

--- a/solution.py
+++ b/solution.py
@@ -139,13 +139,16 @@
         return carry
 
     lax.fori_loop(0, turns, turn, 0)
-    for half, pair in ((core, (keep0, keep1)), (1 - core, (send0, send1))):
+    left = []
+    for half in (core, 1 - core):
         for t in range(2):
             low = half * 2 + t
-            left = [held[third, hi * 4 + low] for hi in range(4) for third in range(3)]
-            out = dot(jnp.concatenate(left, axis=1), select[...]).astype(BF16)
-            pair[0][t * 256 : (t + 1) * 256, :] = out[:, :128]
-            pair[1][t * 256 : (t + 1) * 256, :] = out[:, 128:]
+            some_rows = [held[third, hi * 4 + low] for hi in range(4) for third in range(3)]
+            left.append(jnp.concatenate(some_rows, axis=1))
+    out = dot(jnp.concatenate(left, axis=0), select[...]).astype(BF16)
+    for k, (first, second) in enumerate(((keep0, keep1), (send0, send1))):
+        first[...] = out[k * 512 : (k + 1) * 512, :128]
+        second[...] = out[k * 512 : (k + 1) * 512, 128:]
     for i in range(turns):
         for third in range(3):
             write(i, third).wait()

time: 82.2 us -> 82.2 us (level)
  no operation moved by 1% of the time
where the time goes in v7:
time: 82.2 us; the launch traced here: 82.1 us
  starting transfers between devices  34.3 us (42%)
  Pallas kernels  24.1 us (29%)
  waiting for transfers between devices  21.3 us (26%)
  other arithmetic  2.11 us (3%)
    ppermute x16, starting transfers between devices, win_swap(): return lax.ppermute(x, 'win', [(i, i ^ bits) for i in range(8)])  20.7 us
    ppermute x12, starting transfers between devices, chan_swap(): return lax.ppermute(x, 'chan', [(i, i ^ bits) for i in range(16)])  13.6 us
    ppermute x12, waiting for transfers between devices, chan_swap(): return lax.ppermute(x, 'chan', [(i, i ^ bits) for i in range(16)])  11.8 us
    ppermute x16, waiting for transfers between devices, win_swap(): return lax.ppermute(x, 'win', [(i, i ^ bits) for i in range(8)])  9.58 us
    pallas_call x2, Pallas kernels, correlate(): pl.pallas_call(functools.partial(correlate_kernel, thirds, steps, parts),...  8.53 us
    pallas_call x1, Pallas kernels, spectra(): pl.pallas_call(spectra_kernel, out_shape=[third] * 3 + [shape] * 4, in_sp...  7.48 us
    pallas_call x1, Pallas kernels, correlate_own(): pl.pallas_call(functools.partial(own_kernel, steps), out_shape=[jax.Shape...  5.49 us
    add x2, other arithmetic, on_device(): part0, part1 = (keep0 + chan_swap(send0, 1), keep1 + chan_swap(send1, 1))  1.88 us
  transfers between devices with their start and end apart: 28, of which 14 were waited for; matrix products, arithmetic and copies ran while one was open for 3% of the time, Pallas kernels for 18%

profile of v7, /device:TPU:0, one launch (start us, length us, event | category | flops | bytes accessed | tf_op | source)
XLA Modules:
  0.0 82.1 jit_solution(15277248652986912864)
XLA Ops:
  0.0 7.5 %spectra.1 = (bf16[16,256,128]{2,1,0:T(8,128)(2,1)}, bf16[16,256,128]{2,1,0:T(8,128)(2,1)}, bf16[16,256,128]{2,1,0:T(8,128)(2,1)}, bf16[512,128]{1,0:T(8,128)(2,...) custom-call(s32[2,4]{1,0:T(2,128)} %blocks_ref.1, ...), custom_call_target="tpu_custom_call" | custom-call | flops 1000000000 | bytes 10000000 | tf_op jit(solution)/shard_map/spectra/pallas_call | solution.py:162
  7.5 1.7 %collective-permute-start.8 = (bf16[16,256,128]{2,1,0:T(8,128)(2,1)}, bf16[16,256,128]{2,1,0:T(8,128)(2,1)S(1)}, u32[]{:S(2)}, u32[]{:S(2)}) collective-permute-start(bf16[16,256,128]{2,1,0:T(8,128)(2,1)} %get-tuple-element.71.rest_1_), channel_id=1, source_target_pairs={{0,1},{1,0},{2,3},{3,2},{4,5},{5,4},{6,7},{7,6},{8,9},{9,8},{10,11... | collective-permute-start | bytes 3145736 | tf_op jit(solution)/shard_map/ppermute | solution.py:446
  9.2 2.1 %collective-permute-start.9 = (bf16[16,256,128]{2,1,0:T(8,128)(2,1)}, bf16[16,256,128]{2,1,0:T(8,128)(2,1)S(1)}, u32[]{:S(2)}, u32[]{:S(2)}) collective-permute-start(bf16[16,256,128]{2,1,0:T(8,128)(2,1)} %get-tuple-element.72.rest_2_), channel_id=1, source_target_pairs={{0,3},{1,2},{2,1},{3,0},{4,7},{5,6},{6,5},{7,4},{8,11},{9,10},{10,... | collective-permute-start | bytes 3145736 | tf_op jit(solution)/shard_map/ppermute | solution.py:446
  13.8 2.0 %collective-permute-start.4 = (bf16[512,128]{1,0:T(8,128)(2,1)S(1)}, bf16[512,128]{1,0:T(8,128)(2,1)S(1)}, u32[]{:S(2)}, u32[]{:S(2)}) collective-permute-start(bf16[512,128]{1,0:T(8,128)(2,1)S(1)} %add.27), channel_id=1, source_target_pairs={{0,16},{8,24},{16,0},{24,8},{32,48},{40,56},{48,32},{56,40},{64,80... | collective-permute-start | bytes 393224 | tf_op jit(solution)/shard_map/ppermute | solution.py:442
  16.7 3.3 %collective-permute-start.1 = (bf16[512,128]{1,0:T(8,128)(2,1)S(1)}, bf16[512,128]{1,0:T(8,128)(2,1)S(1)}, u32[]{:S(2)}, u32[]{:S(2)}) collective-permute-start(bf16[512,128]{1,0:T(8,128)(2,1)S(1)} %add.24), channel_id=1, source_target_pairs={{0,64},{8,72},{16,80},{24,88},{32,96},{40,104},{48,112},{56,120},{... | collective-permute-start | bytes 393224 | tf_op jit(solution)/shard_map/ppermute | solution.py:442
  20.0 2.9 %collective-permute-start.5 = (bf16[512,128]{1,0:T(8,128)(2,1)S(1)}, bf16[512,128]{1,0:T(8,128)(2,1)S(1)}, u32[]{:S(2)}, u32[]{:S(2)}) collective-permute-start(bf16[512,128]{1,0:T(8,128)(2,1)S(1)} %add.28), channel_id=1, source_target_pairs={{0,64},{8,72},{16,80},{24,88},{32,96},{40,104},{48,112},{56,120},{... | collective-permute-start | bytes 393224 | tf_op jit(solution)/shard_map/ppermute | solution.py:442
  25.2 1.4 %collective-permute-done.5 = bf16[512,128]{1,0:T(8,128)(2,1)S(1)} collective-permute-done((bf16[512,128]{1,0:T(8,128)(2,1)S(1)}, bf16[512,128]{1,0:T(8,128)(2,1)S(1)}, u32[]{:S(2)}, u32[]{:S(2)}) %collective-permute-start.5) | collective-permute-done | bytes 131104 | tf_op jit(solution)/shard_map/ppermute | solution.py:442
  26.7 2.0 %collective-permute-done.2 = bf16[512,128]{1,0:T(8,128)(2,1)S(1)} collective-permute-done((bf16[512,128]{1,0:T(8,128)(2,1)S(1)}, bf16[512,128]{1,0:T(8,128)(2,1)S(1)}, u32[]{:S(2)}, u32[]{:S(2)}) %collective-permute-start.2) | collective-permute-done | bytes 131104 | tf_op jit(solution)/shard_map/ppermute | solution.py:442
  28.7 1.8 %collective-permute-start.16 = (bf16[16,256,128]{2,1,0:T(8,128)(2,1)S(1)}, bf16[16,256,128]{2,1,0:T(8,128)(2,1)S(1)}, u32[]{:S(2)}, u32[]{:S(2)}) collective-permute-start(bf16[16,256,128]{2,1,0:T(8,128)(2,1)S(1)} %copy-done), channel_id=1, source_target_pairs={{0,4},{1,5},{2,6},{3,7},{4,0},{5,1},{6,2},{7,3},{8,12},{9,13},{10,... | collective-permute-start | bytes 3145736 | tf_op jit(solution)/shard_map/ppermute | solution.py:446
  30.6 2.3 %collective-permute-start.7 = (bf16[512,128]{1,0:T(8,128)(2,1)S(1)}, bf16[512,128]{1,0:T(8,128)(2,1)S(1)}, u32[]{:S(2)}, u32[]{:S(2)}) collective-permute-start(bf16[512,128]{1,0:T(8,128)(2,1)S(1)} %add.29), channel_id=1, source_target_pairs={{0,48},{8,56},{16,32},{24,40},{32,16},{40,24},{48,0},{56,8},{64,11... | collective-permute-start | bytes 393224 | tf_op jit(solution)/shard_map/ppermute | solution.py:442
  33.8 3.3 %collective-permute-done.7 = bf16[512,128]{1,0:T(8,128)(2,1)S(1)} collective-permute-done((bf16[512,128]{1,0:T(8,128)(2,1)S(1)}, bf16[512,128]{1,0:T(8,128)(2,1)S(1)}, u32[]{:S(2)}, u32[]{:S(2)}) %collective-permute-start.7) | collective-permute-done | bytes 131104 | tf_op jit(solution)/shard_map/ppermute | solution.py:442
  37.1 1.9 %collective-permute-done.6 = bf16[512,128]{1,0:T(8,128)(2,1)S(1)} collective-permute-done((bf16[512,128]{1,0:T(8,128)(2,1)S(1)}, bf16[512,128]{1,0:T(8,128)(2,1)S(1)}, u32[]{:S(2)}, u32[]{:S(2)}) %collective-permute-start.6) | collective-permute-done | bytes 131104 | tf_op jit(solution)/shard_map/ppermute | solution.py:442
  41.2 5.5 %correlate_own.1 = (bf16[2,16,16,16,128]{4,3,2,1,0:T(8,128)(2,1)S(1)}, bf16[2,16,16,16,128]{4,3,2,1,0:T(8,128)(2,1)S(1)}, bf16[2,16,16,16,128]{4,3,2,1,0:T(8,128)(2,1)S(1)}) custom-call(bf16[4,448,256]{2,1,0:T(8,128)(2,1)S(1)} %get-tuple-element.77.pick, bf16[1024,128]{1,0:T(8,128)(2,1)S(1)} %constant_dynamic-update-slice_fusion.a, ...), custom_call_target="tpu_custom_call" | custom-call | flops 1000000 | bytes 1000000 | tf_op jit(solution)/shard_map/correlate_own/pallas_call | solution.py:283
  48.8 5.5 %correlate.2 = (bf16[8,128,128]{2,1,0:T(8,128)(2,1)S(1)}, bf16[12,128,128]{2,1,0:T(8,128)(2,1)S(1)}, bf16[12,128,128]{2,1,0:T(8,128)(2,1)S(1)}, bf16[8,128,128]{...) custom-call(bf16[8,256,256]{2,1,0:T(8,128)(2,1)S(1)} %get-tuple-elem, ...), custom_call_target="tpu_custom_call" | custom-call | flops 1000000 | bytes 1000000 | tf_op jit(solution)/shard_map/correlate/pallas_call | solution.py:336
  55.4 1.8 %collective-permute-start.19 = (bf16[12,128,128]{2,1,0:T(8,128)(2,1)S(1)}, bf16[12,128,128]{2,1,0:T(8,128)(2,1)S(1)}, u32[]{:S(2)}, u32[]{:S(2)}) collective-permute-start(bf16[12,128,128]{2,1,0:T(8,128)(2,1)S(1)} %get-tuple-element.96), channel_id=1, source_target_pairs={{0,3},{1,2},{2,1},{3,0},{4,7},{5,6},{6,5},{7,4},{8,11},{9,10},{10,... | collective-permute-start | bytes 1179656 | tf_op jit(solution)/shard_map/ppermute | solution.py:446
  58.3 1.3 %collective-permute-done.20.rest_1_ = bf16[512,128]{1,0:T(8,128)(2,1)S(1)} collective-permute-done((bf16[512,128]{1,0:T(8,128)(2,1)S(1)}, bf16[512,128]{1,0:T(8,128)(2,1)S(1)}, u32[]{:S(2)}, u32[]{:S(2)}) %collective-permute-start.20) | collective-permute-done | bytes 131104 | tf_op jit(solution)/shard_map/ppermute | solution.py:442
  59.6 3.0 %correlate.3 = (bf16[4,128,128]{2,1,0:T(8,128)(2,1)S(1)}, bf16[4,128,128]{2,1,0:T(8,128)(2,1)S(1)}, bf16[8,128,128]{2,1,0:T(8,128)(2,1)S(1)}, bf16[8,128,128]{2,1,0:T(8,128)(2,1)S(1)}, bf16[8,128,128]{2,1,0:T(8,128)(2,1)S(1)}) custom-call(bf16[8,256,256]{2,1,0:T(8,128)(2,1)S(1)} %get-tuple-element.68.pick, bf16[128,256]{1,0:T(8,128)(2,1)S(1)} %copy-done.3, ...), custom_call_target="tpu_custom_call" | custom-call | flops 1000000 | bytes 1000000 | tf_op jit(solution)/shard_map/correlate/pallas_call | solution.py:336
  63.4 2.1 %collective-permute-start.23 = (bf16[4,128,128]{2,1,0:T(8,128)(2,1)S(1)}, bf16[4,128,128]{2,1,0:T(8,128)(2,1)S(1)}, u32[]{:S(2)}, u32[]{:S(2)}) collective-permute-start(bf16[4,128,128]{2,1,0:T(8,128)(2,1)S(1)} %get-tuple-element.112), channel_id=1, source_target_pairs={{0,3},{1,2},{2,1},{3,0},{4,7},{5,6},{6,5},{7,4},{8,11},{9,10},{10,... | collective-permute-start | bytes 393224 | tf_op jit(solution)/shard_map/ppermute | solution.py:446
  65.8 1.7 %collective-permute-done.19.refs_3_.refs_4_ = bf16[12,128,128]{2,1,0:T(8,128)(2,1)S(1)} collective-permute-done((bf16[12,128,128]{2,1,0:T(8,128)(2,1)S(1)}, bf16[12,128,128]{2,1,0:T(8,128)(2,1)S(1)}, u32[]{:S(2)}, u32[]{:S(2)}) %collective-permute-start.19) | collective-permute-done | bytes 393248 | tf_op jit(solution)/shard_map/ppermute | solution.py:446
  67.6 1.4 %collective-permute-start.21 = (bf16[12,128,128]{2,1,0:T(8,128)(2,1)S(1)}, bf16[12,128,128]{2,1,0:T(8,128)(2,1)S(1)}, u32[]{:S(2)}, u32[]{:S(2)}) collective-permute-start(bf16[12,128,128]{2,1,0:T(8,128)(2,1)S(1)} %merge.4), channel_id=1, source_target_pairs={{0,4},{1,5},{2,6},{3,7},{4,0},{5,1},{6,2},{7,3},{8,12},{9,13},{10,... | collective-permute-start | bytes 1179656 | tf_op jit(solution)/shard_map/ppermute | solution.py:446
  70.4 2.1 %collective-permute-start.25 = (bf16[8,128,128]{2,1,0:T(8,128)(2,1)S(1)}, bf16[8,128,128]{2,1,0:T(8,128)(2,1)S(1)}, u32[]{:S(2)}, u32[]{:S(2)}) collective-permute-start(bf16[8,128,128]{2,1,0:T(8,128)(2,1)S(1)} %get-tuple-element.114), channel_id=1, source_target_pairs={{0,3},{1,2},{2,1},{3,0},{4,7},{5,6},{6,5},{7,4},{8,11},{9,10},{10,... | collective-permute-start | bytes 786440 | tf_op jit(solution)/shard_map/ppermute | solution.py:446
  72.5 1.3 %collective-permute-start.26 = (bf16[2,128,128]{2,1,0:T(8,128)(2,1)S(1)}, bf16[2,128,128]{2,1,0:T(8,128)(2,1)S(1)}, u32[]{:S(2)}, u32[]{:S(2)}) collective-permute-start(bf16[2,128,128]{2,1,0:T(8,128)(2,1)S(1)} %get-tuple-element.115), channel_id=1, source_target_pairs={{0,1},{1,0},{2,3},{3,2},{4,5},{5,4},{6,7},{7,6},{8,9},{9,8},{10,11... | collective-permute-start | bytes 196616 | tf_op jit(solution)/shard_map/ppermute | solution.py:446
  74.9 4.2 %collective-permute-done.26.refs_9_ = bf16[2,128,128]{2,1,0:T(8,128)(2,1)S(1)} collective-permute-done((bf16[2,128,128]{2,1,0:T(8,128)(2,1)S(1)}, bf16[2,128,128]{2,1,0:T(8,128)(2,1)S(1)}, u32[]{:S(2)}, u32[]{:S(2)}) %collective-permute-start.26) | collective-permute-done | bytes 65568 | tf_op jit(solution)/shard_map/ppermute | solution.py:446
  80.4 1.6 %finish.1 = f32[4,2,384,128]{3,2,1,0:T(8,128)} custom-call(bf16[8,128,128]{2,1,0:T(8,128)(2,1)S(1)} %get-tuple-element.88.refs_0_, bf16[8,128,128]{2,1,0:T(8,128)(2,1)S(1)} %get-tuple-element.89.refs_1_, bf16[8,128,128]{2,1,0:T(8,128)(2,1)S(1)} %collective-permute-done.17.refs_2_, bf16[12,128,128]{2,1,0:T(8,128)(2,1)S(1)} %collective-permute-done.18.refs_2_.refs_3_, ...), custom_call_target="tpu_custom_call" | custom-call | tf_op jit(solution)/shard_map/finish/pallas_call | solution.py:385
  (60 shorter events, 18.0 us)
Async XLA Ops:
  7.5 31.6 %collective-permute-start.8 = (bf16[16,256,128]{2,1,0:T(8,128)(2,1)}, bf16[16,256,128]{2,1,0:T(8,128)(2,1)S(1)}, u32[]{:S(2)}, u32[]{:S(2)}) collective-permute-start(bf16[16,256,128]{2,1,0:T(8,128)(2,1)} %get-tuple-element.71.rest_1_), channel_id=1, source_target_pairs={{0,1},{1,0},{2,3},{3,2},{4,5},{5,4},{6,7},{7,6},{8,9},{9,8},{10,11... | collective-permute-start | bytes 3145736 | tf_op jit(solution)/shard_map/ppermute | solution.py:446
  9.2 30.0 %collective-permute-start.9 = (bf16[16,256,128]{2,1,0:T(8,128)(2,1)}, bf16[16,256,128]{2,1,0:T(8,128)(2,1)S(1)}, u32[]{:S(2)}, u32[]{:S(2)}) collective-permute-start(bf16[16,256,128]{2,1,0:T(8,128)(2,1)} %get-tuple-element.72.rest_2_), channel_id=1, source_target_pairs={{0,3},{1,2},{2,1},{3,0},{4,7},{5,6},{6,5},{7,4},{8,11},{9,10},{10,... | collective-permute-start | bytes 3145736 | tf_op jit(solution)/shard_map/ppermute | solution.py:446
  11.3 4.5 %collective-permute-start = (bf16[512,128]{1,0:T(8,128)(2,1)}, bf16[512,128]{1,0:T(8,128)(2,1)S(1)}, u32[]{:S(2)}, u32[]{:S(2)}) collective-permute-start(bf16[512,128]{1,0:T(8,128)(2,1)} %get-tuple-element.62), channel_id=1, source_target_pairs={{0,8},{8,0},{16,24},{24,16},{32,40},{40,32},{48,56},{56,48},{64,72... | collective-permute-start | bytes 393224 | tf_op jit(solution)/shard_map/ppermute | solution.py:442
  13.8 6.2 %collective-permute-start.4 = (bf16[512,128]{1,0:T(8,128)(2,1)S(1)}, bf16[512,128]{1,0:T(8,128)(2,1)S(1)}, u32[]{:S(2)}, u32[]{:S(2)}) collective-permute-start(bf16[512,128]{1,0:T(8,128)(2,1)S(1)} %add.27), channel_id=1, source_target_pairs={{0,16},{8,24},{16,0},{24,8},{32,48},{40,56},{48,32},{56,40},{64,80... | collective-permute-start | bytes 393224 | tf_op jit(solution)/shard_map/ppermute | solution.py:442
  16.7 6.9 %collective-permute-start.1 = (bf16[512,128]{1,0:T(8,128)(2,1)S(1)}, bf16[512,128]{1,0:T(8,128)(2,1)S(1)}, u32[]{:S(2)}, u32[]{:S(2)}) collective-permute-start(bf16[512,128]{1,0:T(8,128)(2,1)S(1)} %add.24), channel_id=1, source_target_pairs={{0,64},{8,72},{16,80},{24,88},{32,96},{40,104},{48,112},{56,120},{... | collective-permute-start | bytes 393224 | tf_op jit(solution)/shard_map/ppermute | solution.py:442
  20.0 6.6 %collective-permute-start.5 = (bf16[512,128]{1,0:T(8,128)(2,1)S(1)}, bf16[512,128]{1,0:T(8,128)(2,1)S(1)}, u32[]{:S(2)}, u32[]{:S(2)}) collective-permute-start(bf16[512,128]{1,0:T(8,128)(2,1)S(1)} %add.28), channel_id=1, source_target_pairs={{0,64},{8,72},{16,80},{24,88},{32,96},{40,104},{48,112},{56,120},{... | collective-permute-start | bytes 393224 | tf_op jit(solution)/shard_map/ppermute | solution.py:442
  23.6 5.0 %collective-permute-start.2 = (bf16[512,128]{1,0:T(8,128)(2,1)S(1)}, bf16[512,128]{1,0:T(8,128)(2,1)S(1)}, u32[]{:S(2)}, u32[]{:S(2)}) collective-permute-start(bf16[512,128]{1,0:T(8,128)(2,1)S(1)} %add.25), channel_id=1, source_target_pairs={{0,16},{8,24},{16,0},{24,8},{32,48},{40,56},{48,32},{56,40},{64,80... | collective-permute-start | bytes 393224 | tf_op jit(solution)/shard_map/ppermute | solution.py:442
  28.7 26.1 %collective-permute-start.16 = (bf16[16,256,128]{2,1,0:T(8,128)(2,1)S(1)}, bf16[16,256,128]{2,1,0:T(8,128)(2,1)S(1)}, u32[]{:S(2)}, u32[]{:S(2)}) collective-permute-start(bf16[16,256,128]{2,1,0:T(8,128)(2,1)S(1)} %copy-done), channel_id=1, source_target_pairs={{0,4},{1,5},{2,6},{3,7},{4,0},{5,1},{6,2},{7,3},{8,12},{9,13},{10,... | collective-permute-start | bytes 3145736 | tf_op jit(solution)/shard_map/ppermute | solution.py:446
  30.6 6.5 %collective-permute-start.7 = (bf16[512,128]{1,0:T(8,128)(2,1)S(1)}, bf16[512,128]{1,0:T(8,128)(2,1)S(1)}, u32[]{:S(2)}, u32[]{:S(2)}) collective-permute-start(bf16[512,128]{1,0:T(8,128)(2,1)S(1)} %add.29), channel_id=1, source_target_pairs={{0,48},{8,56},{16,32},{24,40},{32,16},{40,24},{48,0},{56,8},{64,11... | collective-permute-start | bytes 393224 | tf_op jit(solution)/shard_map/ppermute | solution.py:442
  32.9 6.2 %collective-permute-start.6 = (bf16[512,128]{1,0:T(8,128)(2,1)S(1)}, bf16[512,128]{1,0:T(8,128)(2,1)S(1)}, u32[]{:S(2)}, u32[]{:S(2)}) collective-permute-start(bf16[512,128]{1,0:T(8,128)(2,1)S(1)} %add.26), channel_id=1, source_target_pairs={{0,48},{8,56},{16,32},{24,40},{32,16},{40,24},{48,0},{56,8},{64,11... | collective-permute-start | bytes 393224 | tf_op jit(solution)/shard_map/ppermute | solution.py:442
  39.2 2.0 %collective-permute-start.12 = (bf16[1024,128]{1,0:T(8,128)(2,1)S(1)}, bf16[1024,128]{1,0:T(8,128)(2,1)S(1)}, u32[]{:S(2)}, u32[]{:S(2)}) collective-permute-start(bf16[1024,128]{1,0:T(8,128)(2,1)S(1)} %constant_dynamic-update-slice_fusion.a), channel_id=1, source_target_pairs={{0,8},{8,0},{16,24},{24,16},{32,40},{40,32},{48,56},{56,48},{64,72... | collective-permute-start | bytes 786440 | tf_op jit(solution)/shard_map/ppermute | solution.py:442
  39.6 7.0 %collective-permute-start.10 = (bf16[512,128]{1,0:T(8,128)(2,1)S(1)}, bf16[512,128]{1,0:T(8,128)(2,1)S(1)}, u32[]{:S(2)}, u32[]{:S(2)}) collective-permute-start(bf16[512,128]{1,0:T(8,128)(2,1)S(1)} %get-tuple-element.75), channel_id=1, source_target_pairs={{0,1},{1,0},{2,3},{3,2},{4,5},{5,4},{6,7},{7,6},{8,9},{9,8},{10,11... | collective-permute-start | bytes 393224 | tf_op jit(solution)/shard_map/ppermute | solution.py:446
  40.3 6.8 %collective-permute-start.11 = (bf16[512,128]{1,0:T(8,128)(2,1)S(1)}, bf16[512,128]{1,0:T(8,128)(2,1)S(1)}, u32[]{:S(2)}, u32[]{:S(2)}) collective-permute-start(bf16[512,128]{1,0:T(8,128)(2,1)S(1)} %get-tuple-element.76), channel_id=1, source_target_pairs={{0,3},{1,2},{2,1},{3,0},{4,7},{5,6},{6,5},{7,4},{8,11},{9,10},{10,... | collective-permute-start | bytes 393224 | tf_op jit(solution)/shard_map/ppermute | solution.py:446
  47.7 7.2 %collective-permute-start.15 = (bf16[512,128]{1,0:T(8,128)(2,1)S(1)}, bf16[512,128]{1,0:T(8,128)(2,1)S(1)}, u32[]{:S(2)}, u32[]{:S(2)}) collective-permute-start(bf16[512,128]{1,0:T(8,128)(2,1)S(1)} %get-tuple-element.90), channel_id=1, source_target_pairs={{0,4},{1,5},{2,6},{3,7},{4,0},{5,1},{6,2},{7,3},{8,12},{9,13},{10,... | collective-permute-start | bytes 393224 | tf_op jit(solution)/shard_map/ppermute | solution.py:446
  54.8 11.0 %collective-permute-start.18 = (bf16[12,128,128]{2,1,0:T(8,128)(2,1)S(1)}, bf16[12,128,128]{2,1,0:T(8,128)(2,1)S(1)}, u32[]{:S(2)}, u32[]{:S(2)}) collective-permute-start(bf16[12,128,128]{2,1,0:T(8,128)(2,1)S(1)} %get-tuple-element.95), channel_id=1, source_target_pairs={{0,1},{1,0},{2,3},{3,2},{4,5},{5,4},{6,7},{7,6},{8,9},{9,8},{10,11... | collective-permute-start | bytes 1179656 | tf_op jit(solution)/shard_map/ppermute | solution.py:446
  55.4 12.1 %collective-permute-start.19 = (bf16[12,128,128]{2,1,0:T(8,128)(2,1)S(1)}, bf16[12,128,128]{2,1,0:T(8,128)(2,1)S(1)}, u32[]{:S(2)}, u32[]{:S(2)}) collective-permute-start(bf16[12,128,128]{2,1,0:T(8,128)(2,1)S(1)} %get-tuple-element.96), channel_id=1, source_target_pairs={{0,3},{1,2},{2,1},{3,0},{4,7},{5,6},{6,5},{7,4},{8,11},{9,10},{10,... | collective-permute-start | bytes 1179656 | tf_op jit(solution)/shard_map/ppermute | solution.py:446
  57.2 8.3 %collective-permute-start.17 = (bf16[8,128,128]{2,1,0:T(8,128)(2,1)S(1)}, bf16[8,128,128]{2,1,0:T(8,128)(2,1)S(1)}, u32[]{:S(2)}, u32[]{:S(2)}) collective-permute-start(bf16[8,128,128]{2,1,0:T(8,128)(2,1)S(1)} %get-tuple-element.94), channel_id=1, source_target_pairs={{0,4},{1,5},{2,6},{3,7},{4,0},{5,1},{6,2},{7,3},{8,12},{9,13},{10,... | collective-permute-start | bytes 786440 | tf_op jit(solution)/shard_map/ppermute | solution.py:446
  62.6 6.3 %collective-permute-start.22 = (bf16[4,128,128]{2,1,0:T(8,128)(2,1)S(1)}, bf16[4,128,128]{2,1,0:T(8,128)(2,1)S(1)}, u32[]{:S(2)}, u32[]{:S(2)}) collective-permute-start(bf16[4,128,128]{2,1,0:T(8,128)(2,1)S(1)} %get-tuple-element.111), channel_id=1, source_target_pairs={{0,1},{1,0},{2,3},{3,2},{4,5},{5,4},{6,7},{7,6},{8,9},{9,8},{10,11... | collective-permute-start | bytes 393224 | tf_op jit(solution)/shard_map/ppermute | solution.py:446
  63.4 6.7 %collective-permute-start.23 = (bf16[4,128,128]{2,1,0:T(8,128)(2,1)S(1)}, bf16[4,128,128]{2,1,0:T(8,128)(2,1)S(1)}, u32[]{:S(2)}, u32[]{:S(2)}) collective-permute-start(bf16[4,128,128]{2,1,0:T(8,128)(2,1)S(1)} %get-tuple-element.112), channel_id=1, source_target_pairs={{0,3},{1,2},{2,1},{3,0},{4,7},{5,6},{6,5},{7,4},{8,11},{9,10},{10,... | collective-permute-start | bytes 393224 | tf_op jit(solution)/shard_map/ppermute | solution.py:446
  67.6 12.9 %collective-permute-start.21 = (bf16[12,128,128]{2,1,0:T(8,128)(2,1)S(1)}, bf16[12,128,128]{2,1,0:T(8,128)(2,1)S(1)}, u32[]{:S(2)}, u32[]{:S(2)}) collective-permute-start(bf16[12,128,128]{2,1,0:T(8,128)(2,1)S(1)} %merge.4), channel_id=1, source_target_pairs={{0,4},{1,5},{2,6},{3,7},{4,0},{5,1},{6,2},{7,3},{8,12},{9,13},{10,... | collective-permute-start | bytes 1179656 | tf_op jit(solution)/shard_map/ppermute | solution.py:446
  70.2 10.2 %collective-permute-start.24 = (bf16[8,128,128]{2,1,0:T(8,128)(2,1)S(1)}, bf16[8,128,128]{2,1,0:T(8,128)(2,1)S(1)}, u32[]{:S(2)}, u32[]{:S(2)}) collective-permute-start(bf16[8,128,128]{2,1,0:T(8,128)(2,1)S(1)} %get-tuple-element.113), channel_id=1, source_target_pairs={{0,1},{1,0},{2,3},{3,2},{4,5},{5,4},{6,7},{7,6},{8,9},{9,8},{10,11... | collective-permute-start | bytes 786440 | tf_op jit(solution)/shard_map/ppermute | solution.py:446
  70.4 10.1 %collective-permute-start.25 = (bf16[8,128,128]{2,1,0:T(8,128)(2,1)S(1)}, bf16[8,128,128]{2,1,0:T(8,128)(2,1)S(1)}, u32[]{:S(2)}, u32[]{:S(2)}) collective-permute-start(bf16[8,128,128]{2,1,0:T(8,128)(2,1)S(1)} %get-tuple-element.114), channel_id=1, source_target_pairs={{0,3},{1,2},{2,1},{3,0},{4,7},{5,6},{6,5},{7,4},{8,11},{9,10},{10,... | collective-permute-start | bytes 786440 | tf_op jit(solution)/shard_map/ppermute | solution.py:446
  72.5 6.7 %collective-permute-start.26 = (bf16[2,128,128]{2,1,0:T(8,128)(2,1)S(1)}, bf16[2,128,128]{2,1,0:T(8,128)(2,1)S(1)}, u32[]{:S(2)}, u32[]{:S(2)}) collective-permute-start(bf16[2,128,128]{2,1,0:T(8,128)(2,1)S(1)} %get-tuple-element.115), channel_id=1, source_target_pairs={{0,1},{1,0},{2,3},{3,2},{4,5},{5,4},{6,7},{7,6},{8,9},{9,8},{10,11... | collective-permute-start | bytes 196616 | tf_op jit(solution)/shard_map/ppermute | solution.py:446
  73.8 6.6 %collective-permute-start.27 = (bf16[2,128,128]{2,1,0:T(8,128)(2,1)S(1)}, bf16[2,128,128]{2,1,0:T(8,128)(2,1)S(1)}, u32[]{:S(2)}, u32[]{:S(2)}) collective-permute-start(bf16[2,128,128]{2,1,0:T(8,128)(2,1)S(1)} %get-tuple-element.116), channel_id=1, source_target_pairs={{0,3},{1,2},{2,1},{3,0},{4,7},{5,6},{6,5},{7,4},{8,11},{9,10},{10,... | collective-permute-start | bytes 196616 | tf_op jit(solution)/shard_map/ppermute | solution.py:446
  (8 other events, 103.1 us)
